TPU v7x, 32 devices: a whole 2x2x4 slice. The times are simulated.
32 devices in a mesh: grp: 2 (over x), pi: 16 (over z, y, core).
Axes of the slice: x: 2, y: 2, z: 4, core: 2. Of those that a mesh axis runs over, the one named last changes fastest.
Arguments:
- left: bfloat16 [128, 1024], P(('grp', 'pi')), parts along dimension 0, may hold values from -6 to 6
- right: bfloat16 [128, 1024], P(('grp', 'pi')), parts along dimension 0, may hold values from -6 to 6
- depth: int32 [128], P(('grp', 'pi')), parts along dimension 0, may hold values from 1 to 32
- w_out: bfloat16 [1024, 128], replicated, may hold values from -0.1875 to 0.1875
- bias: float32 [128], replicated, may hold values from -4 to 4
- pair_cot: bfloat16 [128, 64, 128], P(('grp', 'pi')), parts along dimension 0, may hold values from -6 to 6
Outputs:
- pair_update: bfloat16 [128, 64, 128], P(('grp', 'pi')), parts along dimension 0
- grad_left: float32 [128, 1024], P(('grp', 'pi')), parts along dimension 0
- grad_right: float32 [128, 1024], P(('grp', 'pi')), parts along dimension 0
- grad_w: float32 [2048, 128], P('grp'), parts along dimension 0
- grad_bias: float32 [256], P('grp'), parts along dimension 0
There are 2 independent parts, one for each index of `grp`. A program takes and returns all parts, laid end to end along the dimension named above; an argument that names none is the same for every part. Nothing has to cross between parts.
All inputs are finite; a program needn't handle non-finite values.
Results may differ from a plain program's by a relative error of at most 0.0034.
Values may be sent and summed in bfloat16 or wider, within the bound.
No kernel may reach another device: no remote copies, remote signals or barrier semaphores. Data moves between devices by JAX's collectives and lax.ppermute only.
A program may use at most 64 MiB of HBM per device.

v0:
```python
import math

import jax
import jax.numpy as jnp
from jax import lax
from jax.sharding import PartitionSpec as P

C = 32


epsilon = 0.001


def local(left, right, depth, w_out, bias, pair_cot):
    rows = left.shape[0]
    width = left.shape[1]
    alignment = width // C
    total = pair_cot.shape[1]
    channels = w_out.shape[1]
    row_ids = jnp.arange(alignment, dtype=jnp.int32)
    own_mask = (row_ids[None, :] < depth[:, None]).astype(jnp.bfloat16)
    own_left = left.reshape(rows, alignment, C) * own_mask[:, :, None]
    w_back = w_out.T
    pair_cols = lax.all_to_all(pair_cot, "pi", split_axis=1, concat_axis=0, tiled=True)
    init = (
        jnp.zeros((rows, total, channels), jnp.bfloat16),
        jnp.zeros((rows, width), jnp.float32),
        jnp.zeros((C * C, channels), jnp.float32),
        jnp.zeros((channels,), jnp.float32),
    )
    carry = init
    start = jnp.int32(0)
    right_piece = lax.all_gather(right, "pi", axis=0, tiled=True)
    depth_piece = lax.all_gather(depth, "pi", axis=0, tiled=True)
    length = right_piece.shape[0]
    block = math.gcd(length, 256)
    for offset in range(0, length, block):
        begin = start + offset
        depth_block = depth_piece[offset : offset + block]
        mask_block = (row_ids[None, :] < depth_block[:, None]).astype(jnp.bfloat16)
        right_block = (
            right_piece[offset : offset + block].reshape(block, alignment, C)
            * mask_block[:, :, None]
        )
        count = epsilon + jnp.minimum(depth[:, None], depth_block[None, :]).astype(jnp.float32)
        outer = jnp.einsum(
            "isc,jsd->ijcd", own_left, right_block, preferred_element_type=jnp.float32
        )
        outer = (outer / count[:, :, None, None]).reshape(rows, block, C * C).astype(jnp.bfloat16)
        update = (jnp.dot(outer, w_out, preferred_element_type=jnp.float32) + bias).astype(
            jnp.bfloat16
        )
        cot_block = lax.dynamic_slice_in_dim(pair_cot, begin, block, 1)
        pair_out = lax.dynamic_update_slice(carry[0], update, (0, begin, 0))
        weight_acc = carry[2] + jnp.dot(
            outer.reshape(-1, C * C).T,
            cot_block.reshape(-1, channels),
            preferred_element_type=jnp.float32,
        )
        bias_acc = carry[3] + jnp.sum(cot_block, axis=(0, 1), dtype=jnp.float32)
        grad_pair = (
            jnp.dot(cot_block, w_back, preferred_element_type=jnp.float32) / count[:, :, None]
        )
        grad_pair = grad_pair.astype(jnp.bfloat16).reshape(rows, block, C, C)
        left_acc = carry[1] + jnp.einsum(
            "ijcd,jsd->isc", grad_pair, right_block, preferred_element_type=jnp.float32
        ).reshape(rows, width)
        carry = (pair_out, left_acc, weight_acc, bias_acc)
    pair_update = carry[0]
    left_acc = carry[1]
    accum = jnp.zeros((rows, width), jnp.float32)
    start = jnp.int32(0)
    left_piece = lax.all_gather(left, "pi", axis=0, tiled=True)
    depth_piece = lax.all_gather(depth, "pi", axis=0, tiled=True)
    length = left_piece.shape[0]
    block = math.gcd(length, 256)
    for offset in range(0, length, block):
        begin = start + offset
        depth_block = depth_piece[offset : offset + block]
        mask_block = (row_ids[None, :] < depth_block[:, None]).astype(jnp.bfloat16)
        left_block = (
            left_piece[offset : offset + block].reshape(block, alignment, C)
            * mask_block[:, :, None]
        )
        count = epsilon + jnp.minimum(depth_block[:, None], depth[None, :]).astype(jnp.float32)
        cot_block = lax.dynamic_slice_in_dim(pair_cols, begin, block, 0)
        grad_pair = (
            jnp.dot(cot_block, w_back, preferred_element_type=jnp.float32) / count[:, :, None]
        )
        grad_pair = grad_pair.astype(jnp.bfloat16).reshape(block, rows, C, C)
        accum = accum + jnp.einsum(
            "ijcd,isc->jsd", grad_pair, left_block, preferred_element_type=jnp.float32
        ).reshape(rows, width)
    grad_w, grad_bias = lax.psum((carry[2], carry[3]), "pi")
    grad_left = (left_acc.reshape(rows, alignment, C) * own_mask[:, :, None]).reshape(rows, width)
    grad_right = (accum.reshape(rows, alignment, C) * own_mask[:, :, None]).reshape(rows, width)
    return (pair_update, grad_left, grad_right, grad_w, grad_bias)


def solution(mesh):
    placed = (
        P(("grp", "pi"), None),
        P(("grp", "pi"), None),
        P(("grp", "pi")),
        P(),
        P(),
        P(("grp", "pi"), None, None),
    )
    return jax.shard_map(
        local,
        mesh=mesh,
        in_specs=placed,
        out_specs=(
            P(("grp", "pi"), None, None),
            P(("grp", "pi"), None),
            P(("grp", "pi"), None),
            P("grp", None),
            P("grp"),
        ),
        check_vma=False,
    )
```

profile of v0, /device:TPU:0, one launch (start us, length us, event | category | flops | bytes accessed | tf_op | source)
XLA Modules:
  0.0 145.5 jit_solution(4158764540035762436)
XLA Ops:
  7.2 1.3 dynamic-slice
  9.2 0.9 dynamic-update-slice
  10.0 13.7 %all-reduce = s32[64]{0:T(128)S(1)} all-reduce(s32[64]{0:T(128)S(1)} %dynamic-update-slice), channel_id=1, replica_groups=mesh['grp'=2,'pi'=16] {'pi'}, use_global_device_ids=true, to_apply=%add | all-reduce | flops 64 | bytes 512
  23.8 0.7 convert_add_fusion.1
  24.6 1.3 fusion.19
  25.9 18.5 %all-gather = bf16[16,4,1024]{2,1,0:T(4,128)(2,1)S(1)} all-gather(bf16[1,4,1024]{2,1,0:T(4,128)(2,1)} %bitcast.65), channel_id=1, replica_groups=mesh['grp'=2,'pi'=16] {'pi'}, dimensions={0}, use_global_device_ids=true | all-gather | bytes 139264 | tf_op jit(solution)/shard_map/all_gather | solution.py:33
  45.1 0.7 mul.54
  46.4 0.7 copy.48
  47.2 1.2 convolution_bitcast_fusion
  48.4 0.7 copy.52
  49.1 4.1 %all-to-all-start = ((bf16[4,64,128]{2,0,1:T(4,128)(2,1)}), bf16[4,64,128]{2,0,1:T(4,128)(2,1)}, u32[]{:S(2)}, u32[]{:S(2)}) async-start(bf16[4,64,128]{2,0,1:T(4,128)(2,1)} %copy.52), calls=%async_computation | async-start | bytes 131072 | tf_op jit(solution)/shard_map/all_to_all | solution.py:24
  54.9 3.8 %copy.51 = bf16[4,64,32,32]{3,2,1,0:T(8,128)(2,1)} copy(bf16[4,64,32,32]{1,3,2,0:T(8,128)(2,1)S(1)} %bitcast.59) | data formatting | bytes 1048576 | tf_op jit(solution)/shard_map/reshape | solution.py:64
  58.7 2.9 %fusion.4 = f32[4,32,32]{2,1,0:T(8,128)S(1)} fusion(bf16[4,64,32,32]{3,2,1,0:T(8,128)(2,1)} %copy.51, bf16[64,32,32]{2,1,0:T(8,128)(2,1)S(1)} %reshape.180, bf16[64,32]{1,0:T(8,128)(2,1)S(1)} %fusion.17, f32[4,32]{1,0:T(4,128)S(1)} %copy-done.6), kind=kOutput, calls=%fused_computation.11 | convolution fusion | flops 17043456 | bytes 676352 | tf_op jit(solution)/shard_map/ijcd,jsd->isc/dot_general | solution.py:65
  61.6 0.7 reshape.182
  62.3 1.1 fusion.3
  63.4 21.9 %all-gather.1 = bf16[16,4,1024]{2,1,0:T(4,128)(2,1)S(1)} all-gather(bf16[1,4,1024]{2,1,0:T(4,128)(2,1)S(1)} %bitcast.64), channel_id=1, replica_groups=mesh['grp'=2,'pi'=16] {'pi'}, dimensions={0}, use_global_device_ids=true | all-gather | bytes 139264 | tf_op jit(solution)/shard_map/all_gather | solution.py:73
  85.4 1.1 reshape.183
  86.4 30.3 %psum.15 = f32[128]{0:T(128)} all-reduce(f32[128]{0:T(128)S(1)} %copy-done.9), channel_id=1, replica_groups=mesh['grp'=2,'pi'=16] {'pi'}, use_global_device_ids=true, to_apply=%region_2.0 | all-reduce | flops 128 | bytes 1024 | tf_op jit(solution)/shard_map/psum | solution.py:94
  116.8 0.9 copy.53
  118.5 3.1 %copy.55 = bf16[64,4,32,32]{3,2,0,1:T(8,128)(2,1)S(1)} copy(bf16[64,4,32,32]{0,3,2,1:T(8,128)(2,1)S(1)} %bitcast.60) | data formatting | bytes 1048576 | tf_op jit(solution)/shard_map/reshape | solution.py:90
  121.6 1.9 %fusion.5 = f32[4,32,32]{2,1,0:T(8,128)S(1)} fusion(bf16[64,4,32,32]{3,2,0,1:T(8,128)(2,1)S(1)} %copy.55, bf16[64,32,32]{2,1,0:T(8,128)(2,1)} %reshape.183, bf16[64,32]{1,0:T(8,128)(2,1)S(1)} %fusion.17, f32[4,32]{1,0:T(4,128)S(1)} %copy-done.7), kind=kOutput, calls=%fused_computation.12 | convolution fusion | flops 17043456 | bytes 676352 | tf_op jit(solution)/shard_map/ijcd,isc->jsd/dot_general | solution.py:91
  123.5 0.7 reshape.185
  124.2 12.5 %all-reduce.3.cloned.1.call-done = f32[1024,128]{1,0:T(8,128)} async-done(((f32[1024,128]{1,0:T(8,128)}), f32[1024,128]{1,0:T(8,128)}) %all-reduce.3.cloned.1.call-update) | async-done | bytes 524304 | tf_op jit(solution)/shard_map/psum | solution.py:94
  136.8 1.9 %copy.71 = f32[1024,128]{1,0:T(8,128)} copy(f32[1024,128]{1,0:T(8,128)} %all-reduce.3.cloned.1.call-done) | data formatting | bytes 1048576
  (42 shorter events, 4.0 us)
Async XLA Ops:
  7.2 46.9 %copy-start = (bf16[1024,128]{1,0:T(8,128)(2,1)S(1)}, bf16[1024,128]{1,0:T(8,128)(2,1)}, u32[]{:S(2)}) copy-start(bf16[1024,128]{1,0:T(8,128)(2,1)} %param.9) | copy-start | bytes 786436
  7.2 129.6 %all-reduce.3.cloned.1.call-start = ((), (), s32[]{:S(2)}) async-start(), calls=%async_computation.1 | async-start | bytes 1048576 | tf_op jit(solution)/shard_map/psum | solution.py:94
  23.8 2.1 %copy-start.4 = (s32[64]{0:T(128)}, s32[64]{0:T(128)S(1)}, u32[]{:S(2)}) copy-start(s32[64]{0:T(128)S(1)} %all-reduce) | copy-start | bytes 772
  46.4 0.8 copy-start.1
  49.1 67.7 %all-to-all-start = ((bf16[4,64,128]{2,0,1:T(4,128)(2,1)}), bf16[4,64,128]{2,0,1:T(4,128)(2,1)}, u32[]{:S(2)}, u32[]{:S(2)}) async-start(bf16[4,64,128]{2,0,1:T(4,128)(2,1)} %copy.52), calls=%async_computation | async-start | bytes 131072 | tf_op jit(solution)/shard_map/all_to_all | solution.py:24
  54.4 4.3 %copy-start.6 = (f32[4,32]{1,0:T(4,128)S(1)}, f32[4,32]{1,0:T(4,128)}, u32[]{:S(2)}) copy-start(f32[4,32]{1,0:T(4,128)} %get-tuple-element.5) | copy-start | bytes 1540
  58.7 3.7 %copy-start.8 = (f32[128]{0:T(128)S(1)}, f32[128]{0:T(128)}, u32[]{:S(2)}) copy-start(f32[128]{0:T(128)} %param.10) | copy-start | bytes 1540
  58.7 4.8 %copy-start.2 = (bf16[4,1024]{1,0:T(4,128)(2,1)S(1)}, bf16[4,1024]{1,0:T(4,128)(2,1)}, u32[]{:S(2)}) copy-start(bf16[4,1024]{1,0:T(4,128)(2,1)} %param.6) | copy-start | bytes 24580
  58.7 27.8 %copy-start.9 = (f32[128]{0:T(128)S(1)}, f32[128]{0:T(128)}, u32[]{:S(2)}) copy-start(f32[128]{0:T(128)} %convert_reduce_fusion) | copy-start | bytes 1540
  58.7 58.1 %copy-start.3 = (s32[4]{0:T(128)S(1)}, s32[4]{0:T(128)}, u32[]{:S(2)}) copy-start(s32[4]{0:T(128)} %param.8) | copy-start | bytes 52
  58.7 58.1 %copy-start.5 = (s32[64]{0:T(128)S(1)}, s32[64]{0:T(128)}, u32[]{:S(2)}) copy-start(s32[64]{0:T(128)} %copy-done.4) | copy-start | bytes 772
  118.0 3.6 %copy-start.7 = (f32[4,32]{1,0:T(4,128)S(1)}, f32[4,32]{1,0:T(4,128)}, u32[]{:S(2)}) copy-start(f32[4,32]{1,0:T(4,128)} %get-tuple-element.5) | copy-start | bytes 1540
Sparse Core Ops, SparseCore 0:
  48.5 88.1 all-reduce.2
where the time goes:
time: 146 us; the launch traced here: 145 us
  blocking collectives  84.5 us (58%)
  local copies, waits for them, and re-layouts  17.7 us (12%)
  between operations  14.9 us (10%)
  waiting for transfers between devices  12.5 us (9%)
  matrix products  8.19 us (6%)
  starting transfers between devices  4.15 us (3%)
  other arithmetic  3.48 us (2%)
    psum x1, blocking collectives, local(): grad_w, grad_bias = lax.psum((carry[2], carry[3]), 'pi')  30.3 us
    all_gather x1, blocking collectives, local(): left_piece = lax.all_gather(left, 'pi', axis=0, tiled=True)  21.9 us
    all_gather x1, blocking collectives, local(): right_piece = lax.all_gather(right, 'pi', axis=0, tiled=True)  18.5 us
    unnamed x1, blocking collectives  13.7 us
    psum x1, waiting for transfers between devices, local(): grad_w, grad_bias = lax.psum((carry[2], carry[3]), 'pi')  12.5 us
    unnamed x27, local copies, waits for them, and re-layouts  4.99 us
    all_to_all x1, starting transfers between devices, local(): lax.all_to_all(pair_cot, 'pi', split_axis=1, concat_axis=0, tiled=True)  4.11 us
    reshape x1, local copies, waits for them, and re-layouts, local(): grad_pair = grad_pair.astype(jnp.bfloat16).reshape(rows, block, C, C)  3.77 us
  transfers between devices with their start and end apart: 2, of which 1 were waited for; matrix products, arithmetic and copies ran while one was open for 13% of the time, Pallas kernels for 0%

commit v1 on v0

--- a/solution.py
+++ b/solution.py
@@ -1,17 +1,324 @@
+import functools
 import math
 
 import jax
 import jax.numpy as jnp
 from jax import lax
+from jax.experimental import pallas as pl
+from jax.experimental.pallas import tpu as pltpu
 from jax.sharding import PartitionSpec as P
 
 C = 32
+LANES = 128
+CORES = 2
 
 
 epsilon = 0.001
 
+F32 = jnp.float32
+BF16 = jnp.bfloat16
+
+
+def iota(shape, dim):
+    return lax.broadcasted_iota(jnp.int32, shape, dim)
+
+
+def dot(x, y, contract_x, contract_y):
+    return lax.dot_general(
+        x, y, (((contract_x,), (contract_y,)), ((), ())), preferred_element_type=F32
+    )
+
+
+def sum_kernel(rows, own_ref, other_ref, w_ref, right_ref, bias_ref):
+    wide = w_ref.shape[0]
+    w_ref[...] = own_ref[:wide, :] + other_ref[:wide, :]
+    core = lax.rem(lax.axis_index("pi"), CORES)
+    tiles = right_ref.shape[1] // LANES
+    begin = pl.multiple_of(wide + core * rows * tiles, 8)
+    part = own_ref[pl.ds(begin, rows * tiles), :] + other_ref[pl.ds(begin, rows * tiles), :]
+    for row in range(rows):
+        for tile in range(tiles):
+            at = row * tiles + tile
+            right_ref[row : row + 1, tile * LANES : (tile + 1) * LANES] = part[at : at + 1, :]
+    last = wide + CORES * rows * tiles
+    bias_ref[...] = own_ref[last : last + 1, :] + other_ref[last : last + 1, :]
+
+
+def main_kernel(sizes, *refs):
+    rows, total, pieces, depth_rows = sizes
+    piece = refs[:pieces]
+    w_ref, w_swap_ref, bias_ref = refs[pieces : pieces + 3]
+    update_ref, left_ref, partial_ref = refs[pieces + 3 : pieces + 6]
+    (
+        right_all, turned, spread, left_all, left_wide, cots, inverse, outer, outer_own,
+        window, picked, weights, g_left, g_right, stage,
+    ) = refs[pieces + 6 :]
+    chip_rows = CORES * rows
+    pairs = rows * total
+    tiles = C * C // LANES
+    per_tile = LANES // total
+    group = LANES // C
+    me = lax.axis_index("pi")
+    chip = me // CORES
+    at_left = pairs
+    at_right = pairs + C
+    at_depth = at_right + (tiles + 1) * chip_rows
+
+    for m in range(pieces):
+        block = piece[m][at_right : at_right + depth_rows, :].astype(F32)
+        for tile in range(tiles + 1):
+            right_all[tile, m * chip_rows : (m + 1) * chip_rows, :] = block[
+                tile * chip_rows : (tile + 1) * chip_rows
+            ]
+        left_all[m * C : (m + 1) * C, :] = piece[m][at_left : at_left + C, :]
+        left_wide[m * C : (m + 1) * C, :] = piece[m][at_left : at_left + C, :].astype(F32)
+        cots[m * pairs : (m + 1) * pairs, :] = piece[m][:pairs, :]
+    place = lax.bitwise_xor(iota((total, LANES), 0), me * rows) == lax.rem(
+        iota((total, LANES), 1), total
+    )
+    place = place.astype(F32).astype(BF16)
+    for tile in range(tiles):
+        turned[tile * LANES : (tile + 1) * LANES, :] = dot(
+            right_all[tile].astype(BF16), place, 0, 0
+        )
+    depth_all = right_all[tiles].astype(BF16)
+    depth_lane = dot(depth_all, place, 0, 0)
+
+    for m in range(pieces):
+        block = piece[m][at_right : at_right + depth_rows, :].astype(F32)
+        for tile in range(pairs // LANES):
+            at = at_depth - at_right + tile
+            least = jnp.minimum(block[at : at + 1, :], depth_lane[:1, :])
+            inverse[m * C : (m + 1) * C, tile * LANES : (tile + 1) * LANES] = jnp.broadcast_to(
+                1.0 / (epsilon + least), (C, LANES)
+            )
+
+    alignment = spread.shape[0] // rows
+    alive = iota((alignment, LANES), 0).astype(F32) < depth_lane[:alignment, :]
+    part_of = iota((alignment, LANES), 1) // total
+    keep = [jnp.where(alive & (part_of == k), 1.0, 0.0).astype(F32) for k in range(per_tile)]
+    nothing = jnp.zeros((alignment, LANES), BF16)
+    for d in range(C):
+        block = turned[pl.ds(d, alignment, stride=C), :]
+        kept = [(block * keep[k]).astype(BF16) for k in range(per_tile)]
+        for i in range(rows):
+            for tile in range(pairs // LANES):
+                spread[
+                    i * alignment : (i + 1) * alignment,
+                    d * pairs + tile * LANES : d * pairs + (tile + 1) * LANES,
+                ] = kept[i % per_tile] if i // per_tile == tile else nothing
+
+    chunk = outer.shape[0] // C
+
+    def some_channels(step, carry):
+        for k in range(chunk):
+            d = step * chunk + k
+            begin = pl.multiple_of(d * pairs, pairs)
+            o = dot(left_all[...], spread[:, pl.ds(begin, pairs)], 1, 0)
+            o = (o * inverse[...]).astype(BF16)
+            for m in range(pieces):
+                outer[k * C : (k + 1) * C, m * pairs : (m + 1) * pairs] = o[m * C : (m + 1) * C, :]
+        own_at = pl.multiple_of(step * chunk * C, chunk * C)
+        outer_own[pl.ds(own_at, chunk * C), :] = outer[:, :pairs]
+        grad = dot(outer[...], cots[...], 1, 0)
+        for k in range(chunk):
+            partial_ref[pl.ds(step * chunk + k, C, stride=C), :] = grad[k * C : (k + 1) * C, :]
+        return carry
+
+    lax.fori_loop(0, C // chunk, some_channels, 0)
+    wide = C * C
+    last = wide + chip_rows * tiles
+    partial_ref[last : last + 8, :] = dot(
+        jnp.ones((8, pieces * pairs), BF16), cots[...], 1, 0
+    )
+
+    half = lax.rem(chip, 16 // chip_rows)
+    for m in range(pieces):
+        for i in range(rows):
+            begin = i * total + chip * chip_rows - half * chip_rows
+            two = piece[m][pl.ds(pl.multiple_of(begin, 16), 16), :].astype(F32)
+            one = two[:chip_rows]
+            for k in range(1, 16 // chip_rows):
+                one = jnp.where(half == k, two[k * chip_rows : (k + 1) * chip_rows], one)
+            at = (i * pieces + m) * chip_rows
+            window[at : at + chip_rows, :] = one
+    mine = rows * pieces
+    for j in range(chip_rows):
+        picked[j * mine : (j + 1) * mine, :] = window[
+            pl.ds(j, mine, stride=chip_rows), :
+        ].astype(BF16)
+    count_lanes = chip_rows * mine
+    row = iota((total, count_lanes), 0)
+    lane = iota((total, count_lanes), 1)
+    own_lane = lax.rem(lane, mine)
+    from_i = row == lax.rem(own_lane, pieces) * chip_rows + own_lane // pieces
+    from_j = lax.bitwise_xor(row, me * rows) == chip * chip_rows + lane // mine
+    depth_i = dot(depth_all, from_i.astype(F32).astype(BF16), 0, 0)[:8, :]
+    depth_j = dot(depth_all, from_j.astype(F32).astype(BF16), 0, 0)[:8, :]
+    inverse_right = (1.0 / (epsilon + jnp.minimum(depth_i, depth_j)))[:1, :]
+    for c in range(C):
+        g = dot(w_ref[c * C : (c + 1) * C, :], picked[...], 1, 1)
+        g = (g * inverse_right).astype(BF16)
+        for k in range(count_lanes // LANES):
+            g_right[k * C : (k + 1) * C, c * LANES : (c + 1) * LANES] = g[
+                :, k * LANES : (k + 1) * LANES
+            ]
+        feature = left_wide[pl.ds(c, pieces, stride=C), :]
+        turns = [feature] + [pltpu.roll(feature, k * alignment, 1) for k in range(1, rows)]
+        block_of = iota((pieces, LANES), 1) // alignment
+        for j in range(group):
+            both = jnp.concatenate(
+                [jnp.where(block_of == j, turns[(j - i) % rows], 0.0) for i in range(rows)], 0
+            )
+            at = c * LANES + j * mine
+            weights[at : at + mine, :] = both.astype(BF16)
+    right_grad = dot(g_right[...], weights[...], 1, 0)
+    in_tile = iota((8, LANES), 1) // C
+    row_of = (iota((8, LANES), 0) * group + in_tile).astype(F32)
+    for k in range(count_lanes // LANES):
+        part = right_grad[k * C : (k + 1) * C, :]
+        stage[...] = jnp.concatenate([part] * group, 0).T
+        for j in range(group):
+            flat = jnp.zeros((8, LANES), F32)
+            for q in range(group):
+                flat = jnp.where(
+                    in_tile == q, stage[pl.ds(j * alignment + q, tiles, stride=group), :], flat
+                )
+            residue = lax.bitwise_xor(k * group + j, lax.rem(me, CORES) * rows)
+            depth = right_all[tiles, pl.ds(residue, 1), :]
+            at = wide + (k * group + j) * tiles
+            partial_ref[at : at + tiles, :] = jnp.where(row_of < depth, flat, 0.0)
+
+    update = dot(outer_own[...], w_swap_ref[...], 0, 0)
+    update_ref[...] = (update + bias_ref[...]).astype(BF16)
+    for d in range(C):
+        g = dot(w_swap_ref[d * C : (d + 1) * C, :], piece[0][:pairs, :], 1, 1)
+        g_left[:, d * pairs : (d + 1) * pairs] = (g * inverse[:C, :]).astype(BF16)
+    left_grad = dot(g_left[...], spread[...], 1, 1)
+    stage[...] = jnp.concatenate([left_grad] * group, 0).T
+    for i in range(rows):
+        flat = jnp.zeros((8, LANES), F32)
+        for q in range(group):
+            flat = jnp.where(
+                in_tile == q, stage[pl.ds(i * alignment + q, tiles, stride=group), :], flat
+            )
+        flat = jnp.where(row_of < right_all[tiles, i : i + 1, :], flat, 0.0)
+        for tile in range(tiles):
+            left_ref[i : i + 1, tile * LANES : (tile + 1) * LANES] = flat[tile : tile + 1, :]
+
+
+def swap(x, mask, size):
+    return lax.ppermute(x, "pi", [(i, i ^ mask) for i in range(size)])
+
+
+def gathered(left, right, depth, w_out, bias, pair_cot):
+    rows, width = left.shape
+    alignment = width // C
+    total, channels = pair_cot.shape[1:]
+    size = lax.axis_size("pi")
+    pieces = size // CORES
+    pairs = rows * total
+    chip_rows = CORES * rows
+    tiles = width // LANES
+    depth_wide = jnp.broadcast_to(depth.astype(BF16)[:, None], (rows, LANES))
+    right_own = jnp.concatenate([right, depth_wide], 1)
+    right_chip = jnp.concatenate([right_own, swap(right_own, 1, size)], 0)
+    right_chip = right_chip.reshape(chip_rows, tiles + 1, LANES).swapaxes(0, 1)
+    row_ids = jnp.arange(alignment, dtype=jnp.int32)
+    own_mask = (row_ids[None, :] < depth[:, None]).astype(BF16)
+    own_left = left.reshape(rows, alignment, C) * own_mask[:, :, None]
+    depth_pairs = jnp.broadcast_to(depth.astype(BF16)[:, None], (rows, total))
+    used = pairs + C + (tiles + 1) * chip_rows + pairs // LANES
+    spare = -used % 16
+    payload = jnp.concatenate(
+        [
+            pair_cot.reshape(pairs, channels),
+            own_left.transpose(2, 0, 1).reshape(C, LANES),
+            right_chip.reshape(-1, LANES),
+            depth_pairs.reshape(-1, LANES),
+            jnp.zeros((spare, LANES), BF16),
+        ],
+        0,
+    )
+    far = [payload] + [swap(payload, mask, size) for mask in range(2 * CORES, size, 2 * CORES)]
+    near = [swap(x, CORES, size) for x in far]
+    arrived = [x for both in zip(far, near) for x in both]
+    w_swap = w_out.reshape(C, C, channels).swapaxes(0, 1).reshape(C * C, channels)
+    depth_rows = used + spare - pairs - C
+    partial_rows = C * C + chip_rows * tiles + 8
+    count_lanes = chip_rows * rows * pieces
+    chunk = 8
+    update, grad_left, partial = pl.pallas_call(
+        functools.partial(main_kernel, (rows, total, pieces, depth_rows)),
+        out_shape=(
+            jax.ShapeDtypeStruct((pairs, channels), BF16),
+            jax.ShapeDtypeStruct((rows, width), F32),
+            jax.ShapeDtypeStruct((partial_rows, LANES), F32),
+        ),
+        scratch_shapes=[
+            pltpu.VMEM((tiles + 1, total, LANES), F32),
+            pltpu.VMEM((width, LANES), F32),
+            pltpu.VMEM((rows * alignment, C * pairs), BF16),
+            pltpu.VMEM((pieces * C, LANES), BF16),
+            pltpu.VMEM((pieces * C, LANES), F32),
+            pltpu.VMEM((pieces * pairs, channels), BF16),
+            pltpu.VMEM((pieces * C, pairs), F32),
+            pltpu.VMEM((chunk * C, pieces * pairs), BF16),
+            pltpu.VMEM((C * C, pairs), BF16),
+            pltpu.VMEM((count_lanes, channels), F32),
+            pltpu.VMEM((count_lanes, channels), BF16),
+            pltpu.VMEM((C * LANES, LANES), BF16),
+            pltpu.VMEM((C, C * pairs), BF16),
+            pltpu.VMEM((count_lanes // LANES * C, C * LANES), BF16),
+            pltpu.VMEM((LANES, LANES), F32),
+        ],
+        compiler_params=pltpu.CompilerParams(vmem_limit_bytes=40 * 1024 * 1024),
+    )(*arrived, w_out, w_swap, bias.reshape(1, channels))
+    other = swap(partial, 1, size)
+    grad_w, grad_right, grad_bias = pl.pallas_call(
+        functools.partial(sum_kernel, rows),
+        out_shape=(
+            jax.ShapeDtypeStruct((C * C, channels), F32),
+            jax.ShapeDtypeStruct((rows, width), F32),
+            jax.ShapeDtypeStruct((1, channels), F32),
+        ),
+    )(partial, other)
+    return (
+        update.reshape(rows, total, channels),
+        grad_left,
+        grad_right,
+        grad_w,
+        grad_bias.reshape(channels),
+    )
+
+
+def gathers(left, pair_cot, w_out):
+    rows, width = left.shape
+    total, channels = pair_cot.shape[1:]
+    size = lax.axis_size("pi")
+    gather_bytes = size * pair_cot.size * 2
+    reduce_bytes = 2 * w_out.size * 4
+    return (
+        gather_bytes <= reduce_bytes
+        and size >= 2 * CORES
+        and size & (size - 1) == 0
+        and rows & (rows - 1) == 0
+        and channels == LANES
+        and rows * (width // C) == LANES
+        and LANES % total == 0
+        and width == C * C == 8 * LANES
+        and rows * CORES == 8
+        and (rows * size // CORES) * (LANES // C) == LANES
+    )
+
 
 def local(left, right, depth, w_out, bias, pair_cot):
+    if gathers(left, pair_cot, w_out):
+        return gathered(left, right, depth, w_out, bias, pair_cot)
+    return reduced(left, right, depth, w_out, bias, pair_cot)
+
+
+def reduced(left, right, depth, w_out, bias, pair_cot):
     rows = left.shape[0]
     width = left.shape[1]
     alignment = width // C

time: 146 us -> 39.6 us (0.27)
  blocking collectives: 84.5 us -> 0 us
  between operations: 14.9 us -> 0.7 us
  local copies, waits for them, and re-layouts: 17.7 us -> 3.78 us
  Pallas kernels: 0 us -> 9.81 us
  matrix products: 8.19 us -> 0 us
  starting transfers between devices: 4.15 us -> 11.1 us
  waiting for transfers between devices: 12.5 us -> 11 us
    all_gather x2 -> x0, blocking collectives: 40.5 us -> none  [the longest x1 21.9 us: local(): left_piece = lax.all_gather(left, 'pi', axis=0, tiled=True)]
    psum x1 -> x0, blocking collectives: 30.3 us -> none  [local(): grad_w, grad_bias = lax.psum((carry[2], carry[3]), 'pi')]
    unnamed x1 -> x0, blocking collectives: 13.7 us -> none
    psum x1 -> x0, waiting for transfers between devices: 12.5 us -> none  [local(): grad_w, grad_bias = lax.psum((carry[2], carry[3]), 'pi')]
    ppermute x0 -> x9, starting transfers between devices: none -> 11.1 us  [swap(): return lax.ppermute(x, 'pi', [(i, i ^ mask) for i in range(size)])]
    ppermute x0 -> x9, waiting for transfers between devices: none -> 11 us  [swap(): return lax.ppermute(x, 'pi', [(i, i ^ mask) for i in range(size)])]
    pallas_call x0 -> x2, Pallas kernels: none -> 9.81 us  [the longest x1 7.74 us: gathered(): pl.pallas_call(functools.partial(main_kernel, (rows, total, pieces, depth...]
    reshape x6 -> x4, local copies, waits for them, and re-layouts: 9.61 us -> 1.08 us  [the longest x2 0.89 us: gathered(): own_left = left.reshape(rows, alignment, C) * own_mask[:, :, None]]
  transfers between devices with their start and end apart: 2 -> 9, of which waited for: 1 -> 5; matrix products, arithmetic and copies ran while one was open for 13% -> 5% of each run, Pallas kernels for 0% -> 0%
where the time goes in v1:
time: 39.6 us; the launch traced here: 39.3 us
  starting transfers between devices  11.1 us (28%)
  waiting for transfers between devices  11 us (28%)
  Pallas kernels  9.81 us (25%)
  local copies, waits for them, and re-layouts  3.78 us (10%)
  other arithmetic  2.87 us (7%)
  between operations  0.7 us (2%)
    ppermute x9, starting transfers between devices, swap(): return lax.ppermute(x, 'pi', [(i, i ^ mask) for i in range(size)])  11.1 us
    ppermute x9, waiting for transfers between devices, swap(): return lax.ppermute(x, 'pi', [(i, i ^ mask) for i in range(size)])  11 us
    pallas_call x1, Pallas kernels, gathered(): pl.pallas_call(functools.partial(main_kernel, (rows, total, pieces, depth...  7.74 us
    pallas_call x1, Pallas kernels, gathered(): pl.pallas_call(functools.partial(sum_kernel, rows), out_shape=(jax.ShapeD...  2.08 us
    unnamed x8, local copies, waits for them, and re-layouts  1.47 us
    concatenate x1, local copies, waits for them, and re-layouts, gathered(): jnp.concatenate([pair_cot.reshape(pairs, channels), own_left.transpose(2,...  0.91 us
    reshape x2, local copies, waits for them, and re-layouts, gathered(): own_left = left.reshape(rows, alignment, C) * own_mask[:, :, None]  0.89 us
  transfers between devices with their start and end apart: 9, of which 5 were waited for; matrix products, arithmetic and copies ran while one was open for 5% of the time, Pallas kernels for 0%

profile of v1, /device:TPU:0, one launch (start us, length us, event | category | flops | bytes accessed | tf_op | source)
XLA Modules:
  0.0 39.3 jit_solution(10016917880439056286)
XLA Ops:
  0.6 0.7 %convert_element_type.12 = bf16[4]{0:T(256)(128)(2,1)S(1)} convert(s32[4]{0:T(128)} %param.8) | non-fusion elementwise | flops 4 | bytes 24 | tf_op jit(solution)/shard_map/convert_element_type | solution.py:223
  1.4 0.7 %pad_maximum_fusion = bf16[4,1152]{1,0:T(4,128)(2,1)S(1)} fusion(bf16[4,128]{1,0:T(4,128)(2,1)S(1)} %broadcast_in_dim.10, bf16[4,1024]{1,0:T(4,128)(2,1)} %param.7), kind=kLoop, calls=%fused_computation.2 | loop fusion | flops 18432 | bytes 18432 | tf_op jit(solution)/shard_map/concatenate | solution.py:224
  2.1 0.5 %collective-permute-start = (bf16[4,1152]{1,0:T(4,128)(2,1)S(1)}, bf16[4,1152]{1,0:T(4,128)(2,1)S(1)}, u32[]{:S(2)}, u32[]{:S(2)}) collective-permute-start(bf16[4,1152]{1,0:T(4,128)(2,1)S(1)} %pad_maximum_fusion), channel_id=1, source_target_pairs={{0,1},{1,0},{2,3},{3,2},{4,5},{5,4},{6,7},{7,6},{8,9},{9,8},{10,11... | collective-permute-start | bytes 27656 | tf_op jit(solution)/shard_map/ppermute | solution.py:211
  2.6 0.7 %fusion = bf16[4,32]{1,0:T(4,128)(2,1)S(1)} fusion(s32[4]{0:T(128)} %param.8), kind=kLoop, calls=%fused_computation.4 | loop fusion | flops 256 | bytes 272 | tf_op jit(solution)/shard_map/convert_element_type | solution.py:228
  3.3 0.8 %reshape.67 = bf16[4,32,32]{2,1,0:T(8,128)(2,1)S(1)} reshape(bf16[4,1024]{1,0:T(4,128)(2,1)} %param.6) | data formatting | bytes 16384 | tf_op jit(solution)/shard_map/reshape | solution.py:229
  4.1 0.1 copy.11
  4.6 0.7 %maximum_bitcast_fusion = bf16[72,128]{1,0:T(8,128)(2,1)S(1)} fusion(bf16[4,1152]{1,0:T(4,128)(2,1)S(1)} %collective-permute-done, bf16[4,128]{1,0:T(4,128)(2,1)S(1)} %broadcast_in_dim.10, bf16[4,1024]{1,0:T(4,128)(2,1)} %param.7), kind=kLoop, calls=%fused_computation.1 | loop fusion | flops 55296 | bytes 36864 | tf_op jit(solution)/shard_map/reshape | solution.py:237
  5.3 0.9 %concatenate.11.refs_0_ = bf16[368,128]{1,0:T(8,128)(2,1)S(1)} concatenate(bf16[256,128]{1,0:T(8,128)(2,1)} %bitcast.19, bf16[32,128]{1,0:T(8,128)(2,1)S(1)} %reshape.68, bf16[72,128]{1,0:T(8,128)(2,1)S(1)} %maximum_bitcast_fusion, bf16[2,128]{1,0:T(2,128)(2,1)S(1)} %broadcast_in_dim.25, bf16[6,128]{1,0:T(8,128)(2,1)S(1)} %broadcast_in_dim.26), dimensions={0} | concatenate | bytes 188416 | tf_op jit(solution)/shard_map/concatenate | solution.py:233
  6.2 4.7 %collective-permute-start.6 = (bf16[368,128]{1,0:T(8,128)(2,1)S(1)}, bf16[368,128]{1,0:T(8,128)(2,1)S(1)}, u32[]{:S(2)}, u32[]{:S(2)}) collective-permute-start(bf16[368,128]{1,0:T(8,128)(2,1)S(1)} %concatenate.11.refs_0_), channel_id=1, source_target_pairs={{0,12},{1,13},{2,14},{3,15},{4,8},{5,9},{6,10},{7,11},{8,4},{9,5},... | collective-permute-start | bytes 282632 | tf_op jit(solution)/shard_map/ppermute | solution.py:211
  10.9 0.6 %collective-permute-start.2 = (bf16[368,128]{1,0:T(8,128)(2,1)S(1)}, bf16[368,128]{1,0:T(8,128)(2,1)S(1)}, u32[]{:S(2)}, u32[]{:S(2)}) collective-permute-start(bf16[368,128]{1,0:T(8,128)(2,1)S(1)} %concatenate.11.refs_0_), channel_id=1, source_target_pairs={{0,4},{1,5},{2,6},{3,7},{4,0},{5,1},{6,2},{7,3},{8,12},{9,13},{10,... | collective-permute-start | bytes 282632 | tf_op jit(solution)/shard_map/ppermute | solution.py:211
  11.5 1.7 %collective-permute-start.1 = (bf16[368,128]{1,0:T(8,128)(2,1)S(1)}, bf16[368,128]{1,0:T(8,128)(2,1)S(1)}, u32[]{:S(2)}, u32[]{:S(2)}) collective-permute-start(bf16[368,128]{1,0:T(8,128)(2,1)S(1)} %concatenate.11.refs_0_), channel_id=1, source_target_pairs={{0,2},{1,3},{2,0},{3,1},{4,6},{5,7},{6,4},{7,5},{8,10},{9,11},{10,... | collective-permute-start | bytes 282632 | tf_op jit(solution)/shard_map/ppermute | solution.py:211
  13.2 1.4 %collective-permute-done.6.refs_6_ = bf16[368,128]{1,0:T(8,128)(2,1)S(1)} collective-permute-done((bf16[368,128]{1,0:T(8,128)(2,1)S(1)}, bf16[368,128]{1,0:T(8,128)(2,1)S(1)}, u32[]{:S(2)}, u32[]{:S(2)}) %collective-permute-start.6) | collective-permute-done | bytes 94240 | tf_op jit(solution)/shard_map/ppermute | solution.py:211
  14.5 1.7 %collective-permute-start.7 = (bf16[368,128]{1,0:T(8,128)(2,1)S(1)}, bf16[368,128]{1,0:T(8,128)(2,1)S(1)}, u32[]{:S(2)}, u32[]{:S(2)}) collective-permute-start(bf16[368,128]{1,0:T(8,128)(2,1)S(1)} %collective-permute-done.6.refs_6_), channel_id=1, source_target_pairs={{0,2},{1,3},{2,0},{3,1},{4,6},{5,7},{6,4},{7,5},{8,10},{9,11},{10,... | collective-permute-start | bytes 282632 | tf_op jit(solution)/shard_map/ppermute | solution.py:211
  16.2 3.3 %collective-permute-done.4.refs_4_ = bf16[368,128]{1,0:T(8,128)(2,1)S(1)} collective-permute-done((bf16[368,128]{1,0:T(8,128)(2,1)S(1)}, bf16[368,128]{1,0:T(8,128)(2,1)S(1)}, u32[]{:S(2)}, u32[]{:S(2)}) %collective-permute-start.4) | collective-permute-done | bytes 94240 | tf_op jit(solution)/shard_map/ppermute | solution.py:211
  19.4 1.5 %collective-permute-start.5 = (bf16[368,128]{1,0:T(8,128)(2,1)S(1)}, bf16[368,128]{1,0:T(8,128)(2,1)S(1)}, u32[]{:S(2)}, u32[]{:S(2)}) collective-permute-start(bf16[368,128]{1,0:T(8,128)(2,1)S(1)} %collective-permute-done.4.refs_4_), channel_id=1, source_target_pairs={{0,2},{1,3},{2,0},{3,1},{4,6},{5,7},{6,4},{7,5},{8,10},{9,11},{10,... | collective-permute-start | bytes 282632 | tf_op jit(solution)/shard_map/ppermute | solution.py:211
  21.0 0.5 %collective-permute-start.3 = (bf16[368,128]{1,0:T(8,128)(2,1)S(1)}, bf16[368,128]{1,0:T(8,128)(2,1)S(1)}, u32[]{:S(2)}, u32[]{:S(2)}) collective-permute-start(bf16[368,128]{1,0:T(8,128)(2,1)S(1)} %collective-permute-done.2.refs_2_), channel_id=1, source_target_pairs={{0,2},{1,3},{2,0},{3,1},{4,6},{5,7},{6,4},{7,5},{8,10},{9,11},{10,... | collective-permute-start | bytes 282632 | tf_op jit(solution)/shard_map/ppermute | solution.py:211
  21.5 0.1 copy.12
  21.6 3.4 %collective-permute-done.5.refs_5_ = bf16[368,128]{1,0:T(8,128)(2,1)S(1)} collective-permute-done((bf16[368,128]{1,0:T(8,128)(2,1)S(1)}, bf16[368,128]{1,0:T(8,128)(2,1)S(1)}, u32[]{:S(2)}, u32[]{:S(2)}) %collective-permute-start.5) | collective-permute-done | bytes 94240 | tf_op jit(solution)/shard_map/ppermute | solution.py:211
  25.0 1.0 %collective-permute-done.3.refs_3_ = bf16[368,128]{1,0:T(8,128)(2,1)S(1)} collective-permute-done((bf16[368,128]{1,0:T(8,128)(2,1)S(1)}, bf16[368,128]{1,0:T(8,128)(2,1)S(1)}, u32[]{:S(2)}, u32[]{:S(2)}) %collective-permute-start.3) | collective-permute-done | bytes 94240 | tf_op jit(solution)/shard_map/ppermute | solution.py:211
  26.0 0.7 %copy-done.2 = f32[128]{0:T(128)S(1)} copy-done((f32[128]{0:T(128)S(1)}, f32[128]{0:T(128)}, u32[]{:S(2)}) %copy-start.2) | copy-done | bytes 536
  26.7 7.7 %shard_map.101 = (bf16[256,128]{1,0:T(8,128)(2,1)}, f32[4,1024]{1,0:T(4,128)}, f32[1096,128]{1,0:T(8,128)S(1)}) custom-call(bf16[368,128]{1,0:T(8,128)(2,1)S(1)} %concatenate.11.refs_0_, bf16[368,128]{1,0:T(8,128)(2,1)S(1)} %collective-permute-done.1.refs_1_, bf16[368,128]{1,0:T(8,128)(2,1)S(1)} %collective-permute-done.2.refs_2_, ...), custom_call_target="tpu_custom_call" | custom-call | tf_op jit(solution)/shard_map/pallas_call | solution.py:251
  34.4 2.0 %collective-permute-done.8.other_ref = f32[1096,128]{1,0:T(8,128)S(1)} collective-permute-done((f32[1096,128]{1,0:T(8,128)S(1)}, f32[1096,128]{1,0:T(8,128)S(1)}, u32[]{:S(2)}, u32[]{:S(2)}) %collective-permute-start.8) | collective-permute-done | bytes 561184 | tf_op jit(solution)/shard_map/ppermute | solution.py:211
  36.4 0.8 %copy-done.3 = f32[1096,128]{1,0:T(8,128)} copy-done((f32[1096,128]{1,0:T(8,128)}, f32[1096,128]{1,0:T(8,128)S(1)}, u32[]{:S(2)}) %copy-start.3) | copy-done | bytes 561176
  37.2 2.1 %shard_map.102 = (f32[1024,128]{1,0:T(8,128)}, f32[4,1024]{1,0:T(4,128)}, f32[1,128]{1,0:T(1,128)}) custom-call(f32[1096,128]{1,0:T(8,128)} %copy-done.1, f32[1096,128]{1,0:T(8,128)} %copy-done.3), custom_call_target="tpu_custom_call" | custom-call | tf_op jit(solution)/shard_map/pallas_call | solution.py:278
  (19 shorter events, 0.5 us)
Async XLA Ops:
  0.6 20.8 %copy-start = (bf16[1024,128]{1,0:T(8,128)(2,1)S(1)}, bf16[1024,128]{1,0:T(8,128)(2,1)}, u32[]{:S(2)}) copy-start(bf16[1024,128]{1,0:T(8,128)(2,1)} %refs_8_.1) | copy-start | bytes 786436
  2.1 2.4 %collective-permute-start = (bf16[4,1152]{1,0:T(4,128)(2,1)S(1)}, bf16[4,1152]{1,0:T(4,128)(2,1)S(1)}, u32[]{:S(2)}, u32[]{:S(2)}) collective-permute-start(bf16[4,1152]{1,0:T(4,128)(2,1)S(1)} %pad_maximum_fusion), channel_id=1, source_target_pairs={{0,1},{1,0},{2,3},{3,2},{4,5},{5,4},{6,7},{7,6},{8,9},{9,8},{10,11... | collective-permute-start | bytes 27656 | tf_op jit(solution)/shard_map/ppermute | solution.py:211
  6.2 8.3 %collective-permute-start.6 = (bf16[368,128]{1,0:T(8,128)(2,1)S(1)}, bf16[368,128]{1,0:T(8,128)(2,1)S(1)}, u32[]{:S(2)}, u32[]{:S(2)}) collective-permute-start(bf16[368,128]{1,0:T(8,128)(2,1)S(1)} %concatenate.11.refs_0_), channel_id=1, source_target_pairs={{0,12},{1,13},{2,14},{3,15},{4,8},{5,9},{6,10},{7,11},{8,4},{9,5},... | collective-permute-start | bytes 282632 | tf_op jit(solution)/shard_map/ppermute | solution.py:211
  10.9 8.6 %collective-permute-start.4 = (bf16[368,128]{1,0:T(8,128)(2,1)S(1)}, bf16[368,128]{1,0:T(8,128)(2,1)S(1)}, u32[]{:S(2)}, u32[]{:S(2)}) collective-permute-start(bf16[368,128]{1,0:T(8,128)(2,1)S(1)} %concatenate.11.refs_0_), channel_id=1, source_target_pairs={{0,8},{1,9},{2,10},{3,11},{4,12},{5,13},{6,14},{7,15},{8,0},{9,1},... | collective-permute-start | bytes 282632 | tf_op jit(solution)/shard_map/ppermute | solution.py:211
  10.9 10.1 %collective-permute-start.2 = (bf16[368,128]{1,0:T(8,128)(2,1)S(1)}, bf16[368,128]{1,0:T(8,128)(2,1)S(1)}, u32[]{:S(2)}, u32[]{:S(2)}) collective-permute-start(bf16[368,128]{1,0:T(8,128)(2,1)S(1)} %concatenate.11.refs_0_), channel_id=1, source_target_pairs={{0,4},{1,5},{2,6},{3,7},{4,0},{5,1},{6,2},{7,3},{8,12},{9,13},{10,... | collective-permute-start | bytes 282632 | tf_op jit(solution)/shard_map/ppermute | solution.py:211
  11.5 10.1 %collective-permute-start.1 = (bf16[368,128]{1,0:T(8,128)(2,1)S(1)}, bf16[368,128]{1,0:T(8,128)(2,1)S(1)}, u32[]{:S(2)}, u32[]{:S(2)}) collective-permute-start(bf16[368,128]{1,0:T(8,128)(2,1)S(1)} %concatenate.11.refs_0_), channel_id=1, source_target_pairs={{0,2},{1,3},{2,0},{3,1},{4,6},{5,7},{6,4},{7,5},{8,10},{9,11},{10,... | collective-permute-start | bytes 282632 | tf_op jit(solution)/shard_map/ppermute | solution.py:211
  14.5 7.1 %collective-permute-start.7 = (bf16[368,128]{1,0:T(8,128)(2,1)S(1)}, bf16[368,128]{1,0:T(8,128)(2,1)S(1)}, u32[]{:S(2)}, u32[]{:S(2)}) collective-permute-start(bf16[368,128]{1,0:T(8,128)(2,1)S(1)} %collective-permute-done.6.refs_6_), channel_id=1, source_target_pairs={{0,2},{1,3},{2,0},{3,1},{4,6},{5,7},{6,4},{7,5},{8,10},{9,11},{10,... | collective-permute-start | bytes 282632 | tf_op jit(solution)/shard_map/ppermute | solution.py:211
  19.4 5.6 %collective-permute-start.5 = (bf16[368,128]{1,0:T(8,128)(2,1)S(1)}, bf16[368,128]{1,0:T(8,128)(2,1)S(1)}, u32[]{:S(2)}, u32[]{:S(2)}) collective-permute-start(bf16[368,128]{1,0:T(8,128)(2,1)S(1)} %collective-permute-done.4.refs_4_), channel_id=1, source_target_pairs={{0,2},{1,3},{2,0},{3,1},{4,6},{5,7},{6,4},{7,5},{8,10},{9,11},{10,... | collective-permute-start | bytes 282632 | tf_op jit(solution)/shard_map/ppermute | solution.py:211
  21.0 5.1 %collective-permute-start.3 = (bf16[368,128]{1,0:T(8,128)(2,1)S(1)}, bf16[368,128]{1,0:T(8,128)(2,1)S(1)}, u32[]{:S(2)}, u32[]{:S(2)}) collective-permute-start(bf16[368,128]{1,0:T(8,128)(2,1)S(1)} %collective-permute-done.2.refs_2_), channel_id=1, source_target_pairs={{0,2},{1,3},{2,0},{3,1},{4,6},{5,7},{6,4},{7,5},{8,10},{9,11},{10,... | collective-permute-start | bytes 282632 | tf_op jit(solution)/shard_map/ppermute | solution.py:211
  26.0 0.7 %copy-start.2 = (f32[128]{0:T(128)S(1)}, f32[128]{0:T(128)}, u32[]{:S(2)}) copy-start(f32[128]{0:T(128)} %param.10) | copy-start | bytes 1540
  34.4 2.0 %copy-start.1 = (f32[1096,128]{1,0:T(8,128)}, f32[1096,128]{1,0:T(8,128)S(1)}, u32[]{:S(2)}) copy-start(f32[1096,128]{1,0:T(8,128)S(1)} %get-tuple-element.13.own_ref) | copy-start | bytes 1683460
  34.4 2.0 %collective-permute-start.8 = (f32[1096,128]{1,0:T(8,128)S(1)}, f32[1096,128]{1,0:T(8,128)S(1)}, u32[]{:S(2)}, u32[]{:S(2)}) collective-permute-start(f32[1096,128]{1,0:T(8,128)S(1)} %get-tuple-element.13.own_ref), channel_id=1, source_target_pairs={{0,1},{1,0},{2,3},{3,2},{4,5},{5,4},{6,7},{7,6},{8,9},{9,8},{10,11... | collective-permute-start | bytes 1683464 | tf_op jit(solution)/shard_map/ppermute | solution.py:211
  36.4 0.8 %copy-start.3 = (f32[1096,128]{1,0:T(8,128)}, f32[1096,128]{1,0:T(8,128)S(1)}, u32[]{:S(2)}) copy-start(f32[1096,128]{1,0:T(8,128)S(1)} %collective-permute-done.8.other_ref) | copy-start | bytes 1683460

commit v2 on v1

--- a/solution.py
+++ b/solution.py
@@ -11,6 +11,8 @@
 C = 32
 LANES = 128
 CORES = 2
+SMALL = 8 * 2**20
+LARGE = 24 * 2**20
 
 
 epsilon = 0.001
@@ -27,6 +29,88 @@
     return lax.dot_general(
         x, y, (((contract_x,), (contract_y,)), ((), ())), preferred_element_type=F32
     )
+
+
+def pack_kernel(
+    left_ref, right_ref, cot_ref, depth_ref, bias_ref, w_ref,
+    payload_ref, bias_out_ref, w_out_ref,
+    left_here, right_here, depth_here, sems,
+):
+    rows, width = left_here.shape
+    pairs = cot_ref.shape[0]
+    total = pairs // rows
+    alignment = width // C
+    tiles = width // LANES
+    group = LANES // C
+    chip_rows = CORES * rows
+    ends = (
+        (depth_ref, depth_here),
+        (left_ref, left_here),
+        (right_ref, right_here),
+        (cot_ref, payload_ref.at[:pairs, :]),
+        (bias_ref, bias_out_ref),
+        (w_ref, w_out_ref),
+    )
+    copies = [pltpu.make_async_copy(*pair, sems.at[k]) for k, pair in enumerate(ends)]
+    for copy in copies:
+        copy.start()
+    for copy in copies[:3]:
+        copy.wait()
+    left = left_here[...].astype(F32)
+    flat = jnp.concatenate([left[:, t * LANES : (t + 1) * LANES] for t in range(tiles)], 0)
+    flat = flat.astype(BF16)
+    row = iota((tiles * rows, LANES), 0)
+    lane = iota((tiles * rows, LANES), 1)
+    target = lax.rem(row, rows) * alignment + row // rows * group
+    turned = jnp.zeros((C, LANES), F32)
+    for q in range(group):
+        place = (lane == target + q).astype(F32).astype(BF16)
+        turned = turned + dot(flat, place, 0, 0)[q * C : (q + 1) * C, :]
+    lane = iota((C, LANES), 1)
+    depth = jnp.zeros((C, LANES), jnp.int32)
+    for i in range(rows):
+        depth = jnp.where(lane // alignment == i, depth_here[i], depth)
+    turned = jnp.where(lax.rem(lane, alignment) < depth, turned, 0.0)
+    payload_ref[pairs : pairs + C, :] = turned.astype(BF16)
+    own = right_here[...].astype(F32)
+    nothing = jnp.zeros((rows, LANES), F32)
+    parts = []
+    for t in range(tiles):
+        parts += [own[:, t * LANES : (t + 1) * LANES], nothing]
+    row = iota((chip_rows, LANES), 0)
+    depth = jnp.zeros((chip_rows, LANES), jnp.int32)
+    for i in range(rows):
+        depth = jnp.where(row == i, depth_here[i], depth)
+    parts.append(depth.astype(F32))
+    lane = row * LANES + iota((chip_rows, LANES), 1)
+    depth = jnp.zeros((chip_rows, LANES), jnp.int32)
+    for i in range(rows):
+        depth = jnp.where(lane // total == i, depth_here[i], depth)
+    parts.append(depth.astype(F32))
+    payload_ref[pairs + C :, :] = jnp.concatenate(parts, 0).astype(BF16)
+    for copy in copies[3:]:
+        copy.wait()
+
+
+def add_kernel(pairs, payload_ref, right_ref, depth_ref, out_ref):
+    rows, width = right_ref.shape
+    tiles = width // LANES
+    chip_rows = CORES * rows
+    begin = pairs + C
+    block = payload_ref[begin:, :].astype(F32)
+    other = right_ref[...].astype(F32)
+    row = iota((chip_rows, LANES), 0)
+    parts = []
+    for t in range(tiles):
+        both = jnp.concatenate([other[:, t * LANES : (t + 1) * LANES]] * CORES, 0)
+        parts.append(jnp.where(row < rows, block[t * chip_rows : (t + 1) * chip_rows], both))
+    depth = jnp.broadcast_to(depth_ref[...].astype(F32), (chip_rows, rows))
+    mine = iota((chip_rows, rows), 0) == iota((chip_rows, rows), 1) + rows
+    depth = jnp.sum(jnp.where(mine, depth, 0.0), axis=1, keepdims=True)
+    own = block[tiles * chip_rows : (tiles + 1) * chip_rows]
+    parts.append(jnp.where(row < rows, own, jnp.broadcast_to(depth, (chip_rows, LANES))))
+    parts.append(block[(tiles + 1) * chip_rows :])
+    out_ref[begin:, :] = jnp.concatenate(parts, 0).astype(BF16)
 
 
 def sum_kernel(rows, own_ref, other_ref, w_ref, right_ref, bias_ref):
@@ -47,11 +131,10 @@
 def main_kernel(sizes, *refs):
     rows, total, pieces, depth_rows = sizes
     piece = refs[:pieces]
-    w_ref, w_swap_ref, bias_ref = refs[pieces : pieces + 3]
-    update_ref, left_ref, partial_ref = refs[pieces + 3 : pieces + 6]
+    w_ref, partial_ref, spread, outer_own, inverse_own, depth_own = refs[pieces : pieces + 6]
     (
-        right_all, turned, spread, left_all, left_wide, cots, inverse, outer, outer_own,
-        window, picked, weights, g_left, g_right, stage,
+        right_all, turned, left_all, left_wide, cots, inverse, outer, window, picked, weights,
+        g_right, stage,
     ) = refs[pieces + 6 :]
     chip_rows = CORES * rows
     pairs = rows * total
@@ -189,20 +272,34 @@
             at = wide + (k * group + j) * tiles
             partial_ref[at : at + tiles, :] = jnp.where(row_of < depth, flat, 0.0)
 
+    inverse_own[...] = inverse[:8, :]
+    depth_own[...] = right_all[tiles, :8, :]
+
+
+def own_kernel(
+    rows, spread, outer_own, inverse_own, depth_own, payload_ref, w_swap_ref, bias_ref,
+    update_ref, left_ref, g_left, stage,
+):
+    pairs = update_ref.shape[0]
+    alignment = spread.shape[0] // rows
+    tiles = left_ref.shape[1] // LANES
+    group = LANES // C
     update = dot(outer_own[...], w_swap_ref[...], 0, 0)
     update_ref[...] = (update + bias_ref[...]).astype(BF16)
     for d in range(C):
-        g = dot(w_swap_ref[d * C : (d + 1) * C, :], piece[0][:pairs, :], 1, 1)
-        g_left[:, d * pairs : (d + 1) * pairs] = (g * inverse[:C, :]).astype(BF16)
+        g = dot(w_swap_ref[d * C : (d + 1) * C, :], payload_ref[:pairs, :], 1, 1)
+        g_left[:, d * pairs : (d + 1) * pairs] = (g * inverse_own[:1, :]).astype(BF16)
     left_grad = dot(g_left[...], spread[...], 1, 1)
     stage[...] = jnp.concatenate([left_grad] * group, 0).T
+    in_tile = iota((8, LANES), 1) // C
+    row_of = (iota((8, LANES), 0) * group + in_tile).astype(F32)
     for i in range(rows):
         flat = jnp.zeros((8, LANES), F32)
         for q in range(group):
             flat = jnp.where(
                 in_tile == q, stage[pl.ds(i * alignment + q, tiles, stride=group), :], flat
             )
-        flat = jnp.where(row_of < right_all[tiles, i : i + 1, :], flat, 0.0)
+        flat = jnp.where(row_of < depth_own[i : i + 1, :], flat, 0.0)
         for tile in range(tiles):
             left_ref[i : i + 1, tile * LANES : (tile + 1) * LANES] = flat[tile : tile + 1, :]
 
@@ -220,61 +317,87 @@
     pairs = rows * total
     chip_rows = CORES * rows
     tiles = width // LANES
-    depth_wide = jnp.broadcast_to(depth.astype(BF16)[:, None], (rows, LANES))
-    right_own = jnp.concatenate([right, depth_wide], 1)
-    right_chip = jnp.concatenate([right_own, swap(right_own, 1, size)], 0)
-    right_chip = right_chip.reshape(chip_rows, tiles + 1, LANES).swapaxes(0, 1)
-    row_ids = jnp.arange(alignment, dtype=jnp.int32)
-    own_mask = (row_ids[None, :] < depth[:, None]).astype(BF16)
-    own_left = left.reshape(rows, alignment, C) * own_mask[:, :, None]
-    depth_pairs = jnp.broadcast_to(depth.astype(BF16)[:, None], (rows, total))
-    used = pairs + C + (tiles + 1) * chip_rows + pairs // LANES
-    spare = -used % 16
-    payload = jnp.concatenate(
-        [
-            pair_cot.reshape(pairs, channels),
-            own_left.transpose(2, 0, 1).reshape(C, LANES),
-            right_chip.reshape(-1, LANES),
-            depth_pairs.reshape(-1, LANES),
-            jnp.zeros((spare, LANES), BF16),
+    used = pairs + C + (tiles + 2) * chip_rows
+    hbm = pl.BlockSpec(memory_space=pltpu.HBM)
+    vmem = pl.BlockSpec(memory_space=pltpu.VMEM)
+    right_other = swap(right, 1, size)
+    depth_other = swap(depth, 1, size)
+    given = (
+        left, right, pair_cot.reshape(pairs, channels), depth, bias.reshape(1, channels), w_out,
+    )
+    payload, bias_row, w_here = pl.pallas_call(
+        pack_kernel,
+        out_shape=(
+            pltpu.VMEM((used, LANES), BF16),
+            pltpu.VMEM((1, channels), F32),
+            pltpu.VMEM(w_out.shape, BF16),
+        ),
+        in_specs=[hbm] * 6,
+        out_specs=(vmem, vmem, vmem),
+        scratch_shapes=[
+            pltpu.VMEM(left.shape, BF16),
+            pltpu.VMEM(right.shape, BF16),
+            pltpu.SMEM(depth.shape, jnp.int32),
+            pltpu.SemaphoreType.DMA((6,)),
         ],
-        0,
-    )
+        compiler_params=pltpu.CompilerParams(vmem_limit_bytes=SMALL),
+        cost_estimate=pl.CostEstimate(flops=10**9, bytes_accessed=2**20, transcendentals=0),
+    )(*[pltpu.with_memory_space_constraint(x, pltpu.HBM) for x in given])
+    payload = pl.pallas_call(
+        functools.partial(add_kernel, pairs),
+        out_shape=jax.ShapeDtypeStruct((used, LANES), BF16),
+        input_output_aliases={0: 0},
+        compiler_params=pltpu.CompilerParams(vmem_limit_bytes=SMALL),
+    )(payload, right_other, depth_other.reshape(1, rows))
     far = [payload] + [swap(payload, mask, size) for mask in range(2 * CORES, size, 2 * CORES)]
     near = [swap(x, CORES, size) for x in far]
     arrived = [x for both in zip(far, near) for x in both]
-    w_swap = w_out.reshape(C, C, channels).swapaxes(0, 1).reshape(C * C, channels)
-    depth_rows = used + spare - pairs - C
+    w_swap = w_here.reshape(C, C, channels).swapaxes(0, 1).reshape(C * C, channels)
+    depth_rows = used - pairs - C
     partial_rows = C * C + chip_rows * tiles + 8
     count_lanes = chip_rows * rows * pieces
     chunk = 8
-    update, grad_left, partial = pl.pallas_call(
+    partial, spread, outer_own, inverse_own, depth_own = pl.pallas_call(
         functools.partial(main_kernel, (rows, total, pieces, depth_rows)),
         out_shape=(
-            jax.ShapeDtypeStruct((pairs, channels), BF16),
-            jax.ShapeDtypeStruct((rows, width), F32),
             jax.ShapeDtypeStruct((partial_rows, LANES), F32),
+            jax.ShapeDtypeStruct((rows * alignment, C * pairs), BF16),
+            jax.ShapeDtypeStruct((C * C, pairs), BF16),
+            jax.ShapeDtypeStruct((8, pairs), F32),
+            jax.ShapeDtypeStruct((8, LANES), F32),
         ),
         scratch_shapes=[
             pltpu.VMEM((tiles + 1, total, LANES), F32),
             pltpu.VMEM((width, LANES), F32),
-            pltpu.VMEM((rows * alignment, C * pairs), BF16),
             pltpu.VMEM((pieces * C, LANES), BF16),
             pltpu.VMEM((pieces * C, LANES), F32),
             pltpu.VMEM((pieces * pairs, channels), BF16),
             pltpu.VMEM((pieces * C, pairs), F32),
             pltpu.VMEM((chunk * C, pieces * pairs), BF16),
-            pltpu.VMEM((C * C, pairs), BF16),
             pltpu.VMEM((count_lanes, channels), F32),
             pltpu.VMEM((count_lanes, channels), BF16),
             pltpu.VMEM((C * LANES, LANES), BF16),
-            pltpu.VMEM((C, C * pairs), BF16),
             pltpu.VMEM((count_lanes // LANES * C, C * LANES), BF16),
             pltpu.VMEM((LANES, LANES), F32),
         ],
-        compiler_params=pltpu.CompilerParams(vmem_limit_bytes=40 * 1024 * 1024),
-    )(*arrived, w_out, w_swap, bias.reshape(1, channels))
+        compiler_params=pltpu.CompilerParams(vmem_limit_bytes=LARGE),
+    )(*arrived, w_here)
     other = swap(partial, 1, size)
+    update, grad_left = pl.pallas_call(
+        functools.partial(own_kernel, rows),
+        out_shape=(
+            jax.ShapeDtypeStruct((pairs, channels), BF16),
+            jax.ShapeDtypeStruct((rows, width), F32),
+        ),
+        scratch_shapes=[
+            pltpu.VMEM((C, C * pairs), BF16),
+            pltpu.VMEM((LANES, LANES), F32),
+        ],
+        compiler_params=pltpu.CompilerParams(vmem_limit_bytes=LARGE),
+        cost_estimate=pl.CostEstimate(
+            flops=8 * pairs * C * C * channels, bytes_accessed=4 * 2**20, transcendentals=0
+        ),
+    )(spread, outer_own, inverse_own, depth_own, payload, w_swap, bias_row)
     grad_w, grad_right, grad_bias = pl.pallas_call(
         functools.partial(sum_kernel, rows),
         out_shape=(
@@ -282,6 +405,7 @@
             jax.ShapeDtypeStruct((rows, width), F32),
             jax.ShapeDtypeStruct((1, channels), F32),
         ),
+        compiler_params=pltpu.CompilerParams(vmem_limit_bytes=SMALL),
     )(partial, other)
     return (
         update.reshape(rows, total, channels),

time: 39.6 us -> 30.8 us (0.78)
  local copies, waits for them, and re-layouts: 3.78 us -> 0.11 us
  other arithmetic: 2.87 us -> 0 us
  waiting for transfers between devices: 11 us -> 9.85 us
  starting transfers between devices: 11.1 us -> 10.3 us
    pallas_call x0 -> x3, Pallas kernels: none -> 3.52 us  [the longest x1 2.35 us: gathered(): pl.pallas_call(functools.partial(own_kernel, rows), out_shape=(jax.ShapeD...]
    pallas_call x1, Pallas kernels: 7.74 us -> 5.24 us  [gathered(): pl.pallas_call(functools.partial(main_kernel, (rows, total, pieces, depth...]
    unnamed x8 -> x0, local copies, waits for them, and re-layouts: 1.47 us -> none
    convert_element_type x2 -> x0, other arithmetic: 1.43 us -> none  [the longest x1 0.73 us: gathered(): own_mask = (row_ids[None, :] < depth[:, None]).astype(BF16)]
    pallas_call x1, Pallas kernels: 2.08 us -> 0.86 us  [gathered(): pl.pallas_call(functools.partial(sum_kernel, rows), out_shape=(jax.ShapeD...]
    ppermute x9 -> x10, waiting for transfers between devices: 11 us -> 9.85 us  [swap(): return lax.ppermute(x, 'pi', [(i, i ^ mask) for i in range(size)])]
    reshape x4 -> x1, local copies, waits for them, and re-layouts: 1.08 us -> 0.11 us  [gathered(): w_here.reshape(C, C, channels).swapaxes(0, 1).reshape(C * C, channels)]
    concatenate x1 -> x0, local copies, waits for them, and re-layouts: 0.91 us -> none  [gathered(): jnp.concatenate([pair_cot.reshape(pairs, channels), own_left.transpose(2,...]
  transfers between devices with their start and end apart: 9 -> 10, of which waited for: 5 -> 4; matrix products, arithmetic and copies ran while one was open for 5% -> 0% of each run, Pallas kernels for 0% -> 11%
where the time goes in v2:
time: 30.8 us; the launch traced here: 30.6 us
  starting transfers between devices  10.3 us (33%)
  waiting for transfers between devices  9.85 us (32%)
  Pallas kernels  9.62 us (31%)
  between operations  0.67 us (2%)
    ppermute x10, starting transfers between devices, swap(): return lax.ppermute(x, 'pi', [(i, i ^ mask) for i in range(size)])  10.3 us
    ppermute x10, waiting for transfers between devices, swap(): return lax.ppermute(x, 'pi', [(i, i ^ mask) for i in range(size)])  9.85 us
    pallas_call x1, Pallas kernels, gathered(): pl.pallas_call(functools.partial(main_kernel, (rows, total, pieces, depth...  5.24 us
    pallas_call x1, Pallas kernels, gathered(): pl.pallas_call(functools.partial(own_kernel, rows), out_shape=(jax.ShapeD...  2.35 us
    pallas_call x1, Pallas kernels, gathered(): pl.pallas_call(pack_kernel, out_shape=(pltpu.VMEM((used, LANES), BF16), p...  1.09 us
    pallas_call x1, Pallas kernels, gathered(): pl.pallas_call(functools.partial(sum_kernel, rows), out_shape=(jax.ShapeD...  0.86 us
  transfers between devices with their start and end apart: 10, of which 4 were waited for; matrix products, arithmetic and copies ran while one was open for 0% of the time, Pallas kernels for 11%

profile of v2, /device:TPU:0, one launch (start us, length us, event | category | flops | bytes accessed | tf_op | source)
XLA Modules:
  0.0 30.6 jit_solution(2014435167467695185)
XLA Ops:
  0.6 0.5 %collective-permute-start = (bf16[4,1024]{1,0:T(4,128)(2,1)}, bf16[4,1024]{1,0:T(4,128)(2,1)S(1)}, u32[]{:S(2)}, u32[]{:S(2)}) collective-permute-start(bf16[4,1024]{1,0:T(4,128)(2,1)} %right_ref.1), channel_id=1, source_target_pairs={{0,1},{1,0},{2,3},{3,2},{4,5},{5,4},{6,7},{7,6},{8,9},{9,8},{10,11... | collective-permute-start | bytes 24584 | tf_op jit(solution)/shard_map/ppermute | solution.py:308
  1.2 0.1 collective-permute-start.1
  1.2 1.1 %shard_map.101 = (bf16[368,128]{1,0:T(8,128)(2,1)S(1)}, f32[1,128]{1,0:T(1,128)S(1)}, bf16[1024,128]{1,0:T(8,128)(2,1)S(1)}) custom-call(bf16[4,1024]{1,0:T(4,128)(2,1)} %left_ref.1, bf16[4,1024]{1,0:T(4,128)(2,1)} %right_ref.1, bf16[256,128]{1,0:T(8,128)(2,1)} %bitcast.12, s32[4]{0:T(128)} %depth_ref.1, f32[1,128]{1,0:T(1,128)} %bitcast.14, ...), custom_call_target="tpu_custom_call" | custom-call | flops 1000000000 | bytes 1048576 | tf_op jit(solution)/shard_map/pallas_call | solution.py:328
  2.3 0.1 collective-permute-done.1
  2.4 0.0 collective-permute-done.right_ref
  2.4 0.1 shard_map.102.refs_0_.payload_ref
  2.5 2.9 %collective-permute-start.3 = (bf16[368,128]{1,0:T(8,128)(2,1)S(1)}, bf16[368,128]{1,0:T(8,128)(2,1)S(1)}, u32[]{:S(2)}, u32[]{:S(2)}) collective-permute-start(bf16[368,128]{1,0:T(8,128)(2,1)S(1)} %shard_map.102.refs_0_.payload_ref), channel_id=1, source_target_pairs={{0,4},{1,5},{2,6},{3,7},{4,0},{5,1},{6,2},{7,3},{8,12},{9,13},{10,... | collective-permute-start | bytes 282632 | tf_op jit(solution)/shard_map/ppermute | solution.py:308
  5.4 2.6 %collective-permute-start.5 = (bf16[368,128]{1,0:T(8,128)(2,1)S(1)}, bf16[368,128]{1,0:T(8,128)(2,1)S(1)}, u32[]{:S(2)}, u32[]{:S(2)}) collective-permute-start(bf16[368,128]{1,0:T(8,128)(2,1)S(1)} %shard_map.102.refs_0_.payload_ref), channel_id=1, source_target_pairs={{0,8},{1,9},{2,10},{3,11},{4,12},{5,13},{6,14},{7,15},{8,0},{9,1},... | collective-permute-start | bytes 282632 | tf_op jit(solution)/shard_map/ppermute | solution.py:308
  8.0 0.0 collective-permute-start.7
  8.0 1.7 %collective-permute-start.2 = (bf16[368,128]{1,0:T(8,128)(2,1)S(1)}, bf16[368,128]{1,0:T(8,128)(2,1)S(1)}, u32[]{:S(2)}, u32[]{:S(2)}) collective-permute-start(bf16[368,128]{1,0:T(8,128)(2,1)S(1)} %shard_map.102.refs_0_.payload_ref), channel_id=1, source_target_pairs={{0,2},{1,3},{2,0},{3,1},{4,6},{5,7},{6,4},{7,5},{8,10},{9,11},{10,... | collective-permute-start | bytes 282632 | tf_op jit(solution)/shard_map/ppermute | solution.py:308
  9.8 0.0 collective-permute-done.3.refs_2_
  9.8 0.4 %collective-permute-start.4 = (bf16[368,128]{1,0:T(8,128)(2,1)S(1)}, bf16[368,128]{1,0:T(8,128)(2,1)S(1)}, u32[]{:S(2)}, u32[]{:S(2)}) collective-permute-start(bf16[368,128]{1,0:T(8,128)(2,1)S(1)} %collective-permute-done.3.refs_2_), channel_id=1, source_target_pairs={{0,2},{1,3},{2,0},{3,1},{4,6},{5,7},{6,4},{7,5},{8,10},{9,11},{10,... | collective-permute-start | bytes 282632 | tf_op jit(solution)/shard_map/ppermute | solution.py:308
  10.1 5.7 %collective-permute-done.5.refs_4_ = bf16[368,128]{1,0:T(8,128)(2,1)S(1)} collective-permute-done((bf16[368,128]{1,0:T(8,128)(2,1)S(1)}, bf16[368,128]{1,0:T(8,128)(2,1)S(1)}, u32[]{:S(2)}, u32[]{:S(2)}) %collective-permute-start.5) | collective-permute-done | bytes 94240 | tf_op jit(solution)/shard_map/ppermute | solution.py:308
  15.8 1.5 %collective-permute-start.6 = (bf16[368,128]{1,0:T(8,128)(2,1)S(1)}, bf16[368,128]{1,0:T(8,128)(2,1)S(1)}, u32[]{:S(2)}, u32[]{:S(2)}) collective-permute-start(bf16[368,128]{1,0:T(8,128)(2,1)S(1)} %collective-permute-done.5.refs_4_), channel_id=1, source_target_pairs={{0,2},{1,3},{2,0},{3,1},{4,6},{5,7},{6,4},{7,5},{8,10},{9,11},{10,... | collective-permute-start | bytes 282632 | tf_op jit(solution)/shard_map/ppermute | solution.py:308
  17.4 0.5 %collective-permute-start.8 = (bf16[368,128]{1,0:T(8,128)(2,1)S(1)}, bf16[368,128]{1,0:T(8,128)(2,1)S(1)}, u32[]{:S(2)}, u32[]{:S(2)}) collective-permute-start(bf16[368,128]{1,0:T(8,128)(2,1)S(1)} %collective-permute-done.7.refs_6_), channel_id=1, source_target_pairs={{0,2},{1,3},{2,0},{3,1},{4,6},{5,7},{6,4},{7,5},{8,10},{9,11},{10,... | collective-permute-start | bytes 282632 | tf_op jit(solution)/shard_map/ppermute | solution.py:308
  17.9 0.0 collective-permute-done.2.refs_1_
  17.9 2.5 %collective-permute-done.6.refs_5_ = bf16[368,128]{1,0:T(8,128)(2,1)S(1)} collective-permute-done((bf16[368,128]{1,0:T(8,128)(2,1)S(1)}, bf16[368,128]{1,0:T(8,128)(2,1)S(1)}, u32[]{:S(2)}, u32[]{:S(2)}) %collective-permute-start.6) | collective-permute-done | bytes 94240 | tf_op jit(solution)/shard_map/ppermute | solution.py:308
  20.4 1.5 %collective-permute-done.8.refs_7_ = bf16[368,128]{1,0:T(8,128)(2,1)S(1)} collective-permute-done((bf16[368,128]{1,0:T(8,128)(2,1)S(1)}, bf16[368,128]{1,0:T(8,128)(2,1)S(1)}, u32[]{:S(2)}, u32[]{:S(2)}) %collective-permute-start.8) | collective-permute-done | bytes 94240 | tf_op jit(solution)/shard_map/ppermute | solution.py:308
  21.9 5.2 %shard_map.103 = (f32[1096,128]{1,0:T(8,128)S(1)}, bf16[128,8192]{1,0:T(8,128)(2,1)S(1)}, bf16[1024,256]{1,0:T(8,128)(2,1)S(1)}, f32[8,256]{1,0:T(8,128)S(1)}, f32[8,128]{1,0:T(8,128)S(1)}) custom-call(bf16[368,128]{1,0:T(8,128)(2,1)S(1)} %shard_map.102.refs_0_.payload_ref, bf16[368,128]{1,0:T(8,128)(2,1)S(1)} %collective-permute-done.2.refs_1_, ...), custom_call_target="tpu_custom_call" | custom-call | tf_op jit(solution)/shard_map/pallas_call | solution.py:360
  27.2 0.1 collective-permute-start.9
  27.2 0.1 copy.12
  27.4 2.4 %shard_map.104 = (bf16[256,128]{1,0:T(8,128)(2,1)}, f32[4,1024]{1,0:T(4,128)}) custom-call(bf16[128,8192]{1,0:T(8,128)(2,1)S(1)} %get-tuple-element.20.spread, bf16[1024,256]{1,0:T(8,128)(2,1)S(1)} %get-tuple-element.21.outer_own, f32[8,256]{1,0:T(8,128)S(1)} %get-tuple-element.22.inverse_own, f32[8,128]{1,0:T(8,128)S(1)} %get-tuple-element.23.depth_own, ...), custom_call_target="tpu_custom_call" | custom-call | flops 268435456 | bytes 4194304 | tf_op jit(solution)/shard_map/pallas_call | solution.py:386
  29.7 0.0 collective-permute-done.9.other_ref
  29.7 0.9 %shard_map.105 = (f32[1024,128]{1,0:T(8,128)}, f32[4,1024]{1,0:T(4,128)}, f32[1,128]{1,0:T(1,128)}) custom-call(f32[1096,128]{1,0:T(8,128)S(1)} %get-tuple-element.27.own_ref, f32[1096,128]{1,0:T(8,128)S(1)} %collective-permute-done.9.other_ref), custom_call_target="tpu_custom_call" | custom-call | tf_op jit(solution)/shard_map/pallas_call | solution.py:401
  (2 shorter events, 0.0 us)
Async XLA Ops:
  0.6 1.8 %collective-permute-start = (bf16[4,1024]{1,0:T(4,128)(2,1)}, bf16[4,1024]{1,0:T(4,128)(2,1)S(1)}, u32[]{:S(2)}, u32[]{:S(2)}) collective-permute-start(bf16[4,1024]{1,0:T(4,128)(2,1)} %right_ref.1), channel_id=1, source_target_pairs={{0,1},{1,0},{2,3},{3,2},{4,5},{5,4},{6,7},{7,6},{8,9},{9,8},{10,11... | collective-permute-start | bytes 24584 | tf_op jit(solution)/shard_map/ppermute | solution.py:308
  1.2 1.3 %collective-permute-start.1 = (s32[4]{0:T(128)}, s32[4]{0:T(128)S(1)}, u32[]{:S(2)}, u32[]{:S(2)}) collective-permute-start(s32[4]{0:T(128)} %depth_ref.1), channel_id=1, source_target_pairs={{0,1},{1,0},{2,3},{3,2},{4,5},{5,4},{6,7},{7,6},{8,9},{9,8},{10,11... | collective-permute-start | bytes 56 | tf_op jit(solution)/shard_map/ppermute | solution.py:308
  2.5 7.3 %collective-permute-start.3 = (bf16[368,128]{1,0:T(8,128)(2,1)S(1)}, bf16[368,128]{1,0:T(8,128)(2,1)S(1)}, u32[]{:S(2)}, u32[]{:S(2)}) collective-permute-start(bf16[368,128]{1,0:T(8,128)(2,1)S(1)} %shard_map.102.refs_0_.payload_ref), channel_id=1, source_target_pairs={{0,4},{1,5},{2,6},{3,7},{4,0},{5,1},{6,2},{7,3},{8,12},{9,13},{10,... | collective-permute-start | bytes 282632 | tf_op jit(solution)/shard_map/ppermute | solution.py:308
  5.4 10.4 %collective-permute-start.5 = (bf16[368,128]{1,0:T(8,128)(2,1)S(1)}, bf16[368,128]{1,0:T(8,128)(2,1)S(1)}, u32[]{:S(2)}, u32[]{:S(2)}) collective-permute-start(bf16[368,128]{1,0:T(8,128)(2,1)S(1)} %shard_map.102.refs_0_.payload_ref), channel_id=1, source_target_pairs={{0,8},{1,9},{2,10},{3,11},{4,12},{5,13},{6,14},{7,15},{8,0},{9,1},... | collective-permute-start | bytes 282632 | tf_op jit(solution)/shard_map/ppermute | solution.py:308
  8.0 9.3 %collective-permute-start.7 = (bf16[368,128]{1,0:T(8,128)(2,1)S(1)}, bf16[368,128]{1,0:T(8,128)(2,1)S(1)}, u32[]{:S(2)}, u32[]{:S(2)}) collective-permute-start(bf16[368,128]{1,0:T(8,128)(2,1)S(1)} %shard_map.102.refs_0_.payload_ref), channel_id=1, source_target_pairs={{0,12},{1,13},{2,14},{3,15},{4,8},{5,9},{6,10},{7,11},{8,4},{9,5},... | collective-permute-start | bytes 282632 | tf_op jit(solution)/shard_map/ppermute | solution.py:308
  8.0 9.8 %collective-permute-start.2 = (bf16[368,128]{1,0:T(8,128)(2,1)S(1)}, bf16[368,128]{1,0:T(8,128)(2,1)S(1)}, u32[]{:S(2)}, u32[]{:S(2)}) collective-permute-start(bf16[368,128]{1,0:T(8,128)(2,1)S(1)} %shard_map.102.refs_0_.payload_ref), channel_id=1, source_target_pairs={{0,2},{1,3},{2,0},{3,1},{4,6},{5,7},{6,4},{7,5},{8,10},{9,11},{10,... | collective-permute-start | bytes 282632 | tf_op jit(solution)/shard_map/ppermute | solution.py:308
  9.8 8.1 %collective-permute-start.4 = (bf16[368,128]{1,0:T(8,128)(2,1)S(1)}, bf16[368,128]{1,0:T(8,128)(2,1)S(1)}, u32[]{:S(2)}, u32[]{:S(2)}) collective-permute-start(bf16[368,128]{1,0:T(8,128)(2,1)S(1)} %collective-permute-done.3.refs_2_), channel_id=1, source_target_pairs={{0,2},{1,3},{2,0},{3,1},{4,6},{5,7},{6,4},{7,5},{8,10},{9,11},{10,... | collective-permute-start | bytes 282632 | tf_op jit(solution)/shard_map/ppermute | solution.py:308
  15.8 4.6 %collective-permute-start.6 = (bf16[368,128]{1,0:T(8,128)(2,1)S(1)}, bf16[368,128]{1,0:T(8,128)(2,1)S(1)}, u32[]{:S(2)}, u32[]{:S(2)}) collective-permute-start(bf16[368,128]{1,0:T(8,128)(2,1)S(1)} %collective-permute-done.5.refs_4_), channel_id=1, source_target_pairs={{0,2},{1,3},{2,0},{3,1},{4,6},{5,7},{6,4},{7,5},{8,10},{9,11},{10,... | collective-permute-start | bytes 282632 | tf_op jit(solution)/shard_map/ppermute | solution.py:308
  17.4 4.6 %collective-permute-start.8 = (bf16[368,128]{1,0:T(8,128)(2,1)S(1)}, bf16[368,128]{1,0:T(8,128)(2,1)S(1)}, u32[]{:S(2)}, u32[]{:S(2)}) collective-permute-start(bf16[368,128]{1,0:T(8,128)(2,1)S(1)} %collective-permute-done.7.refs_6_), channel_id=1, source_target_pairs={{0,2},{1,3},{2,0},{3,1},{4,6},{5,7},{6,4},{7,5},{8,10},{9,11},{10,... | collective-permute-start | bytes 282632 | tf_op jit(solution)/shard_map/ppermute | solution.py:308
  27.2 2.5 %collective-permute-start.9 = (f32[1096,128]{1,0:T(8,128)S(1)}, f32[1096,128]{1,0:T(8,128)S(1)}, u32[]{:S(2)}, u32[]{:S(2)}) collective-permute-start(f32[1096,128]{1,0:T(8,128)S(1)} %get-tuple-element.27.own_ref), channel_id=1, source_target_pairs={{0,1},{1,0},{2,3},{3,2},{4,5},{5,4},{6,7},{7,6},{8,9},{9,8},{10,11... | collective-permute-start | bytes 1683464 | tf_op jit(solution)/shard_map/ppermute | solution.py:308

commit v3 on v2

--- a/solution.py
+++ b/solution.py
@@ -29,6 +29,14 @@
     return lax.dot_general(
         x, y, (((contract_x,), (contract_y,)), ((), ())), preferred_element_type=F32
     )
+
+
+def views(refs, used):
+    return [
+        ref.at[k * used : (k + 1) * used, :]
+        for ref in refs
+        for k in range(ref.shape[0] // used)
+    ]
 
 
 def pack_kernel(
@@ -73,17 +81,14 @@
     turned = jnp.where(lax.rem(lane, alignment) < depth, turned, 0.0)
     payload_ref[pairs : pairs + C, :] = turned.astype(BF16)
     own = right_here[...].astype(F32)
-    nothing = jnp.zeros((rows, LANES), F32)
-    parts = []
-    for t in range(tiles):
-        parts += [own[:, t * LANES : (t + 1) * LANES], nothing]
-    row = iota((chip_rows, LANES), 0)
-    depth = jnp.zeros((chip_rows, LANES), jnp.int32)
+    parts = [own[:, t * LANES : (t + 1) * LANES] for t in range(tiles)]
+    row = iota((8, LANES), 0)
+    depth = jnp.zeros((8, LANES), jnp.int32)
     for i in range(rows):
         depth = jnp.where(row == i, depth_here[i], depth)
     parts.append(depth.astype(F32))
-    lane = row * LANES + iota((chip_rows, LANES), 1)
-    depth = jnp.zeros((chip_rows, LANES), jnp.int32)
+    lane = row * LANES + iota((8, LANES), 1)
+    depth = jnp.zeros((8, LANES), jnp.int32)
     for i in range(rows):
         depth = jnp.where(lane // total == i, depth_here[i], depth)
     parts.append(depth.astype(F32))
@@ -92,30 +97,30 @@
         copy.wait()
 
 
-def add_kernel(pairs, payload_ref, right_ref, depth_ref, out_ref):
-    rows, width = right_ref.shape
-    tiles = width // LANES
-    chip_rows = CORES * rows
-    begin = pairs + C
-    block = payload_ref[begin:, :].astype(F32)
-    other = right_ref[...].astype(F32)
-    row = iota((chip_rows, LANES), 0)
-    parts = []
-    for t in range(tiles):
-        both = jnp.concatenate([other[:, t * LANES : (t + 1) * LANES]] * CORES, 0)
-        parts.append(jnp.where(row < rows, block[t * chip_rows : (t + 1) * chip_rows], both))
-    depth = jnp.broadcast_to(depth_ref[...].astype(F32), (chip_rows, rows))
-    mine = iota((chip_rows, rows), 0) == iota((chip_rows, rows), 1) + rows
-    depth = jnp.sum(jnp.where(mine, depth, 0.0), axis=1, keepdims=True)
-    own = block[tiles * chip_rows : (tiles + 1) * chip_rows]
-    parts.append(jnp.where(row < rows, own, jnp.broadcast_to(depth, (chip_rows, LANES))))
-    parts.append(block[(tiles + 1) * chip_rows :])
-    out_ref[begin:, :] = jnp.concatenate(parts, 0).astype(BF16)
-
-
-def sum_kernel(rows, own_ref, other_ref, w_ref, right_ref, bias_ref):
+def collect_kernel(used, begin, *refs):
+    piece, out_ref = views(refs[:-1], used), refs[-1]
+    tail = [ref[begin:, :].astype(F32) for ref in piece]
+    tiles = C * C // LANES + 1
+    half = out_ref.shape[0] // tiles
+    rows = half // len(piece)
+    for tile in range(tiles):
+        part = jnp.concatenate([x[tile * rows : (tile + 1) * rows] for x in tail], 0)
+        out_ref[tile * half : (tile + 1) * half, :] = part.astype(BF16)
+
+
+def sum_kernel(
+    rows, own_ref, other_ref, update_here, left_here,
+    update_ref, left_ref, w_ref, right_ref, bias_ref, w_here, right_here, bias_here, sems,
+):
+    copies = [
+        pltpu.make_async_copy(update_here, update_ref, sems.at[0]),
+        pltpu.make_async_copy(left_here, left_ref, sems.at[1]),
+        pltpu.make_async_copy(right_here, right_ref, sems.at[2]),
+        pltpu.make_async_copy(bias_here, bias_ref, sems.at[3]),
+    ]
+    copies[0].start()
+    copies[1].start()
     wide = w_ref.shape[0]
-    w_ref[...] = own_ref[:wide, :] + other_ref[:wide, :]
     core = lax.rem(lax.axis_index("pi"), CORES)
     tiles = right_ref.shape[1] // LANES
     begin = pl.multiple_of(wide + core * rows * tiles, 8)
@@ -123,98 +128,45 @@
     for row in range(rows):
         for tile in range(tiles):
             at = row * tiles + tile
-            right_ref[row : row + 1, tile * LANES : (tile + 1) * LANES] = part[at : at + 1, :]
+            right_here[row : row + 1, tile * LANES : (tile + 1) * LANES] = part[at : at + 1, :]
     last = wide + CORES * rows * tiles
-    bias_ref[...] = own_ref[last : last + 1, :] + other_ref[last : last + 1, :]
-
-
-def main_kernel(sizes, *refs):
-    rows, total, pieces, depth_rows = sizes
-    piece = refs[:pieces]
-    w_ref, partial_ref, spread, outer_own, inverse_own, depth_own = refs[pieces : pieces + 6]
-    (
-        right_all, turned, left_all, left_wide, cots, inverse, outer, window, picked, weights,
-        g_right, stage,
-    ) = refs[pieces + 6 :]
+    bias_here[...] = own_ref[last : last + 1, :] + other_ref[last : last + 1, :]
+    copies[2].start()
+    copies[3].start()
+    count = sems.shape[0] - 4
+    for k in range(count):
+        some = slice(k * wide // count, (k + 1) * wide // count)
+        w_here[some, :] = own_ref[some, :] + other_ref[some, :]
+        copies.append(pltpu.make_async_copy(w_here.at[some], w_ref.at[some], sems.at[4 + k]))
+        copies[-1].start()
+    for copy in copies:
+        copy.wait()
+
+
+def right_kernel(sizes, *refs):
+    rows, total, pieces, alignment, used, arrays = sizes
+    some = 8
+    piece = views(refs[:arrays], used)
+    w_ref, depth_ref, out_ref, w_swap_ref = refs[arrays : arrays + 4]
+    left_wide, window, picked, weights, g_right, stage, depths, w_wide = refs[arrays + 4 :]
     chip_rows = CORES * rows
     pairs = rows * total
     tiles = C * C // LANES
-    per_tile = LANES // total
     group = LANES // C
     me = lax.axis_index("pi")
     chip = me // CORES
-    at_left = pairs
-    at_right = pairs + C
-    at_depth = at_right + (tiles + 1) * chip_rows
-
+    at_depth = pairs + C + tiles * rows
+
+    w_wide[...] = w_ref[...].astype(F32)
+    for d in range(C):
+        w_swap_ref[d * C : (d + 1) * C, :] = w_wide[pl.ds(d, C, stride=C), :].astype(BF16)
     for m in range(pieces):
-        block = piece[m][at_right : at_right + depth_rows, :].astype(F32)
-        for tile in range(tiles + 1):
-            right_all[tile, m * chip_rows : (m + 1) * chip_rows, :] = block[
-                tile * chip_rows : (tile + 1) * chip_rows
-            ]
-        left_all[m * C : (m + 1) * C, :] = piece[m][at_left : at_left + C, :]
-        left_wide[m * C : (m + 1) * C, :] = piece[m][at_left : at_left + C, :].astype(F32)
-        cots[m * pairs : (m + 1) * pairs, :] = piece[m][:pairs, :]
-    place = lax.bitwise_xor(iota((total, LANES), 0), me * rows) == lax.rem(
-        iota((total, LANES), 1), total
-    )
-    place = place.astype(F32).astype(BF16)
-    for tile in range(tiles):
-        turned[tile * LANES : (tile + 1) * LANES, :] = dot(
-            right_all[tile].astype(BF16), place, 0, 0
-        )
-    depth_all = right_all[tiles].astype(BF16)
-    depth_lane = dot(depth_all, place, 0, 0)
-
-    for m in range(pieces):
-        block = piece[m][at_right : at_right + depth_rows, :].astype(F32)
-        for tile in range(pairs // LANES):
-            at = at_depth - at_right + tile
-            least = jnp.minimum(block[at : at + 1, :], depth_lane[:1, :])
-            inverse[m * C : (m + 1) * C, tile * LANES : (tile + 1) * LANES] = jnp.broadcast_to(
-                1.0 / (epsilon + least), (C, LANES)
-            )
-
-    alignment = spread.shape[0] // rows
-    alive = iota((alignment, LANES), 0).astype(F32) < depth_lane[:alignment, :]
-    part_of = iota((alignment, LANES), 1) // total
-    keep = [jnp.where(alive & (part_of == k), 1.0, 0.0).astype(F32) for k in range(per_tile)]
-    nothing = jnp.zeros((alignment, LANES), BF16)
-    for d in range(C):
-        block = turned[pl.ds(d, alignment, stride=C), :]
-        kept = [(block * keep[k]).astype(BF16) for k in range(per_tile)]
-        for i in range(rows):
-            for tile in range(pairs // LANES):
-                spread[
-                    i * alignment : (i + 1) * alignment,
-                    d * pairs + tile * LANES : d * pairs + (tile + 1) * LANES,
-                ] = kept[i % per_tile] if i // per_tile == tile else nothing
-
-    chunk = outer.shape[0] // C
-
-    def some_channels(step, carry):
-        for k in range(chunk):
-            d = step * chunk + k
-            begin = pl.multiple_of(d * pairs, pairs)
-            o = dot(left_all[...], spread[:, pl.ds(begin, pairs)], 1, 0)
-            o = (o * inverse[...]).astype(BF16)
-            for m in range(pieces):
-                outer[k * C : (k + 1) * C, m * pairs : (m + 1) * pairs] = o[m * C : (m + 1) * C, :]
-        own_at = pl.multiple_of(step * chunk * C, chunk * C)
-        outer_own[pl.ds(own_at, chunk * C), :] = outer[:, :pairs]
-        grad = dot(outer[...], cots[...], 1, 0)
-        for k in range(chunk):
-            partial_ref[pl.ds(step * chunk + k, C, stride=C), :] = grad[k * C : (k + 1) * C, :]
-        return carry
-
-    lax.fori_loop(0, C // chunk, some_channels, 0)
-    wide = C * C
-    last = wide + chip_rows * tiles
-    partial_ref[last : last + 8, :] = dot(
-        jnp.ones((8, pieces * pairs), BF16), cots[...], 1, 0
-    )
-
+        left_wide[m * C : (m + 1) * C, :] = piece[m][pairs : pairs + C, :].astype(F32)
+    tail = [ref[at_depth : at_depth + 16, :].astype(F32)[:rows] for ref in piece]
+    other = jnp.broadcast_to(depth_ref[...].astype(F32), (rows, rows))
+    other = jnp.where(iota((rows, rows), 0) == iota((rows, rows), 1), other, 0.0)
+    other = jnp.broadcast_to(jnp.sum(other, axis=1, keepdims=True), (rows, LANES))
+    depths[...] = jnp.concatenate([tail[0], other, jnp.zeros((8, LANES), F32)], 0)
     half = lax.rem(chip, 16 // chip_rows)
     for m in range(pieces):
         for i in range(rows):
@@ -231,20 +183,21 @@
             pl.ds(j, mine, stride=chip_rows), :
         ].astype(BF16)
     count_lanes = chip_rows * mine
-    row = iota((total, count_lanes), 0)
-    lane = iota((total, count_lanes), 1)
-    own_lane = lax.rem(lane, mine)
-    from_i = row == lax.rem(own_lane, pieces) * chip_rows + own_lane // pieces
-    from_j = lax.bitwise_xor(row, me * rows) == chip * chip_rows + lane // mine
-    depth_i = dot(depth_all, from_i.astype(F32).astype(BF16), 0, 0)[:8, :]
-    depth_j = dot(depth_all, from_j.astype(F32).astype(BF16), 0, 0)[:8, :]
+    lane = lax.rem(iota((mine, count_lanes), 1), mine)
+    from_i = iota((mine, count_lanes), 0) == lax.rem(lane, pieces) * rows + lane // pieces
+    lane = iota((16, count_lanes), 1) // mine
+    from_j = iota((16, count_lanes), 0) == lax.bitwise_xor(lane, lax.rem(me, CORES) * rows)
+    depth_i = jnp.concatenate(tail, 0).astype(BF16)
+    depth_i = dot(depth_i, from_i.astype(F32).astype(BF16), 0, 0)[:8, :]
+    depth_j = dot(depths[...].astype(BF16), from_j.astype(F32).astype(BF16), 0, 0)[:8, :]
     inverse_right = (1.0 / (epsilon + jnp.minimum(depth_i, depth_j)))[:1, :]
     for c in range(C):
-        g = dot(w_ref[c * C : (c + 1) * C, :], picked[...], 1, 1)
-        g = (g * inverse_right).astype(BF16)
+        if c % some == 0:
+            g = dot(w_ref[c * C : (c + some) * C, :], picked[...], 1, 1)
+            g = (g * inverse_right).astype(BF16)
         for k in range(count_lanes // LANES):
             g_right[k * C : (k + 1) * C, c * LANES : (c + 1) * LANES] = g[
-                :, k * LANES : (k + 1) * LANES
+                c % some * C : (c % some + 1) * C, k * LANES : (k + 1) * LANES
             ]
         feature = left_wide[pl.ds(c, pieces, stride=C), :]
         turns = [feature] + [pltpu.roll(feature, k * alignment, 1) for k in range(1, rows)]
@@ -268,18 +221,93 @@
                     in_tile == q, stage[pl.ds(j * alignment + q, tiles, stride=group), :], flat
                 )
             residue = lax.bitwise_xor(k * group + j, lax.rem(me, CORES) * rows)
-            depth = right_all[tiles, pl.ds(residue, 1), :]
-            at = wide + (k * group + j) * tiles
-            partial_ref[at : at + tiles, :] = jnp.where(row_of < depth, flat, 0.0)
-
-    inverse_own[...] = inverse[:8, :]
-    depth_own[...] = right_all[tiles, :8, :]
+            depth = depths[pl.ds(residue, 1), :]
+            at = (k * group + j) * tiles
+            out_ref[at : at + tiles, :] = jnp.where(row_of < depth, flat, 0.0)
+
+
+def main_kernel(sizes, *refs):
+    rows, total, pieces, used, arrays, route = sizes
+    piece = views(refs[:arrays], used)
+    own_ref, other_ref, right_ref = refs[arrays : arrays + 3]
+    partial_ref, spread, outer_own, inverse_own = refs[arrays + 3 : arrays + 7]
+    turned, left_all, cots, inverse, outer = refs[arrays + 7 :]
+    pairs = rows * total
+    tiles = C * C // LANES
+    per_tile = LANES // total
+    me = lax.axis_index("pi")
+    at_pairs = pairs + C + tiles * rows
+
+    for m in range(pieces):
+        left_all[m * C : (m + 1) * C, :] = piece[m][pairs : pairs + C, :]
+        cots[m * pairs : (m + 1) * pairs, :] = piece[m][:pairs, :]
+    half = total // CORES
+    row = iota((total, LANES), 0)
+    core = lax.rem(me, CORES)
+    step = jnp.zeros((total, LANES), jnp.int32)
+    for m, offset in enumerate(offsets(route)):
+        for k in range(CORES):
+            at = row // rows == k * pieces + m
+            step = jnp.where(at, jnp.where(core == k, offset[0], offset[1]) + k, step)
+    source = lax.bitwise_xor(step, me) * rows + lax.rem(row, rows)
+    place = (source == lax.rem(iota((total, LANES), 1), total)).astype(F32).astype(BF16)
+    both = [
+        jnp.concatenate([ref[t * half : (t + 1) * half, :] for ref in (own_ref, other_ref)], 0)
+        for t in range(tiles + 1)
+    ]
+    for tile in range(tiles):
+        turned[tile * LANES : (tile + 1) * LANES, :] = dot(both[tile], place, 0, 0)
+    depth_lane = dot(both[tiles], place, 0, 0)
+
+    for m in range(pieces):
+        block = piece[m][at_pairs : at_pairs + 16, :].astype(F32)
+        for tile in range(pairs // LANES):
+            least = jnp.minimum(block[8 + tile : 9 + tile, :], depth_lane[:1, :])
+            inverse[m : m + 1, tile * LANES : (tile + 1) * LANES] = 1.0 / (epsilon + least)
+
+    alignment = spread.shape[0] // rows
+    alive = iota((alignment, LANES), 0).astype(F32) < depth_lane[:alignment, :]
+    part_of = iota((alignment, LANES), 1) // total
+    keep = [jnp.where(alive & (part_of == k), 1.0, 0.0).astype(F32) for k in range(per_tile)]
+    nothing = jnp.zeros((alignment, LANES), BF16)
+    for d in range(C):
+        block = turned[pl.ds(d, alignment, stride=C), :]
+        kept = [(block * keep[k]).astype(BF16) for k in range(per_tile)]
+        for i in range(rows):
+            for tile in range(pairs // LANES):
+                spread[
+                    i * alignment : (i + 1) * alignment,
+                    d * pairs + tile * LANES : d * pairs + (tile + 1) * LANES,
+                ] = kept[i % per_tile] if i // per_tile == tile else nothing
+
+    chunk = 8
+    for d in range(C):
+        o = dot(left_all[...], spread[:, d * pairs : (d + 1) * pairs], 1, 0)
+        for m in range(pieces):
+            outer[d * C : (d + 1) * C, m * pairs : (m + 1) * pairs] = (
+                o[m * C : (m + 1) * C, :] * inverse[m : m + 1, :]
+            ).astype(BF16)
+        if d % chunk == chunk - 1:
+            first = d + 1 - chunk
+            some = slice(first * C, (d + 1) * C)
+            outer_own[some, :] = outer[some, :pairs]
+            grad = dot(outer[some, :], cots[...], 1, 0)
+            for k in range(chunk):
+                partial_ref[pl.ds(first + k, C, stride=C), :] = grad[k * C : (k + 1) * C, :]
+    wide = C * C
+    last = wide + right_ref.shape[0]
+    partial_ref[wide:last, :] = right_ref[...]
+    partial_ref[last : last + 8, :] = dot(
+        jnp.ones((8, pieces * pairs), BF16), cots[...], 1, 0
+    )
+    inverse_own[...] = inverse[...]
 
 
 def own_kernel(
-    rows, spread, outer_own, inverse_own, depth_own, payload_ref, w_swap_ref, bias_ref,
+    rows, spread, outer_own, inverse_own, payload_ref, w_swap_ref, bias_ref,
     update_ref, left_ref, g_left, stage,
 ):
+    some = 8
     pairs = update_ref.shape[0]
     alignment = spread.shape[0] // rows
     tiles = left_ref.shape[1] // LANES
@@ -287,25 +315,51 @@
     update = dot(outer_own[...], w_swap_ref[...], 0, 0)
     update_ref[...] = (update + bias_ref[...]).astype(BF16)
     for d in range(C):
-        g = dot(w_swap_ref[d * C : (d + 1) * C, :], payload_ref[:pairs, :], 1, 1)
-        g_left[:, d * pairs : (d + 1) * pairs] = (g * inverse_own[:1, :]).astype(BF16)
-    left_grad = dot(g_left[...], spread[...], 1, 1)
-    stage[...] = jnp.concatenate([left_grad] * group, 0).T
+        if d % some == 0:
+            g = dot(w_swap_ref[d * C : (d + some) * C, :], payload_ref[:pairs, :], 1, 1)
+            g = (g * inverse_own[:1, :]).astype(BF16)
+        g_left[:, d * pairs : (d + 1) * pairs] = g[d % some * C : (d % some + 1) * C, :]
+    left_grad = dot(spread[...], g_left[...], 1, 1)
+    stage[...] = jnp.concatenate([left_grad] * group, 1)
     in_tile = iota((8, LANES), 1) // C
     row_of = (iota((8, LANES), 0) * group + in_tile).astype(F32)
+    at_depth = pairs + C + tiles * rows
+    depth = payload_ref[at_depth : at_depth + 16, :].astype(F32)
     for i in range(rows):
         flat = jnp.zeros((8, LANES), F32)
         for q in range(group):
             flat = jnp.where(
                 in_tile == q, stage[pl.ds(i * alignment + q, tiles, stride=group), :], flat
             )
-        flat = jnp.where(row_of < depth_own[i : i + 1, :], flat, 0.0)
+        flat = jnp.where(row_of < depth[i : i + 1, :], flat, 0.0)
         for tile in range(tiles):
             left_ref[i : i + 1, tile * LANES : (tile + 1) * LANES] = flat[tile : tile + 1, :]
 
 
-def swap(x, mask, size):
-    return lax.ppermute(x, "pi", [(i, i ^ mask) for i in range(size)])
+def swap(x, masks, size):
+    return lax.ppermute(x, "pi", [(i, i ^ masks[i % CORES]) for i in range(size)])
+
+
+def route_of(size):
+    near, middle, far = CORES, size // 4, size // 2
+    if near * 2 == middle:
+        return (
+            ((0,), (far + middle + near,) * CORES),
+            ((0,), (far + middle,) * CORES),
+            ((0,), (near,) * CORES),
+            ((3,), (middle,) * CORES),
+            ((0,), (middle,) * CORES),
+            ((0,), (far,) * CORES),
+            ((6,), (near,) * CORES),
+        )
+    return tuple(((0,), (offset,) * CORES) for offset in range(CORES, size, CORES))
+
+
+def offsets(route):
+    found = [(0,) * CORES]
+    for sources, hops in route:
+        found += [tuple(a ^ b for a, b in zip(found[k], hops)) for k in sources]
+    return found
 
 
 def gathered(left, right, depth, w_out, bias, pair_cot):
@@ -317,11 +371,10 @@
     pairs = rows * total
     chip_rows = CORES * rows
     tiles = width // LANES
-    used = pairs + C + (tiles + 2) * chip_rows
+    used = pairs + C + tiles * rows + 16
     hbm = pl.BlockSpec(memory_space=pltpu.HBM)
     vmem = pl.BlockSpec(memory_space=pltpu.VMEM)
-    right_other = swap(right, 1, size)
-    depth_other = swap(depth, 1, size)
+    depth_other = swap(depth, (1, 1), size)
     given = (
         left, right, pair_cot.reshape(pairs, channels), depth, bias.reshape(1, channels), w_out,
     )
@@ -343,52 +396,59 @@
         compiler_params=pltpu.CompilerParams(vmem_limit_bytes=SMALL),
         cost_estimate=pl.CostEstimate(flops=10**9, bytes_accessed=2**20, transcendentals=0),
     )(*[pltpu.with_memory_space_constraint(x, pltpu.HBM) for x in given])
-    payload = pl.pallas_call(
-        functools.partial(add_kernel, pairs),
-        out_shape=jax.ShapeDtypeStruct((used, LANES), BF16),
-        input_output_aliases={0: 0},
+    arrived = [payload]
+    place = {0: payload}
+    route = route_of(size)
+    for sources, hops in route:
+        message = [place[k] for k in sources]
+        message = swap(jnp.concatenate(message, 0) if len(message) > 1 else message[0], hops, size)
+        if len(sources) == 1:
+            place[sum(x.shape[0] for x in arrived) // used] = message
+        arrived.append(message)
+    mine = pl.pallas_call(
+        functools.partial(collect_kernel, used, pairs + C),
+        out_shape=pltpu.VMEM((total // CORES * (tiles + 1), LANES), BF16),
         compiler_params=pltpu.CompilerParams(vmem_limit_bytes=SMALL),
-    )(payload, right_other, depth_other.reshape(1, rows))
-    far = [payload] + [swap(payload, mask, size) for mask in range(2 * CORES, size, 2 * CORES)]
-    near = [swap(x, CORES, size) for x in far]
-    arrived = [x for both in zip(far, near) for x in both]
-    w_swap = w_here.reshape(C, C, channels).swapaxes(0, 1).reshape(C * C, channels)
-    depth_rows = used - pairs - C
-    partial_rows = C * C + chip_rows * tiles + 8
+    )(*arrived)
+    theirs = swap(mine, (1, 1), size)
     count_lanes = chip_rows * rows * pieces
-    chunk = 8
-    partial, spread, outer_own, inverse_own, depth_own = pl.pallas_call(
-        functools.partial(main_kernel, (rows, total, pieces, depth_rows)),
-        out_shape=(
-            jax.ShapeDtypeStruct((partial_rows, LANES), F32),
-            jax.ShapeDtypeStruct((rows * alignment, C * pairs), BF16),
-            jax.ShapeDtypeStruct((C * C, pairs), BF16),
-            jax.ShapeDtypeStruct((8, pairs), F32),
-            jax.ShapeDtypeStruct((8, LANES), F32),
-        ),
+    right_partial, w_swap = pl.pallas_call(
+        functools.partial(right_kernel, (rows, total, pieces, alignment, used, len(arrived))),
+        out_shape=(pltpu.VMEM((chip_rows * tiles, LANES), F32), pltpu.VMEM(w_out.shape, BF16)),
         scratch_shapes=[
-            pltpu.VMEM((tiles + 1, total, LANES), F32),
-            pltpu.VMEM((width, LANES), F32),
-            pltpu.VMEM((pieces * C, LANES), BF16),
             pltpu.VMEM((pieces * C, LANES), F32),
-            pltpu.VMEM((pieces * pairs, channels), BF16),
-            pltpu.VMEM((pieces * C, pairs), F32),
-            pltpu.VMEM((chunk * C, pieces * pairs), BF16),
             pltpu.VMEM((count_lanes, channels), F32),
             pltpu.VMEM((count_lanes, channels), BF16),
             pltpu.VMEM((C * LANES, LANES), BF16),
             pltpu.VMEM((count_lanes // LANES * C, C * LANES), BF16),
             pltpu.VMEM((LANES, LANES), F32),
+            pltpu.VMEM((16, LANES), F32),
+            pltpu.VMEM(w_out.shape, F32),
         ],
         compiler_params=pltpu.CompilerParams(vmem_limit_bytes=LARGE),
-    )(*arrived, w_here)
-    other = swap(partial, 1, size)
+        cost_estimate=pl.CostEstimate(flops=10**9, bytes_accessed=2**20, transcendentals=0),
+    )(*arrived, w_here, depth_other.reshape(1, rows))
+    partial, spread, outer_own, inverse_own = pl.pallas_call(
+        functools.partial(main_kernel, (rows, total, pieces, used, len(arrived), route)),
+        out_shape=(
+            pltpu.VMEM((C * C + chip_rows * tiles + 8, LANES), F32),
+            pltpu.VMEM((rows * alignment, C * pairs), BF16),
+            pltpu.VMEM((C * C, pairs), BF16),
+            pltpu.VMEM((pieces, pairs), F32),
+        ),
+        scratch_shapes=[
+            pltpu.VMEM((width, LANES), F32),
+            pltpu.VMEM((pieces * C, LANES), BF16),
+            pltpu.VMEM((pieces * pairs, channels), BF16),
+            pltpu.VMEM((pieces, pairs), F32),
+            pltpu.VMEM((C * C, pieces * pairs), BF16),
+        ],
+        compiler_params=pltpu.CompilerParams(vmem_limit_bytes=LARGE),
+    )(*arrived, mine, theirs, right_partial)
+    other = swap(partial, (1, 1), size)
     update, grad_left = pl.pallas_call(
         functools.partial(own_kernel, rows),
-        out_shape=(
-            jax.ShapeDtypeStruct((pairs, channels), BF16),
-            jax.ShapeDtypeStruct((rows, width), F32),
-        ),
+        out_shape=(pltpu.VMEM((pairs, channels), BF16), pltpu.VMEM((rows, width), F32)),
         scratch_shapes=[
             pltpu.VMEM((C, C * pairs), BF16),
             pltpu.VMEM((LANES, LANES), F32),
@@ -397,16 +457,25 @@
         cost_estimate=pl.CostEstimate(
             flops=8 * pairs * C * C * channels, bytes_accessed=4 * 2**20, transcendentals=0
         ),
-    )(spread, outer_own, inverse_own, depth_own, payload, w_swap, bias_row)
-    grad_w, grad_right, grad_bias = pl.pallas_call(
+    )(spread, outer_own, inverse_own, payload, w_swap, bias_row)
+    update, grad_left, grad_w, grad_right, grad_bias = pl.pallas_call(
         functools.partial(sum_kernel, rows),
         out_shape=(
+            jax.ShapeDtypeStruct((pairs, channels), BF16),
+            jax.ShapeDtypeStruct((rows, width), F32),
             jax.ShapeDtypeStruct((C * C, channels), F32),
             jax.ShapeDtypeStruct((rows, width), F32),
             jax.ShapeDtypeStruct((1, channels), F32),
         ),
+        out_specs=(hbm,) * 5,
+        scratch_shapes=[
+            pltpu.VMEM((C * C, channels), F32),
+            pltpu.VMEM((rows, width), F32),
+            pltpu.VMEM((1, channels), F32),
+            pltpu.SemaphoreType.DMA((8,)),
+        ],
         compiler_params=pltpu.CompilerParams(vmem_limit_bytes=SMALL),
-    )(partial, other)
+    )(partial, other, update, grad_left)
     return (
         update.reshape(rows, total, channels),
         grad_left,

time: 30.8 us -> 26.6 us (0.86)
  waiting for transfers between devices: 9.85 us -> 4.48 us
  starting transfers between devices: 10.3 us -> 13.1 us
  Pallas kernels: 9.62 us -> 8.11 us
    ppermute x10, waiting for transfers between devices: 9.85 us -> 4.48 us  [swap(): lax.ppermute(x, 'pi', [(i, i ^ masks[i % CORES]) for i in range(size)])]
    ppermute x10, starting transfers between devices: 10.3 us -> 13.1 us  [swap(): lax.ppermute(x, 'pi', [(i, i ^ masks[i % CORES]) for i in range(size)])]
    pallas_call x3 -> x4, Pallas kernels: 7.67 us -> 6.11 us  [the longest x1 3.36 us: gathered(): pl.pallas_call(functools.partial(main_kernel, (rows, total, pieces, used,...]
  transfers between devices with their start and end apart: 10 -> 10, of which waited for: 4 -> 5; matrix products, arithmetic and copies ran while one was open for 0% -> 0% of each run, Pallas kernels for 11% -> 10%
where the time goes in v3:
time: 26.6 us; the launch traced here: 26.4 us
  starting transfers between devices  13.1 us (49%)
  Pallas kernels  8.11 us (30%)
  waiting for transfers between devices  4.48 us (17%)
  between operations  0.71 us (3%)
    ppermute x10, starting transfers between devices, swap(): lax.ppermute(x, 'pi', [(i, i ^ masks[i % CORES]) for i in range(size)])  13.1 us
    ppermute x10, waiting for transfers between devices, swap(): lax.ppermute(x, 'pi', [(i, i ^ masks[i % CORES]) for i in range(size)])  4.48 us
    pallas_call x1, Pallas kernels, gathered(): pl.pallas_call(functools.partial(main_kernel, (rows, total, pieces, used,...  3.36 us
    pallas_call x1, Pallas kernels, gathered(): pl.pallas_call(functools.partial(own_kernel, rows), out_shape=(pltpu.VMEM...  1.55 us
    pallas_call x1, Pallas kernels, gathered(): pl.pallas_call(functools.partial(right_kernel, (rows, total, pieces, alig...  1.19 us
    pallas_call x1, Pallas kernels, gathered(): pl.pallas_call(pack_kernel, out_shape=(pltpu.VMEM((used, LANES), BF16), p...  1.1 us
    pallas_call x1, Pallas kernels, gathered(): pl.pallas_call(functools.partial(sum_kernel, rows), out_shape=(jax.ShapeD...  0.9 us
  transfers between devices with their start and end apart: 10, of which 5 were waited for; matrix products, arithmetic and copies ran while one was open for 0% of the time, Pallas kernels for 10%

profile of v3, /device:TPU:0, one launch (start us, length us, event | category | flops | bytes accessed | tf_op | source)
XLA Modules:
  0.0 26.4 jit_solution(5990002847334353265)
XLA Ops:
  0.6 1.1 %shard_map.101 = (bf16[336,128]{1,0:T(8,128)(2,1)S(1)}, f32[1,128]{1,0:T(1,128)S(1)}, bf16[1024,128]{1,0:T(8,128)(2,1)S(1)}) custom-call(bf16[4,1024]{1,0:T(4,128)(2,1)} %left_ref.1, bf16[4,1024]{1,0:T(4,128)(2,1)} %right_ref.1, bf16[256,128]{1,0:T(8,128)(2,1)} %bitcast.6, s32[4]{0:T(128)} %depth_ref.1, f32[1,128]{1,0:T(1,128)} %bitcast.8, ...), custom_call_target="tpu_custom_call" | custom-call | flops 1000000000 | bytes 1048576 | tf_op jit(solution)/shard_map/pallas_call | solution.py:381
  1.7 4.1 %collective-permute-start.5 = (bf16[336,128]{1,0:T(8,128)(2,1)S(1)}, bf16[336,128]{1,0:T(8,128)(2,1)S(1)}, u32[]{:S(2)}, u32[]{:S(2)}) collective-permute-start(bf16[336,128]{1,0:T(8,128)(2,1)S(1)} %get-tuple-element.21.refs_0_.payload_ref), channel_id=1, source_target_pairs={{0,8},{1,9},{2,10},{3,11},{4,12},{5,13},{6,14},{7,15},{8,0},{9,1},... | collective-permute-start | bytes 258056 | tf_op jit(solution)/shard_map/ppermute | solution.py:340
  5.8 1.5 %collective-permute-start.2 = (bf16[336,128]{1,0:T(8,128)(2,1)S(1)}, bf16[336,128]{1,0:T(8,128)(2,1)S(1)}, u32[]{:S(2)}, u32[]{:S(2)}) collective-permute-start(bf16[336,128]{1,0:T(8,128)(2,1)S(1)} %get-tuple-element.21.refs_0_.payload_ref), channel_id=1, source_target_pairs={{0,2},{1,3},{2,0},{3,1},{4,6},{5,7},{6,4},{7,5},{8,10},{9,11},{10,... | collective-permute-start | bytes 258056 | tf_op jit(solution)/shard_map/ppermute | solution.py:340
  7.4 1.6 %collective-permute-start.4 = (bf16[336,128]{1,0:T(8,128)(2,1)S(1)}, bf16[336,128]{1,0:T(8,128)(2,1)S(1)}, u32[]{:S(2)}, u32[]{:S(2)}) collective-permute-start(bf16[336,128]{1,0:T(8,128)(2,1)S(1)} %get-tuple-element.21.refs_0_.payload_ref), channel_id=1, source_target_pairs={{0,4},{1,5},{2,6},{3,7},{4,0},{5,1},{6,2},{7,3},{8,12},{9,13},{10,... | collective-permute-start | bytes 258056 | tf_op jit(solution)/shard_map/ppermute | solution.py:340
  8.9 0.2 collective-permute-start.1
  9.2 3.5 %collective-permute-start = (bf16[336,128]{1,0:T(8,128)(2,1)S(1)}, bf16[336,128]{1,0:T(8,128)(2,1)S(1)}, u32[]{:S(2)}, u32[]{:S(2)}) collective-permute-start(bf16[336,128]{1,0:T(8,128)(2,1)S(1)} %get-tuple-element.21.refs_0_.payload_ref), channel_id=1, source_target_pairs={{0,14},{1,15},{2,12},{3,13},{4,10},{5,11},{6,8},{7,9},{8,6},{9,7},... | collective-permute-start | bytes 258056 | tf_op jit(solution)/shard_map/ppermute | solution.py:340
  12.7 0.0 collective-permute-done.5.refs_6_
  12.7 1.5 %collective-permute-start.6 = (bf16[336,128]{1,0:T(8,128)(2,1)S(1)}, bf16[336,128]{1,0:T(8,128)(2,1)S(1)}, u32[]{:S(2)}, u32[]{:S(2)}) collective-permute-start(bf16[336,128]{1,0:T(8,128)(2,1)S(1)} %collective-permute-done.5.refs_6_), channel_id=1, source_target_pairs={{0,2},{1,3},{2,0},{3,1},{4,6},{5,7},{6,4},{7,5},{8,10},{9,11},{10,... | collective-permute-start | bytes 258056 | tf_op jit(solution)/shard_map/ppermute | solution.py:340
  14.2 0.0 collective-permute-done.2.refs_3_
  14.2 0.0 collective-permute-start.3
  14.3 0.1 collective-permute-start.8
  14.3 1.0 %collective-permute-done.1.refs_2_ = bf16[336,128]{1,0:T(8,128)(2,1)S(1)} collective-permute-done((bf16[336,128]{1,0:T(8,128)(2,1)S(1)}, bf16[336,128]{1,0:T(8,128)(2,1)S(1)}, u32[]{:S(2)}, u32[]{:S(2)}) %collective-permute-start.1) | collective-permute-done | bytes 86048 | tf_op jit(solution)/shard_map/ppermute | solution.py:340
  15.3 1.1 %collective-permute-done.refs_1_ = bf16[336,128]{1,0:T(8,128)(2,1)S(1)} collective-permute-done((bf16[336,128]{1,0:T(8,128)(2,1)S(1)}, bf16[336,128]{1,0:T(8,128)(2,1)S(1)}, u32[]{:S(2)}, u32[]{:S(2)}) %collective-permute-start) | collective-permute-done | bytes 86048 | tf_op jit(solution)/shard_map/ppermute | solution.py:340
  16.4 0.9 %collective-permute-done.6.refs_7_ = bf16[336,128]{1,0:T(8,128)(2,1)S(1)} collective-permute-done((bf16[336,128]{1,0:T(8,128)(2,1)S(1)}, bf16[336,128]{1,0:T(8,128)(2,1)S(1)}, u32[]{:S(2)}, u32[]{:S(2)}) %collective-permute-start.6) | collective-permute-done | bytes 86048 | tf_op jit(solution)/shard_map/ppermute | solution.py:340
  17.3 1.4 %collective-permute-done.3.refs_4_ = bf16[336,128]{1,0:T(8,128)(2,1)S(1)} collective-permute-done((bf16[336,128]{1,0:T(8,128)(2,1)S(1)}, bf16[336,128]{1,0:T(8,128)(2,1)S(1)}, u32[]{:S(2)}, u32[]{:S(2)}) %collective-permute-start.3) | collective-permute-done | bytes 86048 | tf_op jit(solution)/shard_map/ppermute | solution.py:340
  18.8 0.1 collective-permute-start.7
  18.8 0.0 collective-permute-done.8
  18.8 1.2 %shard_map.103 = (f32[64,128]{1,0:T(8,128)S(1)}, bf16[1024,128]{1,0:T(8,128)(2,1)S(1)}) custom-call(bf16[336,128]{1,0:T(8,128)(2,1)S(1)} %get-tuple-element.21.refs_0_.payload_ref, bf16[336,128]{1,0:T(8,128)(2,1)S(1)} %collective-permute-done.refs_1_, bf16[336,128]{1,0:T(8,128)(2,1)S(1)} %collective-permute-done.1.refs_2_, ...), custom_call_target="tpu_custom_call" | custom-call | flops 1000000000 | bytes 1048576 | tf_op jit(solution)/shard_map/pallas_call | solution.py:415
  20.0 0.1 collective-permute-done.7.refs_9_
  20.1 3.4 %shard_map.104 = (f32[1096,128]{1,0:T(8,128)S(1)}, bf16[128,8192]{1,0:T(8,128)(2,1)S(1)}, bf16[1024,256]{1,0:T(8,128)(2,1)S(1)}, f32[8,256]{1,0:T(8,128)S(1)}) custom-call(bf16[336,128]{1,0:T(8,128)(2,1)S(1)} %get-tuple-element.21.refs_0_.payload_ref, bf16[336,128]{1,0:T(8,128)(2,1)S(1)} %collective-permute-done.refs_1_, ...), custom_call_target="tpu_custom_call" | custom-call | tf_op jit(solution)/shard_map/pallas_call | solution.py:431
  23.4 0.5 %collective-permute-start.9 = (f32[1096,128]{1,0:T(8,128)S(1)}, f32[1096,128]{1,0:T(8,128)S(1)}, u32[]{:S(2)}, u32[]{:S(2)}) collective-permute-start(f32[1096,128]{1,0:T(8,128)S(1)} %get-tuple-element.24.own_ref), channel_id=1, source_target_pairs={{0,1},{1,0},{2,3},{3,2},{4,5},{5,4},{6,7},{7,6},{8,9},{9,8},{10,11... | collective-permute-start | bytes 1683464 | tf_op jit(solution)/shard_map/ppermute | solution.py:340
  24.0 1.6 %shard_map.105 = (bf16[256,128]{1,0:T(8,128)(2,1)S(1)}, f32[4,1024]{1,0:T(4,128)S(1)}) custom-call(bf16[128,8192]{1,0:T(8,128)(2,1)S(1)} %get-tuple-element.25.spread, bf16[1024,256]{1,0:T(8,128)(2,1)S(1)} %get-tuple-element.26.outer_own, f32[8,256]{1,0:T(8,128)S(1)} %get-tuple-element.27.inverse_own, ...), custom_call_target="tpu_custom_call" | custom-call | flops 268435456 | bytes 4194304 | tf_op jit(solution)/shard_map/pallas_call | solution.py:449
  25.5 0.0 collective-permute-done.9.other_ref
  25.5 0.9 %shard_map.106 = (bf16[256,128]{1,0:T(8,128)(2,1)}, f32[4,1024]{1,0:T(4,128)}, f32[1024,128]{1,0:T(8,128)}, f32[4,1024]{1,0:T(4,128)}, f32[1,128]{1,0:T(1,128)}) custom-call(f32[1096,128]{1,0:T(8,128)S(1)} %get-tuple-element.24.own_ref, f32[1096,128]{1,0:T(8,128)S(1)} %collective-permute-done.9.other_ref, ...), custom_call_target="tpu_custom_call" | custom-call | tf_op jit(solution)/shard_map/pallas_call | solution.py:461
  (4 shorter events, 0.0 us)
Async XLA Ops:
  0.6 13.6 %copy-start = (s32[4]{0:T(128)S(1)}, s32[4]{0:T(128)}, u32[]{:S(2)}) copy-start(s32[4]{0:T(128)} %depth_ref.1) | copy-start | bytes 52
  1.7 11.0 %collective-permute-start.5 = (bf16[336,128]{1,0:T(8,128)(2,1)S(1)}, bf16[336,128]{1,0:T(8,128)(2,1)S(1)}, u32[]{:S(2)}, u32[]{:S(2)}) collective-permute-start(bf16[336,128]{1,0:T(8,128)(2,1)S(1)} %get-tuple-element.21.refs_0_.payload_ref), channel_id=1, source_target_pairs={{0,8},{1,9},{2,10},{3,11},{4,12},{5,13},{6,14},{7,15},{8,0},{9,1},... | collective-permute-start | bytes 258056 | tf_op jit(solution)/shard_map/ppermute | solution.py:340
  5.8 8.4 %collective-permute-start.2 = (bf16[336,128]{1,0:T(8,128)(2,1)S(1)}, bf16[336,128]{1,0:T(8,128)(2,1)S(1)}, u32[]{:S(2)}, u32[]{:S(2)}) collective-permute-start(bf16[336,128]{1,0:T(8,128)(2,1)S(1)} %get-tuple-element.21.refs_0_.payload_ref), channel_id=1, source_target_pairs={{0,2},{1,3},{2,0},{3,1},{4,6},{5,7},{6,4},{7,5},{8,10},{9,11},{10,... | collective-permute-start | bytes 258056 | tf_op jit(solution)/shard_map/ppermute | solution.py:340
  7.4 6.9 %collective-permute-start.4 = (bf16[336,128]{1,0:T(8,128)(2,1)S(1)}, bf16[336,128]{1,0:T(8,128)(2,1)S(1)}, u32[]{:S(2)}, u32[]{:S(2)}) collective-permute-start(bf16[336,128]{1,0:T(8,128)(2,1)S(1)} %get-tuple-element.21.refs_0_.payload_ref), channel_id=1, source_target_pairs={{0,4},{1,5},{2,6},{3,7},{4,0},{5,1},{6,2},{7,3},{8,12},{9,13},{10,... | collective-permute-start | bytes 258056 | tf_op jit(solution)/shard_map/ppermute | solution.py:340
  8.9 6.4 %collective-permute-start.1 = (bf16[336,128]{1,0:T(8,128)(2,1)S(1)}, bf16[336,128]{1,0:T(8,128)(2,1)S(1)}, u32[]{:S(2)}, u32[]{:S(2)}) collective-permute-start(bf16[336,128]{1,0:T(8,128)(2,1)S(1)} %get-tuple-element.21.refs_0_.payload_ref), channel_id=1, source_target_pairs={{0,12},{1,13},{2,14},{3,15},{4,8},{5,9},{6,10},{7,11},{8,4},{9,5},... | collective-permute-start | bytes 258056 | tf_op jit(solution)/shard_map/ppermute | solution.py:340
  9.2 7.3 %collective-permute-start = (bf16[336,128]{1,0:T(8,128)(2,1)S(1)}, bf16[336,128]{1,0:T(8,128)(2,1)S(1)}, u32[]{:S(2)}, u32[]{:S(2)}) collective-permute-start(bf16[336,128]{1,0:T(8,128)(2,1)S(1)} %get-tuple-element.21.refs_0_.payload_ref), channel_id=1, source_target_pairs={{0,14},{1,15},{2,12},{3,13},{4,10},{5,11},{6,8},{7,9},{8,6},{9,7},... | collective-permute-start | bytes 258056 | tf_op jit(solution)/shard_map/ppermute | solution.py:340
  12.7 4.6 %collective-permute-start.6 = (bf16[336,128]{1,0:T(8,128)(2,1)S(1)}, bf16[336,128]{1,0:T(8,128)(2,1)S(1)}, u32[]{:S(2)}, u32[]{:S(2)}) collective-permute-start(bf16[336,128]{1,0:T(8,128)(2,1)S(1)} %collective-permute-done.5.refs_6_), channel_id=1, source_target_pairs={{0,2},{1,3},{2,0},{3,1},{4,6},{5,7},{6,4},{7,5},{8,10},{9,11},{10,... | collective-permute-start | bytes 258056 | tf_op jit(solution)/shard_map/ppermute | solution.py:340
  14.2 4.5 %collective-permute-start.3 = (bf16[336,128]{1,0:T(8,128)(2,1)S(1)}, bf16[336,128]{1,0:T(8,128)(2,1)S(1)}, u32[]{:S(2)}, u32[]{:S(2)}) collective-permute-start(bf16[336,128]{1,0:T(8,128)(2,1)S(1)} %collective-permute-done.2.refs_3_), channel_id=1, source_target_pairs={{0,4},{1,5},{2,6},{3,7},{4,0},{5,1},{6,2},{7,3},{8,12},{9,13},{10,... | collective-permute-start | bytes 258056 | tf_op jit(solution)/shard_map/ppermute | solution.py:340
  14.3 4.6 %collective-permute-start.8 = (s32[4]{0:T(128)S(1)}, s32[4]{0:T(128)S(1)}, u32[]{:S(2)}, u32[]{:S(2)}) collective-permute-start(s32[4]{0:T(128)S(1)} %copy-done), channel_id=1, source_target_pairs={{0,1},{1,0},{2,3},{3,2},{4,5},{5,4},{6,7},{7,6},{8,9},{9,8},{10,11... | collective-permute-start | bytes 56 | tf_op jit(solution)/shard_map/ppermute | solution.py:340
  18.8 1.3 %collective-permute-start.7 = (bf16[288,128]{1,0:T(8,128)(2,1)S(1)}, bf16[288,128]{1,0:T(8,128)(2,1)S(1)}, u32[]{:S(2)}, u32[]{:S(2)}) collective-permute-start(bf16[288,128]{1,0:T(8,128)(2,1)S(1)} %shard_map.102.refs_8_), channel_id=1, source_target_pairs={{0,1},{1,0},{2,3},{3,2},{4,5},{5,4},{6,7},{7,6},{8,9},{9,8},{10,11... | collective-permute-start | bytes 221192 | tf_op jit(solution)/shard_map/ppermute | solution.py:340
  23.4 2.1 %collective-permute-start.9 = (f32[1096,128]{1,0:T(8,128)S(1)}, f32[1096,128]{1,0:T(8,128)S(1)}, u32[]{:S(2)}, u32[]{:S(2)}) collective-permute-start(f32[1096,128]{1,0:T(8,128)S(1)} %get-tuple-element.24.own_ref), channel_id=1, source_target_pairs={{0,1},{1,0},{2,3},{3,2},{4,5},{5,4},{6,7},{7,6},{8,9},{9,8},{10,11... | collective-permute-start | bytes 1683464 | tf_op jit(solution)/shard_map/ppermute | solution.py:340

commit v4 on v3

--- a/solution.py
+++ b/solution.py
@@ -62,18 +62,19 @@
     copies = [pltpu.make_async_copy(*pair, sems.at[k]) for k, pair in enumerate(ends)]
     for copy in copies:
         copy.start()
+    row = iota((tiles * rows, group * LANES), 0)
+    lane = iota((tiles * rows, group * LANES), 1)
+    target = lax.rem(row, rows) * alignment + row // rows * group + lane // LANES
+    place = (lax.rem(lane, LANES) == target).astype(F32).astype(BF16)
     for copy in copies[:3]:
         copy.wait()
     left = left_here[...].astype(F32)
     flat = jnp.concatenate([left[:, t * LANES : (t + 1) * LANES] for t in range(tiles)], 0)
     flat = flat.astype(BF16)
-    row = iota((tiles * rows, LANES), 0)
-    lane = iota((tiles * rows, LANES), 1)
-    target = lax.rem(row, rows) * alignment + row // rows * group
+    spots = dot(flat, place, 0, 0)
     turned = jnp.zeros((C, LANES), F32)
     for q in range(group):
-        place = (lane == target + q).astype(F32).astype(BF16)
-        turned = turned + dot(flat, place, 0, 0)[q * C : (q + 1) * C, :]
+        turned = turned + spots[q * C : (q + 1) * C, q * LANES : (q + 1) * LANES]
     lane = iota((C, LANES), 1)
     depth = jnp.zeros((C, LANES), jnp.int32)
     for i in range(rows):
@@ -121,6 +122,12 @@
     copies[0].start()
     copies[1].start()
     wide = w_ref.shape[0]
+    count = sems.shape[0] - 4
+    for k in range(count):
+        some = slice(k * wide // count, (k + 1) * wide // count)
+        w_here[some, :] = own_ref[some, :] + other_ref[some, :]
+        copies.append(pltpu.make_async_copy(w_here.at[some], w_ref.at[some], sems.at[4 + k]))
+        copies[-1].start()
     core = lax.rem(lax.axis_index("pi"), CORES)
     tiles = right_ref.shape[1] // LANES
     begin = pl.multiple_of(wide + core * rows * tiles, 8)
@@ -133,22 +140,23 @@
     bias_here[...] = own_ref[last : last + 1, :] + other_ref[last : last + 1, :]
     copies[2].start()
     copies[3].start()
-    count = sems.shape[0] - 4
-    for k in range(count):
-        some = slice(k * wide // count, (k + 1) * wide // count)
-        w_here[some, :] = own_ref[some, :] + other_ref[some, :]
-        copies.append(pltpu.make_async_copy(w_here.at[some], w_ref.at[some], sems.at[4 + k]))
-        copies[-1].start()
     for copy in copies:
         copy.wait()
+
+
+def prepare_kernel(w_ref, early_ref, w_swap_ref, spread_ref, w_wide):
+    w_wide[...] = w_ref[...].astype(F32)
+    for d in range(C):
+        w_swap_ref[d * C : (d + 1) * C, :] = w_wide[pl.ds(d, C, stride=C), :].astype(BF16)
+    spread_ref[...] = jnp.zeros(spread_ref.shape, BF16)
 
 
 def right_kernel(sizes, *refs):
     rows, total, pieces, alignment, used, arrays = sizes
     some = 8
     piece = views(refs[:arrays], used)
-    w_ref, depth_ref, out_ref, w_swap_ref = refs[arrays : arrays + 4]
-    left_wide, window, picked, weights, g_right, stage, depths, w_wide = refs[arrays + 4 :]
+    w_ref, depth_ref, out_ref, cots, left_all = refs[arrays : arrays + 5]
+    left_wide, window, picked, weights, g_right, stage, depths = refs[arrays + 5 :]
     chip_rows = CORES * rows
     pairs = rows * total
     tiles = C * C // LANES
@@ -157,10 +165,9 @@
     chip = me // CORES
     at_depth = pairs + C + tiles * rows
 
-    w_wide[...] = w_ref[...].astype(F32)
-    for d in range(C):
-        w_swap_ref[d * C : (d + 1) * C, :] = w_wide[pl.ds(d, C, stride=C), :].astype(BF16)
     for m in range(pieces):
+        left_all[m * C : (m + 1) * C, :] = piece[m][pairs : pairs + C, :]
+        cots[m * pairs : (m + 1) * pairs, :] = piece[m][:pairs, :]
         left_wide[m * C : (m + 1) * C, :] = piece[m][pairs : pairs + C, :].astype(F32)
     tail = [ref[at_depth : at_depth + 16, :].astype(F32)[:rows] for ref in piece]
     other = jnp.broadcast_to(depth_ref[...].astype(F32), (rows, rows))
@@ -229,18 +236,15 @@
 def main_kernel(sizes, *refs):
     rows, total, pieces, used, arrays, route = sizes
     piece = views(refs[:arrays], used)
-    own_ref, other_ref, right_ref = refs[arrays : arrays + 3]
-    partial_ref, spread, outer_own, inverse_own = refs[arrays + 3 : arrays + 7]
-    turned, left_all, cots, inverse, outer = refs[arrays + 7 :]
+    own_ref, other_ref, right_ref, cots, left_all, _ = refs[arrays : arrays + 6]
+    partial_ref, spread, outer_own, inverse_own = refs[arrays + 6 : arrays + 10]
+    turned, inverse, outer = refs[arrays + 10 :]
     pairs = rows * total
     tiles = C * C // LANES
     per_tile = LANES // total
     me = lax.axis_index("pi")
     at_pairs = pairs + C + tiles * rows
 
-    for m in range(pieces):
-        left_all[m * C : (m + 1) * C, :] = piece[m][pairs : pairs + C, :]
-        cots[m * pairs : (m + 1) * pairs, :] = piece[m][:pairs, :]
     half = total // CORES
     row = iota((total, LANES), 0)
     core = lax.rem(me, CORES)
@@ -269,16 +273,12 @@
     alive = iota((alignment, LANES), 0).astype(F32) < depth_lane[:alignment, :]
     part_of = iota((alignment, LANES), 1) // total
     keep = [jnp.where(alive & (part_of == k), 1.0, 0.0).astype(F32) for k in range(per_tile)]
-    nothing = jnp.zeros((alignment, LANES), BF16)
     for d in range(C):
         block = turned[pl.ds(d, alignment, stride=C), :]
         kept = [(block * keep[k]).astype(BF16) for k in range(per_tile)]
         for i in range(rows):
-            for tile in range(pairs // LANES):
-                spread[
-                    i * alignment : (i + 1) * alignment,
-                    d * pairs + tile * LANES : d * pairs + (tile + 1) * LANES,
-                ] = kept[i % per_tile] if i // per_tile == tile else nothing
+            at = d * pairs + i // per_tile * LANES
+            spread[i * alignment : (i + 1) * alignment, at : at + LANES] = kept[i % per_tile]
 
     chunk = 8
     for d in range(C):
@@ -344,13 +344,13 @@
     near, middle, far = CORES, size // 4, size // 2
     if near * 2 == middle:
         return (
+            ((0,), (far,) * CORES),
             ((0,), (far + middle + near,) * CORES),
-            ((0,), (far + middle,) * CORES),
+            ((1,), (middle,) * CORES),
             ((0,), (near,) * CORES),
-            ((3,), (middle,) * CORES),
+            ((4,), (middle,) * CORES),
             ((0,), (middle,) * CORES),
-            ((0,), (far,) * CORES),
-            ((6,), (near,) * CORES),
+            ((1,), (near,) * CORES),
         )
     return tuple(((0,), (offset,) * CORES) for offset in range(CORES, size, CORES))
 
@@ -412,9 +412,22 @@
     )(*arrived)
     theirs = swap(mine, (1, 1), size)
     count_lanes = chip_rows * rows * pieces
-    right_partial, w_swap = pl.pallas_call(
+    w_swap, spread = pl.pallas_call(
+        prepare_kernel,
+        out_shape=(
+            pltpu.VMEM(w_out.shape, BF16),
+            pltpu.VMEM((rows * alignment, C * pairs), BF16),
+        ),
+        scratch_shapes=[pltpu.VMEM(w_out.shape, F32)],
+        compiler_params=pltpu.CompilerParams(vmem_limit_bytes=SMALL),
+    )(w_here, arrived[1])
+    right_partial, cots, left_all = pl.pallas_call(
         functools.partial(right_kernel, (rows, total, pieces, alignment, used, len(arrived))),
-        out_shape=(pltpu.VMEM((chip_rows * tiles, LANES), F32), pltpu.VMEM(w_out.shape, BF16)),
+        out_shape=(
+            pltpu.VMEM((chip_rows * tiles, LANES), F32),
+            pltpu.VMEM((pieces * pairs, channels), BF16),
+            pltpu.VMEM((pieces * C, LANES), BF16),
+        ),
         scratch_shapes=[
             pltpu.VMEM((pieces * C, LANES), F32),
             pltpu.VMEM((count_lanes, channels), F32),
@@ -423,7 +436,6 @@
             pltpu.VMEM((count_lanes // LANES * C, C * LANES), BF16),
             pltpu.VMEM((LANES, LANES), F32),
             pltpu.VMEM((16, LANES), F32),
-            pltpu.VMEM(w_out.shape, F32),
         ],
         compiler_params=pltpu.CompilerParams(vmem_limit_bytes=LARGE),
         cost_estimate=pl.CostEstimate(flops=10**9, bytes_accessed=2**20, transcendentals=0),
@@ -438,13 +450,12 @@
         ),
         scratch_shapes=[
             pltpu.VMEM((width, LANES), F32),
-            pltpu.VMEM((pieces * C, LANES), BF16),
-            pltpu.VMEM((pieces * pairs, channels), BF16),
             pltpu.VMEM((pieces, pairs), F32),
             pltpu.VMEM((C * C, pieces * pairs), BF16),
         ],
+        input_output_aliases={len(arrived) + 5: 1},
         compiler_params=pltpu.CompilerParams(vmem_limit_bytes=LARGE),
-    )(*arrived, mine, theirs, right_partial)
+    )(*arrived, mine, theirs, right_partial, cots, left_all, spread)
     other = swap(partial, (1, 1), size)
     update, grad_left = pl.pallas_call(
         functools.partial(own_kernel, rows),

time: 26.6 us -> 25.3 us (0.951)
  starting transfers between devices: 13.1 us -> 10.5 us
  waiting for transfers between devices: 4.48 us -> 5.74 us
    ppermute x10, starting transfers between devices: 13.1 us -> 10.5 us  [swap(): lax.ppermute(x, 'pi', [(i, i ^ masks[i % CORES]) for i in range(size)])]
    ppermute x10, waiting for transfers between devices: 4.48 us -> 5.74 us  [swap(): lax.ppermute(x, 'pi', [(i, i ^ masks[i % CORES]) for i in range(size)])]
    pallas_call x0 -> x1, Pallas kernels: none -> 0.45 us  [gathered(): pl.pallas_call(prepare_kernel, out_shape=(pltpu.VMEM(w_out.shape, BF16),...]
    pallas_call x1, Pallas kernels: 1.19 us -> 0.82 us  [gathered(): pl.pallas_call(functools.partial(right_kernel, (rows, total, pieces, alig...]
  transfers between devices with their start and end apart: 10 -> 10, of which waited for: 5 -> 7; matrix products, arithmetic and copies ran while one was open for 0% -> 0% of each run, Pallas kernels for 10% -> 11%
where the time goes in v4:
time: 25.3 us; the launch traced here: 25.2 us
  starting transfers between devices  10.5 us (42%)
  Pallas kernels  8.16 us (32%)
  waiting for transfers between devices  5.74 us (23%)
  between operations  0.72 us (3%)
    ppermute x10, starting transfers between devices, swap(): lax.ppermute(x, 'pi', [(i, i ^ masks[i % CORES]) for i in range(size)])  10.5 us
    ppermute x10, waiting for transfers between devices, swap(): lax.ppermute(x, 'pi', [(i, i ^ masks[i % CORES]) for i in range(size)])  5.74 us
    pallas_call x1, Pallas kernels, gathered(): pl.pallas_call(functools.partial(main_kernel, (rows, total, pieces, used,...  3.35 us
    pallas_call x1, Pallas kernels, gathered(): pl.pallas_call(functools.partial(own_kernel, rows), out_shape=(pltpu.VMEM...  1.55 us
    pallas_call x1, Pallas kernels, gathered(): pl.pallas_call(pack_kernel, out_shape=(pltpu.VMEM((used, LANES), BF16), p...  1.1 us
    pallas_call x1, Pallas kernels, gathered(): pl.pallas_call(functools.partial(sum_kernel, rows), out_shape=(jax.ShapeD...  0.88 us
    pallas_call x1, Pallas kernels, gathered(): pl.pallas_call(functools.partial(right_kernel, (rows, total, pieces, alig...  0.82 us
  transfers between devices with their start and end apart: 10, of which 7 were waited for; matrix products, arithmetic and copies ran while one was open for 0% of the time, Pallas kernels for 11%

profile of v4, /device:TPU:0, one launch (start us, length us, event | category | flops | bytes accessed | tf_op | source)
XLA Modules:
  0.0 25.2 jit_solution(12104117364534588522)
XLA Ops:
  0.6 1.1 %shard_map.101 = (bf16[336,128]{1,0:T(8,128)(2,1)S(1)}, f32[1,128]{1,0:T(1,128)S(1)}, bf16[1024,128]{1,0:T(8,128)(2,1)S(1)}) custom-call(bf16[4,1024]{1,0:T(4,128)(2,1)} %left_ref.1, bf16[4,1024]{1,0:T(4,128)(2,1)} %right_ref.1, bf16[256,128]{1,0:T(8,128)(2,1)} %bitcast.6, s32[4]{0:T(128)} %depth_ref.1, f32[1,128]{1,0:T(1,128)} %bitcast.8, ...), custom_call_target="tpu_custom_call" | custom-call | flops 1000000000 | bytes 1048576 | tf_op jit(solution)/shard_map/pallas_call | solution.py:381
  1.7 3.0 %collective-permute-start.3 = (bf16[336,128]{1,0:T(8,128)(2,1)S(1)}, bf16[336,128]{1,0:T(8,128)(2,1)S(1)}, u32[]{:S(2)}, u32[]{:S(2)}) collective-permute-start(bf16[336,128]{1,0:T(8,128)(2,1)S(1)} %get-tuple-element.24.refs_0_.payload_ref), channel_id=1, source_target_pairs={{0,2},{1,3},{2,0},{3,1},{4,6},{5,7},{6,4},{7,5},{8,10},{9,11},{10,... | collective-permute-start | bytes 258056 | tf_op jit(solution)/shard_map/ppermute | solution.py:340
  4.8 2.6 %collective-permute-start = (bf16[336,128]{1,0:T(8,128)(2,1)S(1)}, bf16[336,128]{1,0:T(8,128)(2,1)S(1)}, u32[]{:S(2)}, u32[]{:S(2)}) collective-permute-start(bf16[336,128]{1,0:T(8,128)(2,1)S(1)} %get-tuple-element.24.refs_0_.payload_ref), channel_id=1, source_target_pairs={{0,8},{1,9},{2,10},{3,11},{4,12},{5,13},{6,14},{7,15},{8,0},{9,1},... | collective-permute-start | bytes 258056 | tf_op jit(solution)/shard_map/ppermute | solution.py:340
  7.4 1.6 %collective-permute-start.5 = (bf16[336,128]{1,0:T(8,128)(2,1)S(1)}, bf16[336,128]{1,0:T(8,128)(2,1)S(1)}, u32[]{:S(2)}, u32[]{:S(2)}) collective-permute-start(bf16[336,128]{1,0:T(8,128)(2,1)S(1)} %get-tuple-element.24.refs_0_.payload_ref), channel_id=1, source_target_pairs={{0,4},{1,5},{2,6},{3,7},{4,0},{5,1},{6,2},{7,3},{8,12},{9,13},{10,... | collective-permute-start | bytes 258056 | tf_op jit(solution)/shard_map/ppermute | solution.py:340
  8.9 0.0 collective-permute-done.3.refs_4_
  9.0 0.8 %collective-permute-start.4 = (bf16[336,128]{1,0:T(8,128)(2,1)S(1)}, bf16[336,128]{1,0:T(8,128)(2,1)S(1)}, u32[]{:S(2)}, u32[]{:S(2)}) collective-permute-start(bf16[336,128]{1,0:T(8,128)(2,1)S(1)} %collective-permute-done.3.refs_4_), channel_id=1, source_target_pairs={{0,4},{1,5},{2,6},{3,7},{4,0},{5,1},{6,2},{7,3},{8,12},{9,13},{10,... | collective-permute-start | bytes 258056 | tf_op jit(solution)/shard_map/ppermute | solution.py:340
  9.8 2.1 %collective-permute-done.refs_1_.early_ref = bf16[336,128]{1,0:T(8,128)(2,1)S(1)} collective-permute-done((bf16[336,128]{1,0:T(8,128)(2,1)S(1)}, bf16[336,128]{1,0:T(8,128)(2,1)S(1)}, u32[]{:S(2)}, u32[]{:S(2)}) %collective-permute-start) | collective-permute-done | bytes 86048 | tf_op jit(solution)/shard_map/ppermute | solution.py:340
  11.9 0.0 collective-permute-start.6
  11.9 2.1 %collective-permute-start.2 = (bf16[336,128]{1,0:T(8,128)(2,1)S(1)}, bf16[336,128]{1,0:T(8,128)(2,1)S(1)}, u32[]{:S(2)}, u32[]{:S(2)}) collective-permute-start(bf16[336,128]{1,0:T(8,128)(2,1)S(1)} %collective-permute-done.refs_1_.early_ref), channel_id=1, source_target_pairs={{0,4},{1,5},{2,6},{3,7},{4,0},{5,1},{6,2},{7,3},{8,12},{9,13},{10,... | collective-permute-start | bytes 258056 | tf_op jit(solution)/shard_map/ppermute | solution.py:340
  14.1 0.5 %shard_map.104 = (bf16[1024,128]{1,0:T(8,128)(2,1)S(1)}, bf16[128,8192]{1,0:T(8,128)(2,1)S(1)}) custom-call(bf16[1024,128]{1,0:T(8,128)(2,1)S(1)} %get-tuple-element.25.refs_8_.w_ref, bf16[336,128]{1,0:T(8,128)(2,1)S(1)} %collective-permute-done.refs_1_.early_ref), custom_call_target="tpu_custom_call" | custom-call | tf_op jit(solution)/shard_map/pallas_call | solution.py:415
  14.5 0.0 collective-permute-done.5.refs_6_
  14.5 0.1 collective-permute-start.8
  14.6 1.7 %collective-permute-done.1.refs_2_ = bf16[336,128]{1,0:T(8,128)(2,1)S(1)} collective-permute-done((bf16[336,128]{1,0:T(8,128)(2,1)S(1)}, bf16[336,128]{1,0:T(8,128)(2,1)S(1)}, u32[]{:S(2)}, u32[]{:S(2)}) %collective-permute-start.1) | collective-permute-done | bytes 86048 | tf_op jit(solution)/shard_map/ppermute | solution.py:340
  16.3 0.3 %collective-permute-done.4.refs_5_ = bf16[336,128]{1,0:T(8,128)(2,1)S(1)} collective-permute-done((bf16[336,128]{1,0:T(8,128)(2,1)S(1)}, bf16[336,128]{1,0:T(8,128)(2,1)S(1)}, u32[]{:S(2)}, u32[]{:S(2)}) %collective-permute-start.4) | collective-permute-done | bytes 86048 | tf_op jit(solution)/shard_map/ppermute | solution.py:340
  16.6 0.5 %collective-permute-done.6.refs_7_ = bf16[336,128]{1,0:T(8,128)(2,1)S(1)} collective-permute-done((bf16[336,128]{1,0:T(8,128)(2,1)S(1)}, bf16[336,128]{1,0:T(8,128)(2,1)S(1)}, u32[]{:S(2)}, u32[]{:S(2)}) %collective-permute-start.6) | collective-permute-done | bytes 86048 | tf_op jit(solution)/shard_map/ppermute | solution.py:340
  17.1 0.4 %collective-permute-done.2.refs_3_ = bf16[336,128]{1,0:T(8,128)(2,1)S(1)} collective-permute-done((bf16[336,128]{1,0:T(8,128)(2,1)S(1)}, bf16[336,128]{1,0:T(8,128)(2,1)S(1)}, u32[]{:S(2)}, u32[]{:S(2)}) %collective-permute-start.2) | collective-permute-done | bytes 86048 | tf_op jit(solution)/shard_map/ppermute | solution.py:340
  17.6 0.1 collective-permute-start.7
  17.6 0.8 %shard_map.103 = (f32[64,128]{1,0:T(8,128)S(1)}, bf16[2048,128]{1,0:T(8,128)(2,1)S(1)}, bf16[256,128]{1,0:T(8,128)(2,1)S(1)}) custom-call(bf16[336,128]{1,0:T(8,128)(2,1)S(1)} %get-tuple-element.24.refs_0_.payload_ref, bf16[336,128]{1,0:T(8,128)(2,1)S(1)} %collective-permute-done.refs_1_.early_ref, bf16[336,128]{1,0:T(8,128)(2,1)S(1)} %collective-permute-done.1.refs_2_, ...), custom_call_target="tpu_custom_call" | custom-call | flops 1000000000 | bytes 1048576 | tf_op jit(solution)/shard_map/pallas_call | solution.py:424
  18.5 0.4 %collective-permute-done.7.refs_9_ = bf16[288,128]{1,0:T(8,128)(2,1)S(1)} collective-permute-done((bf16[288,128]{1,0:T(8,128)(2,1)S(1)}, bf16[288,128]{1,0:T(8,128)(2,1)S(1)}, u32[]{:S(2)}, u32[]{:S(2)}) %collective-permute-start.7) | collective-permute-done | bytes 73760 | tf_op jit(solution)/shard_map/ppermute | solution.py:340
  18.9 3.3 %shard_map.105 = (f32[1096,128]{1,0:T(8,128)S(1)}, bf16[128,8192]{1,0:T(8,128)(2,1)S(1)}, bf16[1024,256]{1,0:T(8,128)(2,1)S(1)}, f32[8,256]{1,0:T(8,128)S(1)}) custom-call(bf16[336,128]{1,0:T(8,128)(2,1)S(1)} %get-tuple-element.24.refs_0_.payload_ref, bf16[336,128]{1,0:T(8,128)(2,1)S(1)} %collective-permute-done.refs_1_.early_ref, ...), custom_call_target="tpu_custom_call", output_to_operand_aliasing={{1}: (13, {})} | custom-call | tf_op jit(solution)/shard_map/pallas_call | solution.py:443
  22.2 0.2 collective-permute-start.9
  22.5 1.5 %shard_map.106 = (bf16[256,128]{1,0:T(8,128)(2,1)S(1)}, f32[4,1024]{1,0:T(4,128)S(1)}) custom-call(bf16[128,8192]{1,0:T(8,128)(2,1)S(1)} %get-tuple-element.31.spread, bf16[1024,256]{1,0:T(8,128)(2,1)S(1)} %get-tuple-element.32.outer_own, f32[8,256]{1,0:T(8,128)S(1)} %get-tuple-element.33.inverse_own, ...), custom_call_target="tpu_custom_call" | custom-call | flops 268435456 | bytes 4194304 | tf_op jit(solution)/shard_map/pallas_call | solution.py:460
  24.0 0.3 %collective-permute-done.9.other_ref = f32[1096,128]{1,0:T(8,128)S(1)} collective-permute-done((f32[1096,128]{1,0:T(8,128)S(1)}, f32[1096,128]{1,0:T(8,128)S(1)}, u32[]{:S(2)}, u32[]{:S(2)}) %collective-permute-start.9) | collective-permute-done | bytes 561184 | tf_op jit(solution)/shard_map/ppermute | solution.py:340
  24.3 0.9 %shard_map.107 = (bf16[256,128]{1,0:T(8,128)(2,1)}, f32[4,1024]{1,0:T(4,128)}, f32[1024,128]{1,0:T(8,128)}, f32[4,1024]{1,0:T(4,128)}, f32[1,128]{1,0:T(1,128)}) custom-call(f32[1096,128]{1,0:T(8,128)S(1)} %get-tuple-element.30.own_ref, f32[1096,128]{1,0:T(8,128)S(1)} %collective-permute-done.9.other_ref, ...), custom_call_target="tpu_custom_call" | custom-call | tf_op jit(solution)/shard_map/pallas_call | solution.py:472
  (5 shorter events, 0.0 us)
Async XLA Ops:
  0.6 13.9 %copy-start = (s32[4]{0:T(128)S(1)}, s32[4]{0:T(128)}, u32[]{:S(2)}) copy-start(s32[4]{0:T(128)} %depth_ref.1) | copy-start | bytes 52
  1.7 7.2 %collective-permute-start.3 = (bf16[336,128]{1,0:T(8,128)(2,1)S(1)}, bf16[336,128]{1,0:T(8,128)(2,1)S(1)}, u32[]{:S(2)}, u32[]{:S(2)}) collective-permute-start(bf16[336,128]{1,0:T(8,128)(2,1)S(1)} %get-tuple-element.24.refs_0_.payload_ref), channel_id=1, source_target_pairs={{0,2},{1,3},{2,0},{3,1},{4,6},{5,7},{6,4},{7,5},{8,10},{9,11},{10,... | collective-permute-start | bytes 258056 | tf_op jit(solution)/shard_map/ppermute | solution.py:340
  4.8 7.2 %collective-permute-start = (bf16[336,128]{1,0:T(8,128)(2,1)S(1)}, bf16[336,128]{1,0:T(8,128)(2,1)S(1)}, u32[]{:S(2)}, u32[]{:S(2)}) collective-permute-start(bf16[336,128]{1,0:T(8,128)(2,1)S(1)} %get-tuple-element.24.refs_0_.payload_ref), channel_id=1, source_target_pairs={{0,8},{1,9},{2,10},{3,11},{4,12},{5,13},{6,14},{7,15},{8,0},{9,1},... | collective-permute-start | bytes 258056 | tf_op jit(solution)/shard_map/ppermute | solution.py:340
  7.4 7.2 %collective-permute-start.5 = (bf16[336,128]{1,0:T(8,128)(2,1)S(1)}, bf16[336,128]{1,0:T(8,128)(2,1)S(1)}, u32[]{:S(2)}, u32[]{:S(2)}) collective-permute-start(bf16[336,128]{1,0:T(8,128)(2,1)S(1)} %get-tuple-element.24.refs_0_.payload_ref), channel_id=1, source_target_pairs={{0,4},{1,5},{2,6},{3,7},{4,0},{5,1},{6,2},{7,3},{8,12},{9,13},{10,... | collective-permute-start | bytes 258056 | tf_op jit(solution)/shard_map/ppermute | solution.py:340
  8.9 7.4 %collective-permute-start.1 = (bf16[336,128]{1,0:T(8,128)(2,1)S(1)}, bf16[336,128]{1,0:T(8,128)(2,1)S(1)}, u32[]{:S(2)}, u32[]{:S(2)}) collective-permute-start(bf16[336,128]{1,0:T(8,128)(2,1)S(1)} %get-tuple-element.24.refs_0_.payload_ref), channel_id=1, source_target_pairs={{0,14},{1,15},{2,12},{3,13},{4,10},{5,11},{6,8},{7,9},{8,6},{9,7},... | collective-permute-start | bytes 258056 | tf_op jit(solution)/shard_map/ppermute | solution.py:340
  9.0 7.7 %collective-permute-start.4 = (bf16[336,128]{1,0:T(8,128)(2,1)S(1)}, bf16[336,128]{1,0:T(8,128)(2,1)S(1)}, u32[]{:S(2)}, u32[]{:S(2)}) collective-permute-start(bf16[336,128]{1,0:T(8,128)(2,1)S(1)} %collective-permute-done.3.refs_4_), channel_id=1, source_target_pairs={{0,4},{1,5},{2,6},{3,7},{4,0},{5,1},{6,2},{7,3},{8,12},{9,13},{10,... | collective-permute-start | bytes 258056 | tf_op jit(solution)/shard_map/ppermute | solution.py:340
  11.9 5.2 %collective-permute-start.6 = (bf16[336,128]{1,0:T(8,128)(2,1)S(1)}, bf16[336,128]{1,0:T(8,128)(2,1)S(1)}, u32[]{:S(2)}, u32[]{:S(2)}) collective-permute-start(bf16[336,128]{1,0:T(8,128)(2,1)S(1)} %collective-permute-done.refs_1_.early_ref), channel_id=1, source_target_pairs={{0,2},{1,3},{2,0},{3,1},{4,6},{5,7},{6,4},{7,5},{8,10},{9,11},{10,... | collective-permute-start | bytes 258056 | tf_op jit(solution)/shard_map/ppermute | solution.py:340
  11.9 5.6 %collective-permute-start.2 = (bf16[336,128]{1,0:T(8,128)(2,1)S(1)}, bf16[336,128]{1,0:T(8,128)(2,1)S(1)}, u32[]{:S(2)}, u32[]{:S(2)}) collective-permute-start(bf16[336,128]{1,0:T(8,128)(2,1)S(1)} %collective-permute-done.refs_1_.early_ref), channel_id=1, source_target_pairs={{0,4},{1,5},{2,6},{3,7},{4,0},{5,1},{6,2},{7,3},{8,12},{9,13},{10,... | collective-permute-start | bytes 258056 | tf_op jit(solution)/shard_map/ppermute | solution.py:340
  14.5 3.1 %collective-permute-start.8 = (s32[4]{0:T(128)S(1)}, s32[4]{0:T(128)S(1)}, u32[]{:S(2)}, u32[]{:S(2)}) collective-permute-start(s32[4]{0:T(128)S(1)} %copy-done), channel_id=1, source_target_pairs={{0,1},{1,0},{2,3},{3,2},{4,5},{5,4},{6,7},{7,6},{8,9},{9,8},{10,11... | collective-permute-start | bytes 56 | tf_op jit(solution)/shard_map/ppermute | solution.py:340
  17.6 1.3 %collective-permute-start.7 = (bf16[288,128]{1,0:T(8,128)(2,1)S(1)}, bf16[288,128]{1,0:T(8,128)(2,1)S(1)}, u32[]{:S(2)}, u32[]{:S(2)}) collective-permute-start(bf16[288,128]{1,0:T(8,128)(2,1)S(1)} %shard_map.102.refs_8_), channel_id=1, source_target_pairs={{0,1},{1,0},{2,3},{3,2},{4,5},{5,4},{6,7},{7,6},{8,9},{9,8},{10,11... | collective-permute-start | bytes 221192 | tf_op jit(solution)/shard_map/ppermute | solution.py:340
  22.2 2.0 %collective-permute-start.9 = (f32[1096,128]{1,0:T(8,128)S(1)}, f32[1096,128]{1,0:T(8,128)S(1)}, u32[]{:S(2)}, u32[]{:S(2)}) collective-permute-start(f32[1096,128]{1,0:T(8,128)S(1)} %get-tuple-element.30.own_ref), channel_id=1, source_target_pairs={{0,1},{1,0},{2,3},{3,2},{4,5},{5,4},{6,7},{7,6},{8,9},{9,8},{10,11... | collective-permute-start | bytes 1683464 | tf_op jit(solution)/shard_map/ppermute | solution.py:340

commit v5 on v4

--- a/solution.py
+++ b/solution.py
@@ -144,19 +144,12 @@
         copy.wait()
 
 
-def prepare_kernel(w_ref, early_ref, w_swap_ref, spread_ref, w_wide):
-    w_wide[...] = w_ref[...].astype(F32)
-    for d in range(C):
-        w_swap_ref[d * C : (d + 1) * C, :] = w_wide[pl.ds(d, C, stride=C), :].astype(BF16)
-    spread_ref[...] = jnp.zeros(spread_ref.shape, BF16)
-
-
 def right_kernel(sizes, *refs):
     rows, total, pieces, alignment, used, arrays = sizes
     some = 8
     piece = views(refs[:arrays], used)
-    w_ref, depth_ref, out_ref, cots, left_all = refs[arrays : arrays + 5]
-    left_wide, window, picked, weights, g_right, stage, depths = refs[arrays + 5 :]
+    w_ref, depth_ref, out_ref, cots, left_halves, w_swap_ref = refs[arrays : arrays + 6]
+    left_wide, window, picked, weights, g_right, stage, depths, w_wide = refs[arrays + 6 :]
     chip_rows = CORES * rows
     pairs = rows * total
     tiles = C * C // LANES
@@ -166,9 +159,15 @@
     at_depth = pairs + C + tiles * rows
 
     for m in range(pieces):
-        left_all[m * C : (m + 1) * C, :] = piece[m][pairs : pairs + C, :]
         cots[m * pairs : (m + 1) * pairs, :] = piece[m][:pairs, :]
         left_wide[m * C : (m + 1) * C, :] = piece[m][pairs : pairs + C, :].astype(F32)
+    width = left_halves.shape[1]
+    for h in range(LANES // width):
+        part = left_wide[...] if h == 0 else pltpu.roll(left_wide[...], LANES - h * width, 1)
+        left_halves[h * pieces * C : (h + 1) * pieces * C, :] = part[:, :width].astype(BF16)
+    w_wide[...] = w_ref[...].astype(F32)
+    for d in range(C):
+        w_swap_ref[d * C : (d + 1) * C, :] = w_wide[pl.ds(d, C, stride=C), :].astype(BF16)
     tail = [ref[at_depth : at_depth + 16, :].astype(F32)[:rows] for ref in piece]
     other = jnp.broadcast_to(depth_ref[...].astype(F32), (rows, rows))
     other = jnp.where(iota((rows, rows), 0) == iota((rows, rows), 1), other, 0.0)
@@ -236,9 +235,9 @@
 def main_kernel(sizes, *refs):
     rows, total, pieces, used, arrays, route = sizes
     piece = views(refs[:arrays], used)
-    own_ref, other_ref, right_ref, cots, left_all, _ = refs[arrays : arrays + 6]
-    partial_ref, spread, outer_own, inverse_own = refs[arrays + 6 : arrays + 10]
-    turned, inverse, outer = refs[arrays + 10 :]
+    own_ref, other_ref, right_ref, cots, left_halves = refs[arrays : arrays + 5]
+    partial_ref, spread, outer_own, inverse_own = refs[arrays + 5 : arrays + 9]
+    turned, inverse, outer = refs[arrays + 9 :]
     pairs = rows * total
     tiles = C * C // LANES
     per_tile = LANES // total
@@ -269,24 +268,33 @@
             least = jnp.minimum(block[8 + tile : 9 + tile, :], depth_lane[:1, :])
             inverse[m : m + 1, tile * LANES : (tile + 1) * LANES] = 1.0 / (epsilon + least)
 
-    alignment = spread.shape[0] // rows
+    alignment = spread.shape[0] // per_tile
     alive = iota((alignment, LANES), 0).astype(F32) < depth_lane[:alignment, :]
     part_of = iota((alignment, LANES), 1) // total
     keep = [jnp.where(alive & (part_of == k), 1.0, 0.0).astype(F32) for k in range(per_tile)]
     for d in range(C):
         block = turned[pl.ds(d, alignment, stride=C), :]
-        kept = [(block * keep[k]).astype(BF16) for k in range(per_tile)]
-        for i in range(rows):
-            at = d * pairs + i // per_tile * LANES
-            spread[i * alignment : (i + 1) * alignment, at : at + LANES] = kept[i % per_tile]
+        for k in range(per_tile):
+            spread[k * alignment : (k + 1) * alignment, d * LANES : (d + 1) * LANES] = (
+                block * keep[k]
+            ).astype(BF16)
 
     chunk = 8
     for d in range(C):
-        o = dot(left_all[...], spread[:, d * pairs : (d + 1) * pairs], 1, 0)
-        for m in range(pieces):
-            outer[d * C : (d + 1) * C, m * pairs : (m + 1) * pairs] = (
-                o[m * C : (m + 1) * C, :] * inverse[m : m + 1, :]
-            ).astype(BF16)
+        if d % 2 == 0:
+            two = spread[:, d * LANES : (d + 2) * LANES]
+            parts = [
+                dot(left_halves[h * pieces * C : (h + 1) * pieces * C, :], two, 1, 0)
+                for h in range(pairs // LANES)
+            ]
+        for h in range(pairs // LANES):
+            o = parts[h][:, d % 2 * LANES : (d % 2 + 1) * LANES]
+            count = inverse[:, h * LANES : (h + 1) * LANES]
+            for m in range(pieces):
+                at = m * pairs + h * LANES
+                outer[d * C : (d + 1) * C, at : at + LANES] = (
+                    o[m * C : (m + 1) * C, :] * count[m : m + 1, :]
+                ).astype(BF16)
         if d % chunk == chunk - 1:
             first = d + 1 - chunk
             some = slice(first * C, (d + 1) * C)
@@ -309,8 +317,9 @@
 ):
     some = 8
     pairs = update_ref.shape[0]
-    alignment = spread.shape[0] // rows
     tiles = left_ref.shape[1] // LANES
+    alignment = tiles * (LANES // C)
+    halves = pairs // LANES
     group = LANES // C
     update = dot(outer_own[...], w_swap_ref[...], 0, 0)
     update_ref[...] = (update + bias_ref[...]).astype(BF16)
@@ -318,9 +327,16 @@
         if d % some == 0:
             g = dot(w_swap_ref[d * C : (d + some) * C, :], payload_ref[:pairs, :], 1, 1)
             g = (g * inverse_own[:1, :]).astype(BF16)
-        g_left[:, d * pairs : (d + 1) * pairs] = g[d % some * C : (d % some + 1) * C, :]
+        for h in range(halves):
+            g_left[h * C : (h + 1) * C, d * LANES : (d + 1) * LANES] = g[
+                d % some * C : (d % some + 1) * C, h * LANES : (h + 1) * LANES
+            ]
     left_grad = dot(spread[...], g_left[...], 1, 1)
-    stage[...] = jnp.concatenate([left_grad] * group, 1)
+    for h in range(halves):
+        part = left_grad[:, h * C : (h + 1) * C]
+        stage[h * spread.shape[0] : (h + 1) * spread.shape[0], :] = jnp.concatenate(
+            [part] * group, 1
+        )
     in_tile = iota((8, LANES), 1) // C
     row_of = (iota((8, LANES), 0) * group + in_tile).astype(F32)
     at_depth = pairs + C + tiles * rows
@@ -412,21 +428,14 @@
     )(*arrived)
     theirs = swap(mine, (1, 1), size)
     count_lanes = chip_rows * rows * pieces
-    w_swap, spread = pl.pallas_call(
-        prepare_kernel,
-        out_shape=(
-            pltpu.VMEM(w_out.shape, BF16),
-            pltpu.VMEM((rows * alignment, C * pairs), BF16),
-        ),
-        scratch_shapes=[pltpu.VMEM(w_out.shape, F32)],
-        compiler_params=pltpu.CompilerParams(vmem_limit_bytes=SMALL),
-    )(w_here, arrived[1])
-    right_partial, cots, left_all = pl.pallas_call(
+    per_tile = LANES // total
+    right_partial, cots, left_halves, w_swap = pl.pallas_call(
         functools.partial(right_kernel, (rows, total, pieces, alignment, used, len(arrived))),
         out_shape=(
             pltpu.VMEM((chip_rows * tiles, LANES), F32),
             pltpu.VMEM((pieces * pairs, channels), BF16),
-            pltpu.VMEM((pieces * C, LANES), BF16),
+            pltpu.VMEM((rows // per_tile * pieces * C, per_tile * alignment), BF16),
+            pltpu.VMEM(w_out.shape, BF16),
         ),
         scratch_shapes=[
             pltpu.VMEM((pieces * C, LANES), F32),
@@ -436,6 +445,7 @@
             pltpu.VMEM((count_lanes // LANES * C, C * LANES), BF16),
             pltpu.VMEM((LANES, LANES), F32),
             pltpu.VMEM((16, LANES), F32),
+            pltpu.VMEM(w_out.shape, F32),
         ],
         compiler_params=pltpu.CompilerParams(vmem_limit_bytes=LARGE),
         cost_estimate=pl.CostEstimate(flops=10**9, bytes_accessed=2**20, transcendentals=0),
@@ -444,7 +454,7 @@
         functools.partial(main_kernel, (rows, total, pieces, used, len(arrived), route)),
         out_shape=(
             pltpu.VMEM((C * C + chip_rows * tiles + 8, LANES), F32),
-            pltpu.VMEM((rows * alignment, C * pairs), BF16),
+            pltpu.VMEM((per_tile * alignment, C * LANES), BF16),
             pltpu.VMEM((C * C, pairs), BF16),
             pltpu.VMEM((pieces, pairs), F32),
         ),
@@ -453,15 +463,14 @@
             pltpu.VMEM((pieces, pairs), F32),
             pltpu.VMEM((C * C, pieces * pairs), BF16),
         ],
-        input_output_aliases={len(arrived) + 5: 1},
         compiler_params=pltpu.CompilerParams(vmem_limit_bytes=LARGE),
-    )(*arrived, mine, theirs, right_partial, cots, left_all, spread)
+    )(*arrived, mine, theirs, right_partial, cots, left_halves)
     other = swap(partial, (1, 1), size)
     update, grad_left = pl.pallas_call(
         functools.partial(own_kernel, rows),
         out_shape=(pltpu.VMEM((pairs, channels), BF16), pltpu.VMEM((rows, width), F32)),
         scratch_shapes=[
-            pltpu.VMEM((C, C * pairs), BF16),
+            pltpu.VMEM((pairs // LANES * C, C * LANES), BF16),
             pltpu.VMEM((LANES, LANES), F32),
         ],
         compiler_params=pltpu.CompilerParams(vmem_limit_bytes=LARGE),

time: 25.3 us -> 25.4 us (level)
  Pallas kernels: 8.16 us -> 7.53 us
  waiting for transfers between devices: 5.74 us -> 6.28 us
  starting transfers between devices: 10.5 us -> 10.8 us
    pallas_call x1, Pallas kernels: 1.55 us -> 0.93 us  [gathered(): pl.pallas_call(functools.partial(own_kernel, rows), out_shape=(pltpu.VMEM...]
    ppermute x10, waiting for transfers between devices: 5.74 us -> 6.28 us  [swap(): lax.ppermute(x, 'pi', [(i, i ^ masks[i % CORES]) for i in range(size)])]
    pallas_call x1 -> x0, Pallas kernels: 0.45 us -> none  [gathered(): pl.pallas_call(prepare_kernel, out_shape=(pltpu.VMEM(w_out.shape, BF16),...]
    pallas_call x1, Pallas kernels: 0.82 us -> 1.22 us  [gathered(): pl.pallas_call(functools.partial(right_kernel, (rows, total, pieces, alig...]
  transfers between devices with their start and end apart: 10 -> 10, of which waited for: 7 -> 6; matrix products, arithmetic and copies ran while one was open for 0% -> 0% of each run, Pallas kernels for 11% -> 9%
where the time goes in v5:
time: 25.4 us; the launch traced here: 25.3 us
  starting transfers between devices  10.8 us (43%)
  Pallas kernels  7.53 us (30%)
  waiting for transfers between devices  6.28 us (25%)
  between operations  0.69 us (3%)
    ppermute x10, starting transfers between devices, swap(): lax.ppermute(x, 'pi', [(i, i ^ masks[i % CORES]) for i in range(size)])  10.8 us
    ppermute x10, waiting for transfers between devices, swap(): lax.ppermute(x, 'pi', [(i, i ^ masks[i % CORES]) for i in range(size)])  6.28 us
    pallas_call x1, Pallas kernels, gathered(): pl.pallas_call(functools.partial(main_kernel, (rows, total, pieces, used,...  3.38 us
    pallas_call x1, Pallas kernels, gathered(): pl.pallas_call(functools.partial(right_kernel, (rows, total, pieces, alig...  1.22 us
    pallas_call x1, Pallas kernels, gathered(): pl.pallas_call(pack_kernel, out_shape=(pltpu.VMEM((used, LANES), BF16), p...  1.09 us
    pallas_call x1, Pallas kernels, gathered(): pl.pallas_call(functools.partial(own_kernel, rows), out_shape=(pltpu.VMEM...  0.93 us
    pallas_call x1, Pallas kernels, gathered(): pl.pallas_call(functools.partial(sum_kernel, rows), out_shape=(jax.ShapeD...  0.88 us
  transfers between devices with their start and end apart: 10, of which 6 were waited for; matrix products, arithmetic and copies ran while one was open for 0% of the time, Pallas kernels for 9%

profile of v5, /device:TPU:0, one launch (start us, length us, event | category | flops | bytes accessed | tf_op | source)
XLA Modules:
  0.0 25.3 jit_solution(8488416040915597360)
XLA Ops:
  0.6 1.1 %shard_map.101 = (bf16[336,128]{1,0:T(8,128)(2,1)S(1)}, f32[1,128]{1,0:T(1,128)S(1)}, bf16[1024,128]{1,0:T(8,128)(2,1)S(1)}) custom-call(bf16[4,1024]{1,0:T(4,128)(2,1)} %left_ref.1, bf16[4,1024]{1,0:T(4,128)(2,1)} %right_ref.1, bf16[256,128]{1,0:T(8,128)(2,1)} %bitcast.6, s32[4]{0:T(128)} %depth_ref.1, f32[1,128]{1,0:T(1,128)} %bitcast.8, ...), custom_call_target="tpu_custom_call" | custom-call | flops 1000000000 | bytes 1048576 | tf_op jit(solution)/shard_map/pallas_call | solution.py:397
  1.7 0.0 copy-start
  1.7 3.0 %collective-permute-start.3 = (bf16[336,128]{1,0:T(8,128)(2,1)S(1)}, bf16[336,128]{1,0:T(8,128)(2,1)S(1)}, u32[]{:S(2)}, u32[]{:S(2)}) collective-permute-start(bf16[336,128]{1,0:T(8,128)(2,1)S(1)} %get-tuple-element.23.refs_0_.payload_ref), channel_id=1, source_target_pairs={{0,2},{1,3},{2,0},{3,1},{4,6},{5,7},{6,4},{7,5},{8,10},{9,11},{10,... | collective-permute-start | bytes 258056 | tf_op jit(solution)/shard_map/ppermute | solution.py:356
  4.8 2.6 %collective-permute-start = (bf16[336,128]{1,0:T(8,128)(2,1)S(1)}, bf16[336,128]{1,0:T(8,128)(2,1)S(1)}, u32[]{:S(2)}, u32[]{:S(2)}) collective-permute-start(bf16[336,128]{1,0:T(8,128)(2,1)S(1)} %get-tuple-element.23.refs_0_.payload_ref), channel_id=1, source_target_pairs={{0,8},{1,9},{2,10},{3,11},{4,12},{5,13},{6,14},{7,15},{8,0},{9,1},... | collective-permute-start | bytes 258056 | tf_op jit(solution)/shard_map/ppermute | solution.py:356
  7.4 1.6 %collective-permute-start.5 = (bf16[336,128]{1,0:T(8,128)(2,1)S(1)}, bf16[336,128]{1,0:T(8,128)(2,1)S(1)}, u32[]{:S(2)}, u32[]{:S(2)}) collective-permute-start(bf16[336,128]{1,0:T(8,128)(2,1)S(1)} %get-tuple-element.23.refs_0_.payload_ref), channel_id=1, source_target_pairs={{0,4},{1,5},{2,6},{3,7},{4,0},{5,1},{6,2},{7,3},{8,12},{9,13},{10,... | collective-permute-start | bytes 258056 | tf_op jit(solution)/shard_map/ppermute | solution.py:356
  8.9 0.0 collective-permute-start.1
  8.9 0.0 collective-permute-done.3.refs_4_
  9.0 0.8 %collective-permute-start.4 = (bf16[336,128]{1,0:T(8,128)(2,1)S(1)}, bf16[336,128]{1,0:T(8,128)(2,1)S(1)}, u32[]{:S(2)}, u32[]{:S(2)}) collective-permute-start(bf16[336,128]{1,0:T(8,128)(2,1)S(1)} %collective-permute-done.3.refs_4_), channel_id=1, source_target_pairs={{0,4},{1,5},{2,6},{3,7},{4,0},{5,1},{6,2},{7,3},{8,12},{9,13},{10,... | collective-permute-start | bytes 258056 | tf_op jit(solution)/shard_map/ppermute | solution.py:356
  9.8 2.1 %collective-permute-done.refs_1_ = bf16[336,128]{1,0:T(8,128)(2,1)S(1)} collective-permute-done((bf16[336,128]{1,0:T(8,128)(2,1)S(1)}, bf16[336,128]{1,0:T(8,128)(2,1)S(1)}, u32[]{:S(2)}, u32[]{:S(2)}) %collective-permute-start) | collective-permute-done | bytes 86048 | tf_op jit(solution)/shard_map/ppermute | solution.py:356
  11.9 0.0 collective-permute-start.6
  11.9 2.1 %collective-permute-start.2 = (bf16[336,128]{1,0:T(8,128)(2,1)S(1)}, bf16[336,128]{1,0:T(8,128)(2,1)S(1)}, u32[]{:S(2)}, u32[]{:S(2)}) collective-permute-start(bf16[336,128]{1,0:T(8,128)(2,1)S(1)} %collective-permute-done.refs_1_), channel_id=1, source_target_pairs={{0,4},{1,5},{2,6},{3,7},{4,0},{5,1},{6,2},{7,3},{8,12},{9,13},{10,... | collective-permute-start | bytes 258056 | tf_op jit(solution)/shard_map/ppermute | solution.py:356
  14.1 0.0 collective-permute-done.5.refs_6_
  14.1 2.2 %collective-permute-done.1.refs_2_ = bf16[336,128]{1,0:T(8,128)(2,1)S(1)} collective-permute-done((bf16[336,128]{1,0:T(8,128)(2,1)S(1)}, bf16[336,128]{1,0:T(8,128)(2,1)S(1)}, u32[]{:S(2)}, u32[]{:S(2)}) %collective-permute-start.1) | collective-permute-done | bytes 86048 | tf_op jit(solution)/shard_map/ppermute | solution.py:356
  16.3 0.3 %collective-permute-done.4.refs_5_ = bf16[336,128]{1,0:T(8,128)(2,1)S(1)} collective-permute-done((bf16[336,128]{1,0:T(8,128)(2,1)S(1)}, bf16[336,128]{1,0:T(8,128)(2,1)S(1)}, u32[]{:S(2)}, u32[]{:S(2)}) %collective-permute-start.4) | collective-permute-done | bytes 86048 | tf_op jit(solution)/shard_map/ppermute | solution.py:356
  16.6 0.5 %collective-permute-done.6.refs_7_ = bf16[336,128]{1,0:T(8,128)(2,1)S(1)} collective-permute-done((bf16[336,128]{1,0:T(8,128)(2,1)S(1)}, bf16[336,128]{1,0:T(8,128)(2,1)S(1)}, u32[]{:S(2)}, u32[]{:S(2)}) %collective-permute-start.6) | collective-permute-done | bytes 86048 | tf_op jit(solution)/shard_map/ppermute | solution.py:356
  17.1 0.4 %collective-permute-done.2.refs_3_ = bf16[336,128]{1,0:T(8,128)(2,1)S(1)} collective-permute-done((bf16[336,128]{1,0:T(8,128)(2,1)S(1)}, bf16[336,128]{1,0:T(8,128)(2,1)S(1)}, u32[]{:S(2)}, u32[]{:S(2)}) %collective-permute-start.2) | collective-permute-done | bytes 86048 | tf_op jit(solution)/shard_map/ppermute | solution.py:356
  17.6 0.1 collective-permute-start.7
  17.6 1.2 %shard_map.103 = (f32[64,128]{1,0:T(8,128)S(1)}, bf16[2048,128]{1,0:T(8,128)(2,1)S(1)}, bf16[512,64]{1,0:T(8,128)(2,1)S(1)}, bf16[1024,128]{1,0:T(8,128)(2,1)S(1)}) custom-call(bf16[336,128]{1,0:T(8,128)(2,1)S(1)} %get-tuple-element.23.refs_0_.payload_ref, bf16[336,128]{1,0:T(8,128)(2,1)S(1)} %collective-permute-done.refs_1_, ...), custom_call_target="tpu_custom_call" | custom-call | flops 1000000000 | bytes 1048576 | tf_op jit(solution)/shard_map/pallas_call | solution.py:432
  18.9 0.0 collective-permute-done.7.refs_9_
  18.9 3.4 %shard_map.104 = (f32[1096,128]{1,0:T(8,128)S(1)}, bf16[64,4096]{1,0:T(8,128)(2,1)S(1)}, bf16[1024,256]{1,0:T(8,128)(2,1)S(1)}, f32[8,256]{1,0:T(8,128)S(1)}) custom-call(bf16[336,128]{1,0:T(8,128)(2,1)S(1)} %get-tuple-element.23.refs_0_.payload_ref, bf16[336,128]{1,0:T(8,128)(2,1)S(1)} %collective-permute-done.refs_1_, ...), custom_call_target="tpu_custom_call" | custom-call | tf_op jit(solution)/shard_map/pallas_call | solution.py:453
  22.3 0.5 %collective-permute-start.9 = (f32[1096,128]{1,0:T(8,128)S(1)}, f32[1096,128]{1,0:T(8,128)S(1)}, u32[]{:S(2)}, u32[]{:S(2)}) collective-permute-start(f32[1096,128]{1,0:T(8,128)S(1)} %get-tuple-element.28.own_ref), channel_id=1, source_target_pairs={{0,1},{1,0},{2,3},{3,2},{4,5},{5,4},{6,7},{7,6},{8,9},{9,8},{10,11... | collective-permute-start | bytes 1683464 | tf_op jit(solution)/shard_map/ppermute | solution.py:356
  22.8 0.9 %shard_map.105 = (bf16[256,128]{1,0:T(8,128)(2,1)S(1)}, f32[4,1024]{1,0:T(4,128)S(1)}) custom-call(bf16[64,4096]{1,0:T(8,128)(2,1)S(1)} %get-tuple-element.29.spread, bf16[1024,256]{1,0:T(8,128)(2,1)S(1)} %get-tuple-element.30.outer_own, f32[8,256]{1,0:T(8,128)S(1)} %get-tuple-element.31.inverse_own, ...), custom_call_target="tpu_custom_call" | custom-call | flops 268435456 | bytes 4194304 | tf_op jit(solution)/shard_map/pallas_call | solution.py:469
  23.7 0.7 %collective-permute-done.9.other_ref = f32[1096,128]{1,0:T(8,128)S(1)} collective-permute-done((f32[1096,128]{1,0:T(8,128)S(1)}, f32[1096,128]{1,0:T(8,128)S(1)}, u32[]{:S(2)}, u32[]{:S(2)}) %collective-permute-start.9) | collective-permute-done | bytes 561184 | tf_op jit(solution)/shard_map/ppermute | solution.py:356
  24.4 0.9 %shard_map.106 = (bf16[256,128]{1,0:T(8,128)(2,1)}, f32[4,1024]{1,0:T(4,128)}, f32[1024,128]{1,0:T(8,128)}, f32[4,1024]{1,0:T(4,128)}, f32[1,128]{1,0:T(1,128)}) custom-call(f32[1096,128]{1,0:T(8,128)S(1)} %get-tuple-element.28.own_ref, f32[1096,128]{1,0:T(8,128)S(1)} %collective-permute-done.9.other_ref, ...), custom_call_target="tpu_custom_call" | custom-call | tf_op jit(solution)/shard_map/pallas_call | solution.py:481
  (4 shorter events, 0.0 us)
Async XLA Ops:
  1.7 12.3 %copy-start = (s32[4]{0:T(128)S(1)}, s32[4]{0:T(128)}, u32[]{:S(2)}) copy-start(s32[4]{0:T(128)} %depth_ref.1) | copy-start | bytes 52
  1.7 7.2 %collective-permute-start.3 = (bf16[336,128]{1,0:T(8,128)(2,1)S(1)}, bf16[336,128]{1,0:T(8,128)(2,1)S(1)}, u32[]{:S(2)}, u32[]{:S(2)}) collective-permute-start(bf16[336,128]{1,0:T(8,128)(2,1)S(1)} %get-tuple-element.23.refs_0_.payload_ref), channel_id=1, source_target_pairs={{0,2},{1,3},{2,0},{3,1},{4,6},{5,7},{6,4},{7,5},{8,10},{9,11},{10,... | collective-permute-start | bytes 258056 | tf_op jit(solution)/shard_map/ppermute | solution.py:356
  4.8 7.2 %collective-permute-start = (bf16[336,128]{1,0:T(8,128)(2,1)S(1)}, bf16[336,128]{1,0:T(8,128)(2,1)S(1)}, u32[]{:S(2)}, u32[]{:S(2)}) collective-permute-start(bf16[336,128]{1,0:T(8,128)(2,1)S(1)} %get-tuple-element.23.refs_0_.payload_ref), channel_id=1, source_target_pairs={{0,8},{1,9},{2,10},{3,11},{4,12},{5,13},{6,14},{7,15},{8,0},{9,1},... | collective-permute-start | bytes 258056 | tf_op jit(solution)/shard_map/ppermute | solution.py:356
  7.4 6.7 %collective-permute-start.5 = (bf16[336,128]{1,0:T(8,128)(2,1)S(1)}, bf16[336,128]{1,0:T(8,128)(2,1)S(1)}, u32[]{:S(2)}, u32[]{:S(2)}) collective-permute-start(bf16[336,128]{1,0:T(8,128)(2,1)S(1)} %get-tuple-element.23.refs_0_.payload_ref), channel_id=1, source_target_pairs={{0,4},{1,5},{2,6},{3,7},{4,0},{5,1},{6,2},{7,3},{8,12},{9,13},{10,... | collective-permute-start | bytes 258056 | tf_op jit(solution)/shard_map/ppermute | solution.py:356
  8.9 7.4 %collective-permute-start.1 = (bf16[336,128]{1,0:T(8,128)(2,1)S(1)}, bf16[336,128]{1,0:T(8,128)(2,1)S(1)}, u32[]{:S(2)}, u32[]{:S(2)}) collective-permute-start(bf16[336,128]{1,0:T(8,128)(2,1)S(1)} %get-tuple-element.23.refs_0_.payload_ref), channel_id=1, source_target_pairs={{0,14},{1,15},{2,12},{3,13},{4,10},{5,11},{6,8},{7,9},{8,6},{9,7},... | collective-permute-start | bytes 258056 | tf_op jit(solution)/shard_map/ppermute | solution.py:356
  9.0 7.7 %collective-permute-start.4 = (bf16[336,128]{1,0:T(8,128)(2,1)S(1)}, bf16[336,128]{1,0:T(8,128)(2,1)S(1)}, u32[]{:S(2)}, u32[]{:S(2)}) collective-permute-start(bf16[336,128]{1,0:T(8,128)(2,1)S(1)} %collective-permute-done.3.refs_4_), channel_id=1, source_target_pairs={{0,4},{1,5},{2,6},{3,7},{4,0},{5,1},{6,2},{7,3},{8,12},{9,13},{10,... | collective-permute-start | bytes 258056 | tf_op jit(solution)/shard_map/ppermute | solution.py:356
  11.9 5.2 %collective-permute-start.6 = (bf16[336,128]{1,0:T(8,128)(2,1)S(1)}, bf16[336,128]{1,0:T(8,128)(2,1)S(1)}, u32[]{:S(2)}, u32[]{:S(2)}) collective-permute-start(bf16[336,128]{1,0:T(8,128)(2,1)S(1)} %collective-permute-done.refs_1_), channel_id=1, source_target_pairs={{0,2},{1,3},{2,0},{3,1},{4,6},{5,7},{6,4},{7,5},{8,10},{9,11},{10,... | collective-permute-start | bytes 258056 | tf_op jit(solution)/shard_map/ppermute | solution.py:356
  11.9 5.6 %collective-permute-start.2 = (bf16[336,128]{1,0:T(8,128)(2,1)S(1)}, bf16[336,128]{1,0:T(8,128)(2,1)S(1)}, u32[]{:S(2)}, u32[]{:S(2)}) collective-permute-start(bf16[336,128]{1,0:T(8,128)(2,1)S(1)} %collective-permute-done.refs_1_), channel_id=1, source_target_pairs={{0,4},{1,5},{2,6},{3,7},{4,0},{5,1},{6,2},{7,3},{8,12},{9,13},{10,... | collective-permute-start | bytes 258056 | tf_op jit(solution)/shard_map/ppermute | solution.py:356
  14.1 3.6 %collective-permute-start.8 = (s32[4]{0:T(128)S(1)}, s32[4]{0:T(128)S(1)}, u32[]{:S(2)}, u32[]{:S(2)}) collective-permute-start(s32[4]{0:T(128)S(1)} %copy-done), channel_id=1, source_target_pairs={{0,1},{1,0},{2,3},{3,2},{4,5},{5,4},{6,7},{7,6},{8,9},{9,8},{10,11... | collective-permute-start | bytes 56 | tf_op jit(solution)/shard_map/ppermute | solution.py:356
  17.6 1.3 %collective-permute-start.7 = (bf16[288,128]{1,0:T(8,128)(2,1)S(1)}, bf16[288,128]{1,0:T(8,128)(2,1)S(1)}, u32[]{:S(2)}, u32[]{:S(2)}) collective-permute-start(bf16[288,128]{1,0:T(8,128)(2,1)S(1)} %shard_map.102.refs_8_), channel_id=1, source_target_pairs={{0,1},{1,0},{2,3},{3,2},{4,5},{5,4},{6,7},{7,6},{8,9},{9,8},{10,11... | collective-permute-start | bytes 221192 | tf_op jit(solution)/shard_map/ppermute | solution.py:356
  22.3 2.1 %collective-permute-start.9 = (f32[1096,128]{1,0:T(8,128)S(1)}, f32[1096,128]{1,0:T(8,128)S(1)}, u32[]{:S(2)}, u32[]{:S(2)}) collective-permute-start(f32[1096,128]{1,0:T(8,128)S(1)} %get-tuple-element.28.own_ref), channel_id=1, source_target_pairs={{0,1},{1,0},{2,3},{3,2},{4,5},{5,4},{6,7},{7,6},{8,9},{9,8},{10,11... | collective-permute-start | bytes 1683464 | tf_op jit(solution)/shard_map/ppermute | solution.py:356

commit v6 on v5

--- a/solution.py
+++ b/solution.py
@@ -110,7 +110,7 @@
 
 
 def sum_kernel(
-    rows, own_ref, other_ref, update_here, left_here,
+    rows, upper_ref, upper_other_ref, own_ref, other_ref, update_here, left_here,
     update_ref, left_ref, w_ref, right_ref, bias_ref, w_here, right_here, bias_here, sems,
 ):
     copies = [
@@ -125,18 +125,22 @@
     count = sems.shape[0] - 4
     for k in range(count):
         some = slice(k * wide // count, (k + 1) * wide // count)
-        w_here[some, :] = own_ref[some, :] + other_ref[some, :]
+        if k < count // 2:
+            w_here[some, :] = upper_ref[some, :] + upper_other_ref[some, :]
+        else:
+            rest = slice(some.start - wide // 2, some.stop - wide // 2)
+            w_here[some, :] = own_ref[rest, :] + other_ref[rest, :]
         copies.append(pltpu.make_async_copy(w_here.at[some], w_ref.at[some], sems.at[4 + k]))
         copies[-1].start()
     core = lax.rem(lax.axis_index("pi"), CORES)
     tiles = right_ref.shape[1] // LANES
-    begin = pl.multiple_of(wide + core * rows * tiles, 8)
+    begin = pl.multiple_of(wide // 2 + core * rows * tiles, 8)
     part = own_ref[pl.ds(begin, rows * tiles), :] + other_ref[pl.ds(begin, rows * tiles), :]
     for row in range(rows):
         for tile in range(tiles):
             at = row * tiles + tile
             right_here[row : row + 1, tile * LANES : (tile + 1) * LANES] = part[at : at + 1, :]
-    last = wide + CORES * rows * tiles
+    last = wide // 2 + CORES * rows * tiles
     bias_here[...] = own_ref[last : last + 1, :] + other_ref[last : last + 1, :]
     copies[2].start()
     copies[3].start()
@@ -236,8 +240,8 @@
     rows, total, pieces, used, arrays, route = sizes
     piece = views(refs[:arrays], used)
     own_ref, other_ref, right_ref, cots, left_halves = refs[arrays : arrays + 5]
-    partial_ref, spread, outer_own, inverse_own = refs[arrays + 5 : arrays + 9]
-    turned, inverse, outer = refs[arrays + 9 :]
+    upper_ref, partial_ref, spread, outer_own, inverse_own = refs[arrays + 5 : arrays + 10]
+    turned, inverse, outer = refs[arrays + 10 :]
     pairs = rows * total
     tiles = C * C // LANES
     per_tile = LANES // total
@@ -301,8 +305,13 @@
             outer_own[some, :] = outer[some, :pairs]
             grad = dot(outer[some, :], cots[...], 1, 0)
             for k in range(chunk):
-                partial_ref[pl.ds(first + k, C, stride=C), :] = grad[k * C : (k + 1) * C, :]
-    wide = C * C
+                half = C // 2
+                begin = k * C
+                upper_ref[pl.ds(first + k, half, stride=C), :] = grad[begin : begin + half, :]
+                partial_ref[pl.ds(first + k, half, stride=C), :] = grad[
+                    begin + half : begin + C, :
+                ]
+    wide = C * C // 2
     last = wide + right_ref.shape[0]
     partial_ref[wide:last, :] = right_ref[...]
     partial_ref[last : last + 8, :] = dot(
@@ -450,10 +459,11 @@
         compiler_params=pltpu.CompilerParams(vmem_limit_bytes=LARGE),
         cost_estimate=pl.CostEstimate(flops=10**9, bytes_accessed=2**20, transcendentals=0),
     )(*arrived, w_here, depth_other.reshape(1, rows))
-    partial, spread, outer_own, inverse_own = pl.pallas_call(
+    upper, partial, spread, outer_own, inverse_own = pl.pallas_call(
         functools.partial(main_kernel, (rows, total, pieces, used, len(arrived), route)),
         out_shape=(
-            pltpu.VMEM((C * C + chip_rows * tiles + 8, LANES), F32),
+            pltpu.VMEM((C * C // 2, LANES), F32),
+            pltpu.VMEM((C * C // 2 + chip_rows * tiles + 8, LANES), F32),
             pltpu.VMEM((per_tile * alignment, C * LANES), BF16),
             pltpu.VMEM((C * C, pairs), BF16),
             pltpu.VMEM((pieces, pairs), F32),
@@ -465,6 +475,7 @@
         ],
         compiler_params=pltpu.CompilerParams(vmem_limit_bytes=LARGE),
     )(*arrived, mine, theirs, right_partial, cots, left_halves)
+    upper_other = swap(upper, (1, 1), size)
     other = swap(partial, (1, 1), size)
     update, grad_left = pl.pallas_call(
         functools.partial(own_kernel, rows),
@@ -495,7 +506,7 @@
             pltpu.SemaphoreType.DMA((8,)),
         ],
         compiler_params=pltpu.CompilerParams(vmem_limit_bytes=SMALL),
-    )(partial, other, update, grad_left)
+    )(upper, upper_other, partial, other, update, grad_left)
     return (
         update.reshape(rows, total, channels),
         grad_left,

time: 25.4 us -> 25.4 us (level)
    ppermute x10 -> x11, starting transfers between devices: 10.8 us -> 10.9 us  [swap(): lax.ppermute(x, 'pi', [(i, i ^ masks[i % CORES]) for i in range(size)])]
    ppermute x10 -> x11, waiting for transfers between devices: 6.28 us -> 6.21 us  [swap(): lax.ppermute(x, 'pi', [(i, i ^ masks[i % CORES]) for i in range(size)])]
  transfers between devices with their start and end apart: 10 -> 11, of which waited for: 6 -> 6; matrix products, arithmetic and copies ran while one was open for 0% -> 0% of each run, Pallas kernels for 9% -> 9%
where the time goes in v6:
time: 25.4 us; the launch traced here: 25.3 us
  starting transfers between devices  10.9 us (43%)
  Pallas kernels  7.51 us (30%)
  waiting for transfers between devices  6.21 us (24%)
  between operations  0.69 us (3%)
    ppermute x11, starting transfers between devices, swap(): lax.ppermute(x, 'pi', [(i, i ^ masks[i % CORES]) for i in range(size)])  10.9 us
    ppermute x11, waiting for transfers between devices, swap(): lax.ppermute(x, 'pi', [(i, i ^ masks[i % CORES]) for i in range(size)])  6.21 us
    pallas_call x1, Pallas kernels, gathered(): pl.pallas_call(functools.partial(main_kernel, (rows, total, pieces, used,...  3.36 us
    pallas_call x1, Pallas kernels, gathered(): pl.pallas_call(functools.partial(right_kernel, (rows, total, pieces, alig...  1.22 us
    pallas_call x1, Pallas kernels, gathered(): pl.pallas_call(pack_kernel, out_shape=(pltpu.VMEM((used, LANES), BF16), p...  1.09 us
    pallas_call x1, Pallas kernels, gathered(): pl.pallas_call(functools.partial(own_kernel, rows), out_shape=(pltpu.VMEM...  0.93 us
    pallas_call x1, Pallas kernels, gathered(): pl.pallas_call(functools.partial(sum_kernel, rows), out_shape=(jax.ShapeD...  0.88 us
  transfers between devices with their start and end apart: 11, of which 6 were waited for; matrix products, arithmetic and copies ran while one was open for 0% of the time, Pallas kernels for 9%

profile of v6, /device:TPU:0, one launch (start us, length us, event | category | flops | bytes accessed | tf_op | source)
XLA Modules:
  0.0 25.3 jit_solution(5846264538653793773)
XLA Ops:
  0.6 1.1 %shard_map.101 = (bf16[336,128]{1,0:T(8,128)(2,1)S(1)}, f32[1,128]{1,0:T(1,128)S(1)}, bf16[1024,128]{1,0:T(8,128)(2,1)S(1)}) custom-call(bf16[4,1024]{1,0:T(4,128)(2,1)} %left_ref.1, bf16[4,1024]{1,0:T(4,128)(2,1)} %right_ref.1, bf16[256,128]{1,0:T(8,128)(2,1)} %bitcast.6, s32[4]{0:T(128)} %depth_ref.1, f32[1,128]{1,0:T(1,128)} %bitcast.8, ...), custom_call_target="tpu_custom_call" | custom-call | flops 1000000000 | bytes 1048576 | tf_op jit(solution)/shard_map/pallas_call | solution.py:406
  1.7 0.0 copy-start
  1.7 3.0 %collective-permute-start.3 = (bf16[336,128]{1,0:T(8,128)(2,1)S(1)}, bf16[336,128]{1,0:T(8,128)(2,1)S(1)}, u32[]{:S(2)}, u32[]{:S(2)}) collective-permute-start(bf16[336,128]{1,0:T(8,128)(2,1)S(1)} %get-tuple-element.24.refs_0_.payload_ref), channel_id=1, source_target_pairs={{0,2},{1,3},{2,0},{3,1},{4,6},{5,7},{6,4},{7,5},{8,10},{9,11},{10,... | collective-permute-start | bytes 258056 | tf_op jit(solution)/shard_map/ppermute | solution.py:365
  4.8 2.6 %collective-permute-start = (bf16[336,128]{1,0:T(8,128)(2,1)S(1)}, bf16[336,128]{1,0:T(8,128)(2,1)S(1)}, u32[]{:S(2)}, u32[]{:S(2)}) collective-permute-start(bf16[336,128]{1,0:T(8,128)(2,1)S(1)} %get-tuple-element.24.refs_0_.payload_ref), channel_id=1, source_target_pairs={{0,8},{1,9},{2,10},{3,11},{4,12},{5,13},{6,14},{7,15},{8,0},{9,1},... | collective-permute-start | bytes 258056 | tf_op jit(solution)/shard_map/ppermute | solution.py:365
  7.4 1.6 %collective-permute-start.5 = (bf16[336,128]{1,0:T(8,128)(2,1)S(1)}, bf16[336,128]{1,0:T(8,128)(2,1)S(1)}, u32[]{:S(2)}, u32[]{:S(2)}) collective-permute-start(bf16[336,128]{1,0:T(8,128)(2,1)S(1)} %get-tuple-element.24.refs_0_.payload_ref), channel_id=1, source_target_pairs={{0,4},{1,5},{2,6},{3,7},{4,0},{5,1},{6,2},{7,3},{8,12},{9,13},{10,... | collective-permute-start | bytes 258056 | tf_op jit(solution)/shard_map/ppermute | solution.py:365
  9.0 0.8 %collective-permute-start.4 = (bf16[336,128]{1,0:T(8,128)(2,1)S(1)}, bf16[336,128]{1,0:T(8,128)(2,1)S(1)}, u32[]{:S(2)}, u32[]{:S(2)}) collective-permute-start(bf16[336,128]{1,0:T(8,128)(2,1)S(1)} %collective-permute-done.3.refs_4_), channel_id=1, source_target_pairs={{0,4},{1,5},{2,6},{3,7},{4,0},{5,1},{6,2},{7,3},{8,12},{9,13},{10,... | collective-permute-start | bytes 258056 | tf_op jit(solution)/shard_map/ppermute | solution.py:365
  9.8 2.1 %collective-permute-done.refs_1_ = bf16[336,128]{1,0:T(8,128)(2,1)S(1)} collective-permute-done((bf16[336,128]{1,0:T(8,128)(2,1)S(1)}, bf16[336,128]{1,0:T(8,128)(2,1)S(1)}, u32[]{:S(2)}, u32[]{:S(2)}) %collective-permute-start) | collective-permute-done | bytes 86048 | tf_op jit(solution)/shard_map/ppermute | solution.py:365
  11.9 0.0 collective-permute-start.6
  11.9 2.1 %collective-permute-start.2 = (bf16[336,128]{1,0:T(8,128)(2,1)S(1)}, bf16[336,128]{1,0:T(8,128)(2,1)S(1)}, u32[]{:S(2)}, u32[]{:S(2)}) collective-permute-start(bf16[336,128]{1,0:T(8,128)(2,1)S(1)} %collective-permute-done.refs_1_), channel_id=1, source_target_pairs={{0,4},{1,5},{2,6},{3,7},{4,0},{5,1},{6,2},{7,3},{8,12},{9,13},{10,... | collective-permute-start | bytes 258056 | tf_op jit(solution)/shard_map/ppermute | solution.py:365
  14.1 0.0 collective-permute-start.8
  14.1 2.2 %collective-permute-done.1.refs_2_ = bf16[336,128]{1,0:T(8,128)(2,1)S(1)} collective-permute-done((bf16[336,128]{1,0:T(8,128)(2,1)S(1)}, bf16[336,128]{1,0:T(8,128)(2,1)S(1)}, u32[]{:S(2)}, u32[]{:S(2)}) %collective-permute-start.1) | collective-permute-done | bytes 86048 | tf_op jit(solution)/shard_map/ppermute | solution.py:365
  16.3 0.3 %collective-permute-done.4.refs_5_ = bf16[336,128]{1,0:T(8,128)(2,1)S(1)} collective-permute-done((bf16[336,128]{1,0:T(8,128)(2,1)S(1)}, bf16[336,128]{1,0:T(8,128)(2,1)S(1)}, u32[]{:S(2)}, u32[]{:S(2)}) %collective-permute-start.4) | collective-permute-done | bytes 86048 | tf_op jit(solution)/shard_map/ppermute | solution.py:365
  16.6 0.5 %collective-permute-done.6.refs_7_ = bf16[336,128]{1,0:T(8,128)(2,1)S(1)} collective-permute-done((bf16[336,128]{1,0:T(8,128)(2,1)S(1)}, bf16[336,128]{1,0:T(8,128)(2,1)S(1)}, u32[]{:S(2)}, u32[]{:S(2)}) %collective-permute-start.6) | collective-permute-done | bytes 86048 | tf_op jit(solution)/shard_map/ppermute | solution.py:365
  17.1 0.4 %collective-permute-done.2.refs_3_ = bf16[336,128]{1,0:T(8,128)(2,1)S(1)} collective-permute-done((bf16[336,128]{1,0:T(8,128)(2,1)S(1)}, bf16[336,128]{1,0:T(8,128)(2,1)S(1)}, u32[]{:S(2)}, u32[]{:S(2)}) %collective-permute-start.2) | collective-permute-done | bytes 86048 | tf_op jit(solution)/shard_map/ppermute | solution.py:365
  17.6 0.1 collective-permute-start.7
  17.6 0.0 collective-permute-done.8
  17.6 1.2 %shard_map.103 = (f32[64,128]{1,0:T(8,128)S(1)}, bf16[2048,128]{1,0:T(8,128)(2,1)S(1)}, bf16[512,64]{1,0:T(8,128)(2,1)S(1)}, bf16[1024,128]{1,0:T(8,128)(2,1)S(1)}) custom-call(bf16[336,128]{1,0:T(8,128)(2,1)S(1)} %get-tuple-element.24.refs_0_.payload_ref, bf16[336,128]{1,0:T(8,128)(2,1)S(1)} %collective-permute-done.refs_1_, ...), custom_call_target="tpu_custom_call" | custom-call | flops 1000000000 | bytes 1048576 | tf_op jit(solution)/shard_map/pallas_call | solution.py:441
  18.9 0.0 collective-permute-done.7.refs_9_
  18.9 3.4 %shard_map.104 = (f32[512,128]{1,0:T(8,128)S(1)}, f32[584,128]{1,0:T(8,128)S(1)}, bf16[64,4096]{1,0:T(8,128)(2,1)S(1)}, bf16[1024,256]{1,0:T(8,128)(2,1)S(1)}, f32[8,256]{1,0:T(8,128)S(1)}) custom-call(bf16[336,128]{1,0:T(8,128)(2,1)S(1)} %get-tuple-element.24.refs_0_.payload_ref, bf16[336,128]{1,0:T(8,128)(2,1)S(1)} %collective-permute-done.refs_1_, ...), custom_call_target="tpu_custom_call" | custom-call | tf_op jit(solution)/shard_map/pallas_call | solution.py:462
  22.3 0.5 %collective-permute-start.10 = (f32[584,128]{1,0:T(8,128)S(1)}, f32[584,128]{1,0:T(8,128)S(1)}, u32[]{:S(2)}, u32[]{:S(2)}) collective-permute-start(f32[584,128]{1,0:T(8,128)S(1)} %get-tuple-element.30.own_ref), channel_id=1, source_target_pairs={{0,1},{1,0},{2,3},{3,2},{4,5},{5,4},{6,7},{7,6},{8,9},{9,8},{10,11... | collective-permute-start | bytes 897032 | tf_op jit(solution)/shard_map/ppermute | solution.py:365
  22.8 0.1 collective-permute-start.9
  22.9 0.9 %shard_map.105 = (bf16[256,128]{1,0:T(8,128)(2,1)S(1)}, f32[4,1024]{1,0:T(4,128)S(1)}) custom-call(bf16[64,4096]{1,0:T(8,128)(2,1)S(1)} %get-tuple-element.31.spread, bf16[1024,256]{1,0:T(8,128)(2,1)S(1)} %get-tuple-element.32.outer_own, f32[8,256]{1,0:T(8,128)S(1)} %get-tuple-element.33.inverse_own, ...), custom_call_target="tpu_custom_call" | custom-call | flops 268435456 | bytes 4194304 | tf_op jit(solution)/shard_map/pallas_call | solution.py:480
  23.8 0.6 %collective-permute-done.9.upper_other_ref = f32[512,128]{1,0:T(8,128)S(1)} collective-permute-done((f32[512,128]{1,0:T(8,128)S(1)}, f32[512,128]{1,0:T(8,128)S(1)}, u32[]{:S(2)}, u32[]{:S(2)}) %collective-permute-start.9) | collective-permute-done | bytes 262176 | tf_op jit(solution)/shard_map/ppermute | solution.py:365
  24.4 0.9 %shard_map.106 = (bf16[256,128]{1,0:T(8,128)(2,1)}, f32[4,1024]{1,0:T(4,128)}, f32[1024,128]{1,0:T(8,128)}, f32[4,1024]{1,0:T(4,128)}, f32[1,128]{1,0:T(1,128)}) custom-call(f32[512,128]{1,0:T(8,128)S(1)} %get-tuple-element.29.upper_ref, f32[512,128]{1,0:T(8,128)S(1)} %collective-permute-done.9.upper_other_ref, f32[584,128]{1,0:T(8,128)S(1)} %get-tuple-element.30.own_ref, ...), custom_call_target="tpu_custom_call" | custom-call | tf_op jit(solution)/shard_map/pallas_call | solution.py:492
  (6 shorter events, 0.0 us)
Async XLA Ops:
  1.7 12.3 %copy-start = (s32[4]{0:T(128)S(1)}, s32[4]{0:T(128)}, u32[]{:S(2)}) copy-start(s32[4]{0:T(128)} %depth_ref.1) | copy-start | bytes 52
  1.7 7.2 %collective-permute-start.3 = (bf16[336,128]{1,0:T(8,128)(2,1)S(1)}, bf16[336,128]{1,0:T(8,128)(2,1)S(1)}, u32[]{:S(2)}, u32[]{:S(2)}) collective-permute-start(bf16[336,128]{1,0:T(8,128)(2,1)S(1)} %get-tuple-element.24.refs_0_.payload_ref), channel_id=1, source_target_pairs={{0,2},{1,3},{2,0},{3,1},{4,6},{5,7},{6,4},{7,5},{8,10},{9,11},{10,... | collective-permute-start | bytes 258056 | tf_op jit(solution)/shard_map/ppermute | solution.py:365
  4.8 7.2 %collective-permute-start = (bf16[336,128]{1,0:T(8,128)(2,1)S(1)}, bf16[336,128]{1,0:T(8,128)(2,1)S(1)}, u32[]{:S(2)}, u32[]{:S(2)}) collective-permute-start(bf16[336,128]{1,0:T(8,128)(2,1)S(1)} %get-tuple-element.24.refs_0_.payload_ref), channel_id=1, source_target_pairs={{0,8},{1,9},{2,10},{3,11},{4,12},{5,13},{6,14},{7,15},{8,0},{9,1},... | collective-permute-start | bytes 258056 | tf_op jit(solution)/shard_map/ppermute | solution.py:365
  7.4 6.7 %collective-permute-start.5 = (bf16[336,128]{1,0:T(8,128)(2,1)S(1)}, bf16[336,128]{1,0:T(8,128)(2,1)S(1)}, u32[]{:S(2)}, u32[]{:S(2)}) collective-permute-start(bf16[336,128]{1,0:T(8,128)(2,1)S(1)} %get-tuple-element.24.refs_0_.payload_ref), channel_id=1, source_target_pairs={{0,4},{1,5},{2,6},{3,7},{4,0},{5,1},{6,2},{7,3},{8,12},{9,13},{10,... | collective-permute-start | bytes 258056 | tf_op jit(solution)/shard_map/ppermute | solution.py:365
  8.9 7.4 %collective-permute-start.1 = (bf16[336,128]{1,0:T(8,128)(2,1)S(1)}, bf16[336,128]{1,0:T(8,128)(2,1)S(1)}, u32[]{:S(2)}, u32[]{:S(2)}) collective-permute-start(bf16[336,128]{1,0:T(8,128)(2,1)S(1)} %get-tuple-element.24.refs_0_.payload_ref), channel_id=1, source_target_pairs={{0,14},{1,15},{2,12},{3,13},{4,10},{5,11},{6,8},{7,9},{8,6},{9,7},... | collective-permute-start | bytes 258056 | tf_op jit(solution)/shard_map/ppermute | solution.py:365
  9.0 7.7 %collective-permute-start.4 = (bf16[336,128]{1,0:T(8,128)(2,1)S(1)}, bf16[336,128]{1,0:T(8,128)(2,1)S(1)}, u32[]{:S(2)}, u32[]{:S(2)}) collective-permute-start(bf16[336,128]{1,0:T(8,128)(2,1)S(1)} %collective-permute-done.3.refs_4_), channel_id=1, source_target_pairs={{0,4},{1,5},{2,6},{3,7},{4,0},{5,1},{6,2},{7,3},{8,12},{9,13},{10,... | collective-permute-start | bytes 258056 | tf_op jit(solution)/shard_map/ppermute | solution.py:365
  11.9 5.2 %collective-permute-start.6 = (bf16[336,128]{1,0:T(8,128)(2,1)S(1)}, bf16[336,128]{1,0:T(8,128)(2,1)S(1)}, u32[]{:S(2)}, u32[]{:S(2)}) collective-permute-start(bf16[336,128]{1,0:T(8,128)(2,1)S(1)} %collective-permute-done.refs_1_), channel_id=1, source_target_pairs={{0,2},{1,3},{2,0},{3,1},{4,6},{5,7},{6,4},{7,5},{8,10},{9,11},{10,... | collective-permute-start | bytes 258056 | tf_op jit(solution)/shard_map/ppermute | solution.py:365
  11.9 5.6 %collective-permute-start.2 = (bf16[336,128]{1,0:T(8,128)(2,1)S(1)}, bf16[336,128]{1,0:T(8,128)(2,1)S(1)}, u32[]{:S(2)}, u32[]{:S(2)}) collective-permute-start(bf16[336,128]{1,0:T(8,128)(2,1)S(1)} %collective-permute-done.refs_1_), channel_id=1, source_target_pairs={{0,4},{1,5},{2,6},{3,7},{4,0},{5,1},{6,2},{7,3},{8,12},{9,13},{10,... | collective-permute-start | bytes 258056 | tf_op jit(solution)/shard_map/ppermute | solution.py:365
  14.1 3.6 %collective-permute-start.8 = (s32[4]{0:T(128)S(1)}, s32[4]{0:T(128)S(1)}, u32[]{:S(2)}, u32[]{:S(2)}) collective-permute-start(s32[4]{0:T(128)S(1)} %copy-done), channel_id=1, source_target_pairs={{0,1},{1,0},{2,3},{3,2},{4,5},{5,4},{6,7},{7,6},{8,9},{9,8},{10,11... | collective-permute-start | bytes 56 | tf_op jit(solution)/shard_map/ppermute | solution.py:365
  17.6 1.3 %collective-permute-start.7 = (bf16[288,128]{1,0:T(8,128)(2,1)S(1)}, bf16[288,128]{1,0:T(8,128)(2,1)S(1)}, u32[]{:S(2)}, u32[]{:S(2)}) collective-permute-start(bf16[288,128]{1,0:T(8,128)(2,1)S(1)} %shard_map.102.refs_8_), channel_id=1, source_target_pairs={{0,1},{1,0},{2,3},{3,2},{4,5},{5,4},{6,7},{7,6},{8,9},{9,8},{10,11... | collective-permute-start | bytes 221192 | tf_op jit(solution)/shard_map/ppermute | solution.py:365
  22.3 2.1 %collective-permute-start.10 = (f32[584,128]{1,0:T(8,128)S(1)}, f32[584,128]{1,0:T(8,128)S(1)}, u32[]{:S(2)}, u32[]{:S(2)}) collective-permute-start(f32[584,128]{1,0:T(8,128)S(1)} %get-tuple-element.30.own_ref), channel_id=1, source_target_pairs={{0,1},{1,0},{2,3},{3,2},{4,5},{5,4},{6,7},{7,6},{8,9},{9,8},{10,11... | collective-permute-start | bytes 897032 | tf_op jit(solution)/shard_map/ppermute | solution.py:365
  22.8 1.6 %collective-permute-start.9 = (f32[512,128]{1,0:T(8,128)S(1)}, f32[512,128]{1,0:T(8,128)S(1)}, u32[]{:S(2)}, u32[]{:S(2)}) collective-permute-start(f32[512,128]{1,0:T(8,128)S(1)} %get-tuple-element.29.upper_ref), channel_id=1, source_target_pairs={{0,1},{1,0},{2,3},{3,2},{4,5},{5,4},{6,7},{7,6},{8,9},{9,8},{10,11... | collective-permute-start | bytes 786440 | tf_op jit(solution)/shard_map/ppermute | solution.py:365

commit v7 on v5

--- a/solution.py
+++ b/solution.py
@@ -236,8 +236,8 @@
     rows, total, pieces, used, arrays, route = sizes
     piece = views(refs[:arrays], used)
     own_ref, other_ref, right_ref, cots, left_halves = refs[arrays : arrays + 5]
-    partial_ref, spread, outer_own, inverse_own = refs[arrays + 5 : arrays + 9]
-    turned, inverse, outer = refs[arrays + 9 :]
+    partial_ref, spread, outer, inverse_own = refs[arrays + 5 : arrays + 9]
+    turned, inverse = refs[arrays + 9 :]
     pairs = rows * total
     tiles = C * C // LANES
     per_tile = LANES // total
@@ -298,7 +298,6 @@
         if d % chunk == chunk - 1:
             first = d + 1 - chunk
             some = slice(first * C, (d + 1) * C)
-            outer_own[some, :] = outer[some, :pairs]
             grad = dot(outer[some, :], cots[...], 1, 0)
             for k in range(chunk):
                 partial_ref[pl.ds(first + k, C, stride=C), :] = grad[k * C : (k + 1) * C, :]
@@ -312,7 +311,7 @@
 
 
 def own_kernel(
-    rows, spread, outer_own, inverse_own, payload_ref, w_swap_ref, bias_ref,
+    rows, spread, outer, inverse_own, payload_ref, w_swap_ref, bias_ref,
     update_ref, left_ref, g_left, stage,
 ):
     some = 8
@@ -321,7 +320,7 @@
     alignment = tiles * (LANES // C)
     halves = pairs // LANES
     group = LANES // C
-    update = dot(outer_own[...], w_swap_ref[...], 0, 0)
+    update = dot(outer[:, :pairs], w_swap_ref[...], 0, 0)
     update_ref[...] = (update + bias_ref[...]).astype(BF16)
     for d in range(C):
         if d % some == 0:
@@ -450,18 +449,17 @@
         compiler_params=pltpu.CompilerParams(vmem_limit_bytes=LARGE),
         cost_estimate=pl.CostEstimate(flops=10**9, bytes_accessed=2**20, transcendentals=0),
     )(*arrived, w_here, depth_other.reshape(1, rows))
-    partial, spread, outer_own, inverse_own = pl.pallas_call(
+    partial, spread, outer, inverse_own = pl.pallas_call(
         functools.partial(main_kernel, (rows, total, pieces, used, len(arrived), route)),
         out_shape=(
             pltpu.VMEM((C * C + chip_rows * tiles + 8, LANES), F32),
             pltpu.VMEM((per_tile * alignment, C * LANES), BF16),
-            pltpu.VMEM((C * C, pairs), BF16),
+            pltpu.VMEM((C * C, pieces * pairs), BF16),
             pltpu.VMEM((pieces, pairs), F32),
         ),
         scratch_shapes=[
             pltpu.VMEM((width, LANES), F32),
             pltpu.VMEM((pieces, pairs), F32),
-            pltpu.VMEM((C * C, pieces * pairs), BF16),
         ],
         compiler_params=pltpu.CompilerParams(vmem_limit_bytes=LARGE),
     )(*arrived, mine, theirs, right_partial, cots, left_halves)
@@ -477,7 +475,7 @@
         cost_estimate=pl.CostEstimate(
             flops=8 * pairs * C * C * channels, bytes_accessed=4 * 2**20, transcendentals=0
         ),
-    )(spread, outer_own, inverse_own, payload, w_swap, bias_row)
+    )(spread, outer, inverse_own, payload, w_swap, bias_row)
     update, grad_left, grad_w, grad_right, grad_bias = pl.pallas_call(
         functools.partial(sum_kernel, rows),
         out_shape=(

time: 25.4 us -> 25.4 us (level)
  no operation moved by 1% of the time
where the time goes in v7:
time: 25.4 us; the launch traced here: 25.2 us
  starting transfers between devices  10.8 us (43%)
  Pallas kernels  7.5 us (30%)
  waiting for transfers between devices  6.28 us (25%)
  between operations  0.68 us (3%)
    ppermute x10, starting transfers between devices, swap(): lax.ppermute(x, 'pi', [(i, i ^ masks[i % CORES]) for i in range(size)])  10.8 us
    ppermute x10, waiting for transfers between devices, swap(): lax.ppermute(x, 'pi', [(i, i ^ masks[i % CORES]) for i in range(size)])  6.28 us
    pallas_call x1, Pallas kernels, gathered(): pl.pallas_call(functools.partial(main_kernel, (rows, total, pieces, used,...  3.34 us
    pallas_call x1, Pallas kernels, gathered(): pl.pallas_call(functools.partial(right_kernel, (rows, total, pieces, alig...  1.22 us
    pallas_call x1, Pallas kernels, gathered(): pl.pallas_call(pack_kernel, out_shape=(pltpu.VMEM((used, LANES), BF16), p...  1.09 us
    pallas_call x1, Pallas kernels, gathered(): pl.pallas_call(functools.partial(own_kernel, rows), out_shape=(pltpu.VMEM...  0.94 us
    pallas_call x1, Pallas kernels, gathered(): pl.pallas_call(functools.partial(sum_kernel, rows), out_shape=(jax.ShapeD...  0.88 us
  transfers between devices with their start and end apart: 10, of which 6 were waited for; matrix products, arithmetic and copies ran while one was open for 0% of the time, Pallas kernels for 9%

profile of v7, /device:TPU:0, one launch (start us, length us, event | category | flops | bytes accessed | tf_op | source)
XLA Modules:
  0.0 25.2 jit_solution(14236349661657887723)
XLA Ops:
  0.6 1.1 %shard_map.101 = (bf16[336,128]{1,0:T(8,128)(2,1)S(1)}, f32[1,128]{1,0:T(1,128)S(1)}, bf16[1024,128]{1,0:T(8,128)(2,1)S(1)}) custom-call(bf16[4,1024]{1,0:T(4,128)(2,1)} %left_ref.1, bf16[4,1024]{1,0:T(4,128)(2,1)} %right_ref.1, bf16[256,128]{1,0:T(8,128)(2,1)} %bitcast.6, s32[4]{0:T(128)} %depth_ref.1, f32[1,128]{1,0:T(1,128)} %bitcast.8, ...), custom_call_target="tpu_custom_call" | custom-call | flops 1000000000 | bytes 1048576 | tf_op jit(solution)/shard_map/pallas_call | solution.py:396
  1.7 3.0 %collective-permute-start.3 = (bf16[336,128]{1,0:T(8,128)(2,1)S(1)}, bf16[336,128]{1,0:T(8,128)(2,1)S(1)}, u32[]{:S(2)}, u32[]{:S(2)}) collective-permute-start(bf16[336,128]{1,0:T(8,128)(2,1)S(1)} %get-tuple-element.23.refs_0_.payload_ref), channel_id=1, source_target_pairs={{0,2},{1,3},{2,0},{3,1},{4,6},{5,7},{6,4},{7,5},{8,10},{9,11},{10,... | collective-permute-start | bytes 258056 | tf_op jit(solution)/shard_map/ppermute | solution.py:355
  4.8 2.6 %collective-permute-start = (bf16[336,128]{1,0:T(8,128)(2,1)S(1)}, bf16[336,128]{1,0:T(8,128)(2,1)S(1)}, u32[]{:S(2)}, u32[]{:S(2)}) collective-permute-start(bf16[336,128]{1,0:T(8,128)(2,1)S(1)} %get-tuple-element.23.refs_0_.payload_ref), channel_id=1, source_target_pairs={{0,8},{1,9},{2,10},{3,11},{4,12},{5,13},{6,14},{7,15},{8,0},{9,1},... | collective-permute-start | bytes 258056 | tf_op jit(solution)/shard_map/ppermute | solution.py:355
  7.4 1.6 %collective-permute-start.5 = (bf16[336,128]{1,0:T(8,128)(2,1)S(1)}, bf16[336,128]{1,0:T(8,128)(2,1)S(1)}, u32[]{:S(2)}, u32[]{:S(2)}) collective-permute-start(bf16[336,128]{1,0:T(8,128)(2,1)S(1)} %get-tuple-element.23.refs_0_.payload_ref), channel_id=1, source_target_pairs={{0,4},{1,5},{2,6},{3,7},{4,0},{5,1},{6,2},{7,3},{8,12},{9,13},{10,... | collective-permute-start | bytes 258056 | tf_op jit(solution)/shard_map/ppermute | solution.py:355
  8.9 0.0 collective-permute-start.1
  8.9 0.0 collective-permute-done.3.refs_4_
  8.9 0.8 %collective-permute-start.4 = (bf16[336,128]{1,0:T(8,128)(2,1)S(1)}, bf16[336,128]{1,0:T(8,128)(2,1)S(1)}, u32[]{:S(2)}, u32[]{:S(2)}) collective-permute-start(bf16[336,128]{1,0:T(8,128)(2,1)S(1)} %collective-permute-done.3.refs_4_), channel_id=1, source_target_pairs={{0,4},{1,5},{2,6},{3,7},{4,0},{5,1},{6,2},{7,3},{8,12},{9,13},{10,... | collective-permute-start | bytes 258056 | tf_op jit(solution)/shard_map/ppermute | solution.py:355
  9.8 2.1 %collective-permute-done.refs_1_ = bf16[336,128]{1,0:T(8,128)(2,1)S(1)} collective-permute-done((bf16[336,128]{1,0:T(8,128)(2,1)S(1)}, bf16[336,128]{1,0:T(8,128)(2,1)S(1)}, u32[]{:S(2)}, u32[]{:S(2)}) %collective-permute-start) | collective-permute-done | bytes 86048 | tf_op jit(solution)/shard_map/ppermute | solution.py:355
  11.9 0.0 collective-permute-start.6
  11.9 2.1 %collective-permute-start.2 = (bf16[336,128]{1,0:T(8,128)(2,1)S(1)}, bf16[336,128]{1,0:T(8,128)(2,1)S(1)}, u32[]{:S(2)}, u32[]{:S(2)}) collective-permute-start(bf16[336,128]{1,0:T(8,128)(2,1)S(1)} %collective-permute-done.refs_1_), channel_id=1, source_target_pairs={{0,4},{1,5},{2,6},{3,7},{4,0},{5,1},{6,2},{7,3},{8,12},{9,13},{10,... | collective-permute-start | bytes 258056 | tf_op jit(solution)/shard_map/ppermute | solution.py:355
  14.1 0.0 collective-permute-done.5.refs_6_
  14.1 0.0 collective-permute-start.8
  14.1 2.2 %collective-permute-done.1.refs_2_ = bf16[336,128]{1,0:T(8,128)(2,1)S(1)} collective-permute-done((bf16[336,128]{1,0:T(8,128)(2,1)S(1)}, bf16[336,128]{1,0:T(8,128)(2,1)S(1)}, u32[]{:S(2)}, u32[]{:S(2)}) %collective-permute-start.1) | collective-permute-done | bytes 86048 | tf_op jit(solution)/shard_map/ppermute | solution.py:355
  16.3 0.3 %collective-permute-done.4.refs_5_ = bf16[336,128]{1,0:T(8,128)(2,1)S(1)} collective-permute-done((bf16[336,128]{1,0:T(8,128)(2,1)S(1)}, bf16[336,128]{1,0:T(8,128)(2,1)S(1)}, u32[]{:S(2)}, u32[]{:S(2)}) %collective-permute-start.4) | collective-permute-done | bytes 86048 | tf_op jit(solution)/shard_map/ppermute | solution.py:355
  16.6 0.5 %collective-permute-done.6.refs_7_ = bf16[336,128]{1,0:T(8,128)(2,1)S(1)} collective-permute-done((bf16[336,128]{1,0:T(8,128)(2,1)S(1)}, bf16[336,128]{1,0:T(8,128)(2,1)S(1)}, u32[]{:S(2)}, u32[]{:S(2)}) %collective-permute-start.6) | collective-permute-done | bytes 86048 | tf_op jit(solution)/shard_map/ppermute | solution.py:355
  17.1 0.4 %collective-permute-done.2.refs_3_ = bf16[336,128]{1,0:T(8,128)(2,1)S(1)} collective-permute-done((bf16[336,128]{1,0:T(8,128)(2,1)S(1)}, bf16[336,128]{1,0:T(8,128)(2,1)S(1)}, u32[]{:S(2)}, u32[]{:S(2)}) %collective-permute-start.2) | collective-permute-done | bytes 86048 | tf_op jit(solution)/shard_map/ppermute | solution.py:355
  17.5 0.1 collective-permute-start.7
  17.6 1.2 %shard_map.103 = (f32[64,128]{1,0:T(8,128)S(1)}, bf16[2048,128]{1,0:T(8,128)(2,1)S(1)}, bf16[512,64]{1,0:T(8,128)(2,1)S(1)}, bf16[1024,128]{1,0:T(8,128)(2,1)S(1)}) custom-call(bf16[336,128]{1,0:T(8,128)(2,1)S(1)} %get-tuple-element.23.refs_0_.payload_ref, bf16[336,128]{1,0:T(8,128)(2,1)S(1)} %collective-permute-done.refs_1_, ...), custom_call_target="tpu_custom_call" | custom-call | flops 1000000000 | bytes 1048576 | tf_op jit(solution)/shard_map/pallas_call | solution.py:431
  18.9 0.0 collective-permute-done.7.refs_9_
  18.9 3.3 %shard_map.104 = (f32[1096,128]{1,0:T(8,128)S(1)}, bf16[64,4096]{1,0:T(8,128)(2,1)S(1)}, bf16[1024,2048]{1,0:T(8,128)(2,1)S(1)}, f32[8,256]{1,0:T(8,128)S(1)}) custom-call(bf16[336,128]{1,0:T(8,128)(2,1)S(1)} %get-tuple-element.23.refs_0_.payload_ref, bf16[336,128]{1,0:T(8,128)(2,1)S(1)} %collective-permute-done.refs_1_, ...), custom_call_target="tpu_custom_call" | custom-call | tf_op jit(solution)/shard_map/pallas_call | solution.py:452
  22.2 0.5 %collective-permute-start.9 = (f32[1096,128]{1,0:T(8,128)S(1)}, f32[1096,128]{1,0:T(8,128)S(1)}, u32[]{:S(2)}, u32[]{:S(2)}) collective-permute-start(f32[1096,128]{1,0:T(8,128)S(1)} %get-tuple-element.28.own_ref), channel_id=1, source_target_pairs={{0,1},{1,0},{2,3},{3,2},{4,5},{5,4},{6,7},{7,6},{8,9},{9,8},{10,11... | collective-permute-start | bytes 1683464 | tf_op jit(solution)/shard_map/ppermute | solution.py:355
  22.8 0.9 %shard_map.105 = (bf16[256,128]{1,0:T(8,128)(2,1)S(1)}, f32[4,1024]{1,0:T(4,128)S(1)}) custom-call(bf16[64,4096]{1,0:T(8,128)(2,1)S(1)} %get-tuple-element.29.spread, bf16[1024,2048]{1,0:T(8,128)(2,1)S(1)} %get-tuple-element.30.outer, f32[8,256]{1,0:T(8,128)S(1)} %get-tuple-element.31.inverse_own, ...), custom_call_target="tpu_custom_call" | custom-call | flops 268435456 | bytes 4194304 | tf_op jit(solution)/shard_map/pallas_call | solution.py:467
  23.7 0.6 %collective-permute-done.9.other_ref = f32[1096,128]{1,0:T(8,128)S(1)} collective-permute-done((f32[1096,128]{1,0:T(8,128)S(1)}, f32[1096,128]{1,0:T(8,128)S(1)}, u32[]{:S(2)}, u32[]{:S(2)}) %collective-permute-start.9) | collective-permute-done | bytes 561184 | tf_op jit(solution)/shard_map/ppermute | solution.py:355
  24.4 0.9 %shard_map.106 = (bf16[256,128]{1,0:T(8,128)(2,1)}, f32[4,1024]{1,0:T(4,128)}, f32[1024,128]{1,0:T(8,128)}, f32[4,1024]{1,0:T(4,128)}, f32[1,128]{1,0:T(1,128)}) custom-call(f32[1096,128]{1,0:T(8,128)S(1)} %get-tuple-element.28.own_ref, f32[1096,128]{1,0:T(8,128)S(1)} %collective-permute-done.9.other_ref, ...), custom_call_target="tpu_custom_call" | custom-call | tf_op jit(solution)/shard_map/pallas_call | solution.py:479
  (2 shorter events, 0.0 us)
Async XLA Ops:
  1.7 7.2 %collective-permute-start.3 = (bf16[336,128]{1,0:T(8,128)(2,1)S(1)}, bf16[336,128]{1,0:T(8,128)(2,1)S(1)}, u32[]{:S(2)}, u32[]{:S(2)}) collective-permute-start(bf16[336,128]{1,0:T(8,128)(2,1)S(1)} %get-tuple-element.23.refs_0_.payload_ref), channel_id=1, source_target_pairs={{0,2},{1,3},{2,0},{3,1},{4,6},{5,7},{6,4},{7,5},{8,10},{9,11},{10,... | collective-permute-start | bytes 258056 | tf_op jit(solution)/shard_map/ppermute | solution.py:355
  4.8 7.2 %collective-permute-start = (bf16[336,128]{1,0:T(8,128)(2,1)S(1)}, bf16[336,128]{1,0:T(8,128)(2,1)S(1)}, u32[]{:S(2)}, u32[]{:S(2)}) collective-permute-start(bf16[336,128]{1,0:T(8,128)(2,1)S(1)} %get-tuple-element.23.refs_0_.payload_ref), channel_id=1, source_target_pairs={{0,8},{1,9},{2,10},{3,11},{4,12},{5,13},{6,14},{7,15},{8,0},{9,1},... | collective-permute-start | bytes 258056 | tf_op jit(solution)/shard_map/ppermute | solution.py:355
  7.4 6.7 %collective-permute-start.5 = (bf16[336,128]{1,0:T(8,128)(2,1)S(1)}, bf16[336,128]{1,0:T(8,128)(2,1)S(1)}, u32[]{:S(2)}, u32[]{:S(2)}) collective-permute-start(bf16[336,128]{1,0:T(8,128)(2,1)S(1)} %get-tuple-element.23.refs_0_.payload_ref), channel_id=1, source_target_pairs={{0,4},{1,5},{2,6},{3,7},{4,0},{5,1},{6,2},{7,3},{8,12},{9,13},{10,... | collective-permute-start | bytes 258056 | tf_op jit(solution)/shard_map/ppermute | solution.py:355
  8.9 7.4 %collective-permute-start.1 = (bf16[336,128]{1,0:T(8,128)(2,1)S(1)}, bf16[336,128]{1,0:T(8,128)(2,1)S(1)}, u32[]{:S(2)}, u32[]{:S(2)}) collective-permute-start(bf16[336,128]{1,0:T(8,128)(2,1)S(1)} %get-tuple-element.23.refs_0_.payload_ref), channel_id=1, source_target_pairs={{0,14},{1,15},{2,12},{3,13},{4,10},{5,11},{6,8},{7,9},{8,6},{9,7},... | collective-permute-start | bytes 258056 | tf_op jit(solution)/shard_map/ppermute | solution.py:355
  8.9 7.7 %collective-permute-start.4 = (bf16[336,128]{1,0:T(8,128)(2,1)S(1)}, bf16[336,128]{1,0:T(8,128)(2,1)S(1)}, u32[]{:S(2)}, u32[]{:S(2)}) collective-permute-start(bf16[336,128]{1,0:T(8,128)(2,1)S(1)} %collective-permute-done.3.refs_4_), channel_id=1, source_target_pairs={{0,4},{1,5},{2,6},{3,7},{4,0},{5,1},{6,2},{7,3},{8,12},{9,13},{10,... | collective-permute-start | bytes 258056 | tf_op jit(solution)/shard_map/ppermute | solution.py:355
  11.9 5.2 %collective-permute-start.6 = (bf16[336,128]{1,0:T(8,128)(2,1)S(1)}, bf16[336,128]{1,0:T(8,128)(2,1)S(1)}, u32[]{:S(2)}, u32[]{:S(2)}) collective-permute-start(bf16[336,128]{1,0:T(8,128)(2,1)S(1)} %collective-permute-done.refs_1_), channel_id=1, source_target_pairs={{0,2},{1,3},{2,0},{3,1},{4,6},{5,7},{6,4},{7,5},{8,10},{9,11},{10,... | collective-permute-start | bytes 258056 | tf_op jit(solution)/shard_map/ppermute | solution.py:355
  11.9 5.6 %collective-permute-start.2 = (bf16[336,128]{1,0:T(8,128)(2,1)S(1)}, bf16[336,128]{1,0:T(8,128)(2,1)S(1)}, u32[]{:S(2)}, u32[]{:S(2)}) collective-permute-start(bf16[336,128]{1,0:T(8,128)(2,1)S(1)} %collective-permute-done.refs_1_), channel_id=1, source_target_pairs={{0,4},{1,5},{2,6},{3,7},{4,0},{5,1},{6,2},{7,3},{8,12},{9,13},{10,... | collective-permute-start | bytes 258056 | tf_op jit(solution)/shard_map/ppermute | solution.py:355
  14.1 3.6 %collective-permute-start.8 = (s32[4]{0:T(128)}, s32[4]{0:T(128)S(1)}, u32[]{:S(2)}, u32[]{:S(2)}) collective-permute-start(s32[4]{0:T(128)} %depth_ref.1), channel_id=1, source_target_pairs={{0,1},{1,0},{2,3},{3,2},{4,5},{5,4},{6,7},{7,6},{8,9},{9,8},{10,11... | collective-permute-start | bytes 56 | tf_op jit(solution)/shard_map/ppermute | solution.py:355
  17.5 1.3 %collective-permute-start.7 = (bf16[288,128]{1,0:T(8,128)(2,1)S(1)}, bf16[288,128]{1,0:T(8,128)(2,1)S(1)}, u32[]{:S(2)}, u32[]{:S(2)}) collective-permute-start(bf16[288,128]{1,0:T(8,128)(2,1)S(1)} %shard_map.102.refs_8_), channel_id=1, source_target_pairs={{0,1},{1,0},{2,3},{3,2},{4,5},{5,4},{6,7},{7,6},{8,9},{9,8},{10,11... | collective-permute-start | bytes 221192 | tf_op jit(solution)/shard_map/ppermute | solution.py:355
  22.2 2.1 %collective-permute-start.9 = (f32[1096,128]{1,0:T(8,128)S(1)}, f32[1096,128]{1,0:T(8,128)S(1)}, u32[]{:S(2)}, u32[]{:S(2)}) collective-permute-start(f32[1096,128]{1,0:T(8,128)S(1)} %get-tuple-element.28.own_ref), channel_id=1, source_target_pairs={{0,1},{1,0},{2,3},{3,2},{4,5},{5,4},{6,7},{7,6},{8,9},{9,8},{10,11... | collective-permute-start | bytes 1683464 | tf_op jit(solution)/shard_map/ppermute | solution.py:355
